TPU v7x, 256 devices: a whole 4x4x8 slice. The times are simulated.
256 devices in a mesh: ctx: 64 (over z, y_lo, x), head: 4 (over y_hi, core).
Axes of the slice: x: 4, y: 4 (y_hi: 2, y_lo: 2; y = y_hi * 2 + y_lo), z: 8, core: 2. Of those that a mesh axis runs over, the one named last changes fastest.
Arguments:
- query: bfloat16 [32768, 1024], P('ctx', 'head'), may hold values from -8 to 8
- key: bfloat16 [32768, 1024], P('ctx', 'head'), may hold values from -8 to 8
- value: bfloat16 [32768, 1024], P('ctx', 'head'), may hold values from -6 to 6
- pos_store: bfloat16 [2048, 1024], P('ctx', 'head'), may hold values from -6 to 6
- owner: int32 [64], replicated, may hold values from 0 to 63, each once
- block_mask: int32 [64, 4], P('ctx'), may hold values from 0 to 1, as said below
- content_bias: float32 [1024], P('head'), may hold values from -3 to 3
- pos_bias: float32 [1024], P('head'), may hold values from -3 to 3
- out_weight: bfloat16 [1024, 1024], P('head'), may hold values from -0.1875 to 0.1875
- d_layer: bfloat16 [32768, 1024], P('ctx', 'head'), may hold values from -6 to 6
Outputs:
- grad_query: bfloat16 [32768, 1024], P('ctx', 'head')
- grad_key: bfloat16 [32768, 1024], P('ctx', 'head')
- grad_value: bfloat16 [32768, 1024], P('ctx', 'head')
- grad_pos: bfloat16 [2048, 1024], P('ctx', 'head')
- grad_out_weight: bfloat16 [1024, 1024], P('head', 'ctx')
Inputs may be any that keep to these rules, and one draw needn't show every extreme that they name: block_mask[c, 0] is 1 for every block c. `owner`: each of the 64 slots is named once.
All inputs are finite; a program needn't handle non-finite values.
Results may differ from a plain program's by a relative error of at most 0.013.
The roundings to bfloat16 on the way count: a program that leaves them out, or rounds other values in their place, can miss the bound.
Values may be sent and summed in bfloat16 or wider, within the bound.
No kernel may reach another device: no remote copies, remote signals or barrier semaphores. Data moves between devices by JAX's collectives and lax.ppermute only.
A program may use at most 128 MiB of HBM per device.

v0:
```python
from functools import reduce
import math

import jax
import jax.numpy as jnp
from jax import lax
from jax.sharding import PartitionSpec as P

HD = 64


def from_behind(x, axis, by):
    count = lax.axis_size(axis)
    pairs = [(i, i + by) for i in range(count) if 0 <= i + by < count]
    return lax.ppermute(x, axis, pairs)


def for_sending(x):

    def short(part):
        return part.astype(jnp.bfloat16) if part.dtype == jnp.float32 else part

    return jax.tree.map(short, x)


def shifted(block, axis, distance):
    devices = range(lax.axis_size(axis))
    route = [((i - distance) % len(devices), i) for i in devices]
    return lax.ppermute(block, axis, route)


def product(spec, first_arg, second_arg):
    return jnp.einsum(spec, first_arg, second_arg, preferred_element_type=jnp.float32)


def relative_shift(wide_scores):
    length = wide_scores.shape[0]
    flipped = wide_scores[:, ::-1].reshape(2 * length * length)
    kept = flipped[length - 1 : length - 1 + length * (2 * length - 1)]
    return kept.reshape(length, 2 * length - 1)[:, :length]


def relative_unshift(narrow):
    length = narrow.shape[0]
    padded = jnp.pad(narrow, ((0, 0), (0, length - 1))).reshape(length * (2 * length - 1))
    padded = jnp.pad(padded, (length - 1, 1))
    return padded.reshape(length, 2 * length)[:, ::-1]


def head_backward(
    content_query, position_query, keys_window, values_window, pos_window, grad_attn, allowed
):
    rows_here = content_query.shape[0]
    window = keys_window.shape[0]
    score_scale = 1.0 / math.sqrt(content_query.shape[1])
    scores = []
    for lag_index in range(window):
        content = product("ae,be->ab", content_query, keys_window[lag_index])
        pos_rows = pos_window[lag_index * rows_here : (lag_index + 2) * rows_here]
        wide_scores = product("ae,te->at", position_query, pos_rows)
        raw_scores = score_scale * (content + relative_shift(wide_scores))
        scores.append(jnp.where(allowed[lag_index], raw_scores, -jnp.inf))
    row_max = reduce(jnp.maximum, [jnp.max(entry, axis=1, keepdims=True) for entry in scores])
    weights = [jnp.exp(entry - row_max) for entry in scores]
    row_total = reduce(jnp.add, [jnp.sum(entry, axis=1, keepdims=True) for entry in weights])
    probs = [entry / row_total for entry in weights]
    probs_low = [entry.astype(jnp.bfloat16) for entry in probs]
    attention = reduce(
        jnp.add,
        [
            product("ab,be->ae", probs_low[lag_index], values_window[lag_index])
            for lag_index in range(window)
        ],
    )
    attention = attention.astype(jnp.bfloat16)
    row_dot = jnp.sum(
        grad_attn.astype(jnp.float32) * attention.astype(jnp.float32), axis=1, keepdims=True
    )
    grad_content = jnp.zeros(content_query.shape, jnp.float32)
    grad_position = jnp.zeros(content_query.shape, jnp.float32)
    grad_window = jnp.zeros(pos_window.shape, jnp.float32)
    grad_keys = []
    grad_values = []
    for lag_index in range(window):
        grad_probs = product("ae,be->ab", grad_attn, values_window[lag_index])
        dscore = (score_scale * probs[lag_index] * (grad_probs - row_dot)).astype(jnp.bfloat16)
        grad_values.append(product("ab,ae->be", probs_low[lag_index], grad_attn))
        grad_keys.append(product("ab,ae->be", dscore, content_query))
        grad_content = grad_content + product("ab,be->ae", dscore, keys_window[lag_index])
        spread = relative_unshift(dscore)
        pos_rows = pos_window[lag_index * rows_here : (lag_index + 2) * rows_here]
        grad_position = grad_position + product("at,te->ae", spread, pos_rows)
        grad_window = grad_window.at[lag_index * rows_here : (lag_index + 2) * rows_here].add(
            product("at,ae->te", spread, position_query)
        )
    grad_query = (grad_content + grad_position).astype(jnp.bfloat16)
    return (attention, grad_query, jnp.stack(grad_keys), jnp.stack(grad_values), grad_window)


def body(
    query, key, value, pos_store, owner, block_mask, content_bias, pos_bias, out_weight, d_layer
):
    rows_here = query.shape[0]
    features = query.shape[1]
    head_count = features // HD
    window = block_mask.shape[1]
    block_index = lax.axis_index("ctx")
    full_grad = lax.all_gather(d_layer, "head", axis=1, tiled=True)
    grad_attn = lax.dot_general(
        full_grad, out_weight, (((1,), (1,)), ((), ())), preferred_element_type=jnp.float32
    ).astype(jnp.bfloat16)
    content_query = (query.astype(jnp.float32) + content_bias).astype(jnp.bfloat16)
    position_query = (query.astype(jnp.float32) + pos_bias).astype(jnp.bfloat16)
    own_pair = jnp.stack([key, value])
    pairs = [own_pair]
    travelling = own_pair
    for lag_index in range(1, window):
        travelling = from_behind(travelling, "ctx", 1)
        pairs.append(travelling)
    gathered = lax.all_gather(pos_store, "ctx", axis=0, tiled=True)
    slot_count = owner.shape[0]
    slot_rows = gathered.shape[0] // slot_count
    dist_order = gathered.reshape(slot_count, slot_rows, features)[owner].reshape(-1, features)
    pos_ext = jnp.concatenate([jnp.zeros((rows_here, features), jnp.bfloat16), dist_order], 0)
    row_ids = jnp.arange(rows_here, dtype=jnp.int32)
    causal_mask = row_ids[None, :] <= row_ids[:, None]
    masks = []
    for lag_index in range(window):
        flag = (block_mask[0, lag_index] == 1) & (block_index - lag_index >= 0)
        if lag_index == 0:
            masks.append(jnp.logical_and(flag, causal_mask))
        else:
            masks.append(jnp.broadcast_to(flag, (rows_here, rows_here)))
    allowed = jnp.stack(masks)
    stacked = jnp.stack(pairs)
    keys_heads = stacked[:, 0].reshape(window, rows_here, head_count, HD).transpose(2, 0, 1, 3)
    values_heads = stacked[:, 1].reshape(window, rows_here, head_count, HD).transpose(2, 0, 1, 3)

    def split_heads(matrix):
        return matrix.reshape(matrix.shape[0], head_count, HD).transpose(1, 0, 2)

    def per_head(packed):
        return head_backward(*packed, allowed)

    results = lax.map(
        per_head,
        (
            split_heads(content_query),
            split_heads(position_query),
            keys_heads,
            values_heads,
            split_heads(pos_ext),
            split_heads(grad_attn),
        ),
    )
    attention_heads, grad_query_heads, grad_keys_heads, grad_values_heads, grad_window_heads = (
        results
    )
    attention_rows = attention_heads.transpose(1, 0, 2).reshape(rows_here, features)
    grad_query_rows = grad_query_heads.transpose(1, 0, 2).reshape(rows_here, features)
    key_terms = grad_keys_heads.transpose(1, 2, 0, 3).reshape(window, rows_here, features)
    value_terms = grad_values_heads.transpose(1, 2, 0, 3).reshape(window, rows_here, features)
    partials = jnp.stack([key_terms, value_terms], 1)
    running = partials[0]
    for lag_index in range(1, window):
        running = (
            shifted(for_sending(running), "ctx", 1).astype(running.dtype) + partials[lag_index]
        )
    homed = shifted(for_sending(running), "ctx", 1 - window).astype(running.dtype)
    dist_grad = grad_window_heads.transpose(1, 0, 2).reshape(-1, features)[rows_here:]
    inverse = jnp.argsort(owner)
    stored_grad = dist_grad.reshape(slot_count, slot_rows, features)[inverse].reshape(-1, features)
    weight_term = lax.dot_general(
        attention_rows, full_grad, (((0,), (0,)), ((), ())), preferred_element_type=jnp.float32
    )
    pos_sum, weight_sum = (
        lax.psum_scatter(stored_grad, "ctx", scatter_dimension=0, tiled=True),
        lax.psum_scatter(weight_term, "ctx", scatter_dimension=1, tiled=True),
    )
    return (
        grad_query_rows,
        homed[0].astype(jnp.bfloat16),
        homed[1].astype(jnp.bfloat16),
        pos_sum.astype(jnp.bfloat16),
        weight_sum.astype(jnp.bfloat16),
    )


def solution(mesh):
    return jax.shard_map(
        body,
        mesh=mesh,
        in_specs=(
            P("ctx", "head"),
            P("ctx", "head"),
            P("ctx", "head"),
            P("ctx", "head"),
            P(),
            P("ctx", None),
            P("head"),
            P("head"),
            P("head", None),
            P("ctx", "head"),
        ),
        out_specs=(
            P("ctx", "head"),
            P("ctx", "head"),
            P("ctx", "head"),
            P("ctx", "head"),
            P("head", "ctx"),
        ),
        check_vma=False,
    )
```

profile of v0, /device:TPU:16, one launch (start us, length us, event | category | flops | bytes accessed | tf_op | source)
XLA Modules:
  0.0 1807.4 jit_solution(7915616241884483458)
XLA Ops:
  10.3 3.4 collective-permute-start
  13.8 11.1 collective-permute-done
  24.9 4.4 collective-permute-start.1
  32.8 6.7 collective-permute-done.1
  39.5 4.4 collective-permute-start.2
  44.8 8.6 collective-permute-done.2
  57.7 277.5 %all-gather.3.cloned.1.call-done = bf16[2048,256]{1,0:T(8,128)(2,1)} async-done(((bf16[32,256]{1,0:T(8,128)(2,1)}), bf16[2048,256]{1,0:T(8,128)(2,1)}) %all-gather.3.cloned.1.call-update) | async-done | bytes 1048592 | tf_op jit(solution)/shard_map/all_gather | solution.py:120
  339.8 825.7 %while.26 = (s32[]{:T(128)}, bf16[4,512,64]{1,2,0:T(8,128)(2,1)}, bf16[4,512,64]{1,2,0:T(8,128)(2,1)}, f32[4,4,512,64]{2,3,0,1:T(8,128)}, f32[4,4,512,64]{2,3,0,...) while((s32[]{:T(128)}, bf16[4,512,64]{1,2,0:T(8,128)(2,1)}, ...), condition=%wide.region_10.11_spmd.clone, body=%wide.region_0.10_spmd.clone.sunk | while | flops 1628371456 | bytes 223848896 | solution.py:145
  363.2 14.9 rev.75
  379.2 2.8 reshape.409
  387.5 14.9 rev.74
  403.5 2.8 reshape.408
  412.0 17.6 rev.73
  433.7 4.3 reshape.407
  445.0 17.6 rev.72
  466.7 4.4 reshape.406
  498.2 3.3 rev.78
  504.5 3.3 rev.77
  514.8 13.7 rev.76
  540.1 13.8 rev.79
  562.9 14.9 rev.75
  579.0 2.8 reshape.409
  587.3 14.9 rev.74
  603.3 2.8 reshape.408
  611.8 17.6 rev.73
  633.5 4.3 reshape.407
  644.8 17.6 rev.72
  666.5 4.4 reshape.406
  698.0 3.3 rev.78
  704.2 3.3 rev.77
  714.6 13.7 rev.76
  739.9 13.8 rev.79
  762.8 14.9 rev.75
  778.8 2.8 reshape.409
  787.1 14.9 rev.74
  803.2 2.8 reshape.408
  811.6 17.6 rev.73
  833.3 4.3 reshape.407
  844.7 17.6 rev.72
  866.3 4.4 reshape.406
  897.8 3.3 rev.78
  904.1 3.3 rev.77
  914.4 13.7 rev.76
  939.7 13.8 rev.79
  962.6 14.9 rev.75
  978.6 2.8 reshape.409
  987.0 14.9 rev.74
  1011.4 17.6 rev.73
  1033.1 4.3 reshape.407
  1044.5 17.6 rev.72
  1066.1 4.4 reshape.406
  1097.7 3.3 rev.78
  1103.9 3.3 rev.77
  1114.2 13.7 rev.76
  1139.5 13.8 rev.79
  1165.6 2.9 fusion.147
  1172.4 3.1 copy.83
  1175.5 4.2 reshape.357
  1186.7 12.6 collective-permute-done.3
  1199.6 13.6 collective-permute-done.4
  1213.4 13.8 collective-permute-done.5
  1229.3 8.9 collective-permute-done.6
  1239.9 242.6 %reduce-scatter.5.cloned.1.call-done = f32[256,16]{0,1:T(8,128)} async-done(((f32[256,1024]{0,1:T(8,128)}), f32[256,16]{0,1:T(8,128)}) %reduce-scatter.5.cloned.1.call-update) | async-done | bytes 16400 | tf_op jit(solution)/shard_map/reduce_scatter | solution.py:178
  1483.9 315.5 %reduce-scatter.3.cloned.1.call-done = f32[32,256]{1,0:T(8,128)} async-done(((f32[2048,256]{1,0:T(8,128)}), f32[32,256]{1,0:T(8,128)}) %reduce-scatter.3.cloned.1.call-update) | async-done | bytes 32784 | tf_op jit(solution)/shard_map/reduce_scatter | solution.py:177
  (543 shorter events, 377.2 us)
Async XLA Ops:
  7.2 48.1 %copy-start = (bf16[256,1024]{1,0:T(8,128)(2,1)S(1)}, bf16[256,1024]{1,0:T(8,128)(2,1)}, u32[]{:S(2)}) copy-start(bf16[256,1024]{1,0:T(8,128)(2,1)} %param.28) | copy-start | bytes 1572868
  7.2 22.2 %copy-start.22 = (s32[1,4]{1,0:T(1,128)S(1)}, s32[1,4]{1,0:T(1,128)}, u32[]{:S(2)}) copy-start(s32[1,4]{1,0:T(1,128)} %param.25) | copy-start | bytes 52
  7.2 25.4 %copy-start.21 = (bf16[512,256]{1,0:T(8,128)(2,1)S(1)}, bf16[512,256]{1,0:T(8,128)(2,1)}, u32[]{:S(2)}) copy-start(bf16[512,256]{1,0:T(8,128)(2,1)} %param.20) | copy-start | bytes 786436
  7.2 36.7 %copy-start.25 = (s32[64]{0:T(128)S(1)}, s32[64]{0:T(128)}, u32[]{:S(2)}) copy-start(s32[64]{0:T(128)} %param.24) | copy-start | bytes 772
  7.2 36.8 %copy-start.23 = (f32[256]{0:T(256)S(1)}, f32[256]{0:T(256)}, u32[]{:S(2)}) copy-start(f32[256]{0:T(256)} %param.27) | copy-start | bytes 3076
  7.2 36.8 %copy-start.24 = (f32[256]{0:T(256)S(1)}, f32[256]{0:T(256)}, u32[]{:S(2)}) copy-start(f32[256]{0:T(256)} %param.26) | copy-start | bytes 3076
  7.2 48.1 %all-gather.5.cloned.1.call-start = ((), (), s32[]{:S(2)}) async-start(), calls=%async_computation.3 | async-start | bytes 1310720 | tf_op jit(solution)/shard_map/all_gather | solution.py:108
  8.0 327.3 %all-gather.3.cloned.1.call-start = ((), (), s32[]{:S(2)}) async-start(), calls=%async_computation.2 | async-start | bytes 1064960 | tf_op jit(solution)/shard_map/all_gather | solution.py:120
  10.3 14.6 collective-permute-start
  13.8 1468.8 %reduce-scatter.5.cloned.1.call-start = ((), (), s32[]{:S(2)}) async-start(), calls=%async_computation.5 | async-start | bytes 1064960 | tf_op jit(solution)/shard_map/reduce_scatter | solution.py:178
  24.9 14.7 collective-permute-start.1
  39.5 13.9 collective-permute-start.2
  360.6 24.2 %copy-start.4 = (bf16[4,2560,64]{1,2,0:T(8,128)(2,1)}, bf16[4,2560,64]{1,2,0:T(8,128)(2,1)S(1)}, u32[]{:S(2)}) copy-start(bf16[4,2560,64]{1,2,0:T(8,128)(2,1)S(1)} %get-tuple-element.663) | copy-start | bytes 3932164 | tf_op jit(solution)/shard_map/while
  491.0 3.4 copy-start.2
  533.7 2.4 copy-start.3
  540.1 15.1 copy-start.16
  556.9 2.3 copy-start.9
  556.9 2.3 copy-start.10
  556.9 2.3 copy-start.11
  556.9 2.3 copy-start.12
  556.9 2.3 copy-start.13
  556.9 2.3 copy-start.14
  556.9 2.3 copy-start.15
  560.4 24.2 %copy-start.4 = (bf16[4,2560,64]{1,2,0:T(8,128)(2,1)}, bf16[4,2560,64]{1,2,0:T(8,128)(2,1)S(1)}, u32[]{:S(2)}) copy-start(bf16[4,2560,64]{1,2,0:T(8,128)(2,1)S(1)} %get-tuple-element.663) | copy-start | bytes 3932164 | tf_op jit(solution)/shard_map/while
  690.8 3.4 copy-start.2
  733.5 2.4 copy-start.3
  739.9 15.1 copy-start.16
  756.7 2.3 copy-start.9
  756.7 2.3 copy-start.10
  756.7 2.3 copy-start.11
  756.7 2.3 copy-start.12
  756.7 2.3 copy-start.13
  756.7 2.3 copy-start.14
  756.7 2.3 copy-start.15
  760.2 24.2 %copy-start.4 = (bf16[4,2560,64]{1,2,0:T(8,128)(2,1)}, bf16[4,2560,64]{1,2,0:T(8,128)(2,1)S(1)}, u32[]{:S(2)}) copy-start(bf16[4,2560,64]{1,2,0:T(8,128)(2,1)S(1)} %get-tuple-element.663) | copy-start | bytes 3932164 | tf_op jit(solution)/shard_map/while
  890.6 3.4 copy-start.2
  933.3 2.4 copy-start.3
  939.7 15.1 copy-start.16
  956.5 2.3 copy-start.9
  956.5 2.3 copy-start.10
  956.5 2.3 copy-start.11
  956.5 2.3 copy-start.12
  956.5 2.3 copy-start.13
  956.5 2.3 copy-start.14
  956.6 2.3 copy-start.15
  960.0 24.2 %copy-start.4 = (bf16[4,2560,64]{1,2,0:T(8,128)(2,1)}, bf16[4,2560,64]{1,2,0:T(8,128)(2,1)S(1)}, u32[]{:S(2)}) copy-start(bf16[4,2560,64]{1,2,0:T(8,128)(2,1)S(1)} %get-tuple-element.663) | copy-start | bytes 3932164 | tf_op jit(solution)/shard_map/while
  1090.4 3.4 copy-start.2
  1133.2 2.4 copy-start.3
  1139.5 15.1 copy-start.16
  1156.4 2.3 copy-start.9
  1156.4 2.3 copy-start.10
  1156.4 2.3 copy-start.11
  1156.4 2.3 copy-start.12
  1156.4 2.3 copy-start.13
  1156.4 2.3 copy-start.14
  1156.4 2.3 copy-start.15
  1165.6 3.0 copy-start.26
  1168.5 630.8 %reduce-scatter.3.cloned.1.call-start = ((), (), s32[]{:S(2)}) async-start(), calls=%async_computation.4 | async-start | bytes 2129920 | tf_op jit(solution)/shard_map/reduce_scatter | solution.py:177
  1185.6 13.7 collective-permute-start.3
  1199.3 27.9 %copy-start.19 = (f32[4,4,512,64]{2,3,0,1:T(8,128)S(1)}, f32[4,4,512,64]{2,3,0,1:T(8,128)}, u32[]{:S(2)}) copy-start(f32[4,4,512,64]{2,3,0,1:T(8,128)} %get-tuple-element.311) | copy-start | bytes 6291460
  1199.5 13.7 collective-permute-start.4
  1213.3 13.9 collective-permute-start.5
  1227.3 573.4 %copy-start.1 = (bf16[256,1024]{1,0:T(8,128)(2,1)S(1)}, bf16[256,1024]{1,0:T(8,128)(2,1)}, u32[]{:S(2)}) copy-start(bf16[256,1024]{1,0:T(8,128)(2,1)} %param.28) | copy-start | bytes 1572868
  1227.4 10.8 collective-permute-start.6
  (37 other events, 51.3 us)
Sparse Core Ops, SparseCore 0:
  9.9 25.1 all-gather.4
  36.9 298.3 all-gather.2
  1168.7 313.8 reduce-scatter.4
  1485.0 314.2 reduce-scatter.2
where the time goes:
time: 1840 us; the launch traced here: 1810 us
  waiting for transfers between devices  912 us (50%)
  local copies, waits for them, and re-layouts  644 us (35%)
  matrix products  175 us (10%)
  loops' own time  28.2 us (2%)
    reduce_scatter x1, waiting for transfers between devices, body(): lax.psum_scatter(stored_grad, 'ctx', scatter_dimension=0, tiled=True)  315 us
    all_gather x1, waiting for transfers between devices, body(): gathered = lax.all_gather(pos_store, 'ctx', axis=0, tiled=True)  278 us
    rev x16, local copies, waits for them, and re-layouts, relative_shift(): flipped = wide_scores[:, ::-1].reshape(2 * length * length)  260 us
    reduce_scatter x1, waiting for transfers between devices, body(): lax.psum_scatter(weight_term, 'ctx', scatter_dimension=1, tiled=True)  243 us
    dot_general x144, matrix products, product(): jnp.einsum(spec, first_arg, second_arg, preferred_element_type=jnp.float32)  169 us
    rev x16, local copies, waits for them, and re-layouts, relative_unshift(): return padded.reshape(length, 2 * length)[:, ::-1]  137 us
    reshape x16, local copies, waits for them, and re-layouts, relative_shift(): return kept.reshape(length, 2 * length - 1)[:, :length]  57.5 us
    while x188, local copies, waits for them, and re-layouts  50.2 us
  transfers between devices with their start and end apart: 11, of which 10 were waited for; matrix products, arithmetic and copies ran while one was open for 2% of the time, Pallas kernels for 0%

commit v1 on v0

v1 whole, which is shorter than its diff:
```python
import functools
import jax
import jax.numpy as jnp
from jax import lax
from jax.experimental import pallas as pl
from jax.experimental.pallas import tpu as pltpu
from jax.sharding import PartitionSpec as P

HD = 64
NEG = -1e30


def nt(a, b):
    return lax.dot_general(a, b, (((1,), (1,)), ((), ())), preferred_element_type=jnp.float32)


def nn(a, b):
    return lax.dot_general(a, b, (((1,), (0,)), ((), ())), preferred_element_type=jnp.float32)


def tn(a, b):
    return lax.dot_general(a, b, (((0,), (0,)), ((), ())), preferred_element_type=jnp.float32)


def pair_kernel(
    owner_ref, flag_ref, q_ref, kv0, kv1, kv2, kv3, slots_ref, cb_ref, pb_ref, ga_ref,
    dq_ref, own_ref, far_ref, dpos_ref, att_ref,
    table, flipped, dkt, dvt, dpt,
):
    tokens = q_ref.shape[0]
    window = 4
    span = tokens * window
    half = tokens // 2
    wide = span + half
    slot_count = owner_ref.shape[0]
    slot_rows = slots_ref.shape[0] // slot_count
    keys = [kv.at[0] for kv in (kv3, kv2, kv1, kv0)]
    values = [kv.at[1] for kv in (kv3, kv2, kv1, kv0)]
    bf = jnp.bfloat16
    anti = (
        lax.broadcasted_iota(jnp.int32, (half, half), 0)
        + lax.broadcasted_iota(jnp.int32, (half, half), 1)
        == half - 1
    ).astype(jnp.float32).astype(bf)

    table[0:tokens, :] = jnp.zeros((tokens, 128), bf)
    for d in range(slot_count):
        at = pl.multiple_of(owner_ref[d] * slot_rows, slot_rows)
        table[tokens + d * slot_rows : tokens + (d + 1) * slot_rows, :] = slots_ref[pl.ds(at, slot_rows), :]
    count = (tokens + span) // half
    for i in range(count):
        flipped[(count - 1 - i) * half : (count - i) * half, :] = nn(
            anti, table[i * half : (i + 1) * half, :]
        ).astype(bf)
    dkt[...] = jnp.zeros_like(dkt)
    dvt[...] = jnp.zeros_like(dvt)
    dpt[...] = jnp.zeros_like(dpt)

    lane = lax.broadcasted_iota(jnp.int32, (1, 128), 1)
    for r in range(2):
        rows = slice(r * half, (r + 1) * half)
        query = q_ref[rows, :].astype(jnp.float32)
        cq = (query + cb_ref[...]).astype(bf)
        pq = (query + pb_ref[...]).astype(bf)
        ga = ga_ref[rows, :]
        att_both = []
        dq_both = []
        for h in range(2):
            mine = (lane // HD) == h
            cqm = jnp.where(mine, cq, jnp.zeros_like(cq))
            pqm = jnp.where(mine, pq, jnp.zeros_like(pq))
            gam = jnp.where(mine, ga, jnp.zeros_like(ga))
            cqs = cqm * jnp.asarray(0.125, bf)
            pqs = pqm * jnp.asarray(0.125, bf)
            base = half * (1 - r)
            rel = nt(pqs, flipped[base : base + wide, :])
            rel = pltpu.roll(rel, span + 1, 1, stride=1, stride_axis=0)
            scores = []
            for w in range(window):
                s = nt(cqs, keys[w][...]) + rel[:, w * tokens : (w + 1) * tokens]
                if w == window - 1:
                    row = lax.broadcasted_iota(jnp.int32, (half, tokens), 0) + r * half
                    col = lax.broadcasted_iota(jnp.int32, (half, tokens), 1)
                    s = jnp.where(col <= row, s, NEG)
                else:
                    s = jnp.where(flag_ref[window - 1 - w] == 1, s, NEG)
                scores.append(s)
            top = functools.reduce(jnp.maximum, [jnp.max(s, axis=1, keepdims=True) for s in scores])
            weights = [jnp.exp(s - top) for s in scores]
            total = functools.reduce(jnp.add, [jnp.sum(e, axis=1, keepdims=True) for e in weights])
            inv = 1.0 / total
            probs = [e * inv for e in weights]
            low = [p.astype(bf) for p in probs]
            att = functools.reduce(jnp.add, [nn(low[w], values[w][...]) for w in range(window)])
            att = jnp.where(mine, att, 0.0).astype(bf)
            att_both.append(att)
            dot = jnp.sum(gam.astype(jnp.float32) * att.astype(jnp.float32), axis=1, keepdims=True)
            flips = [None] * 8
            acc = None
            for w in range(window):
                cols = slice(w * tokens, (w + 1) * tokens)
                dp = nt(gam, values[w][...])
                ds = (0.125 * probs[w] * (dp - dot)).astype(bf)
                dvt[:, cols] += tn(gam, low[w])
                dkt[:, cols] += tn(cqm, ds)
                part = nn(ds, keys[w][...])
                acc = part if acc is None else acc + part
                for x in range(2):
                    flips[7 - (2 * w + x)] = nn(ds[:, x * half : (x + 1) * half], anti)
            spread = jnp.concatenate(flips + [jnp.zeros((half, half), jnp.float32)], axis=1)
            spread = pltpu.roll(spread, 1, 1, stride=1, stride_axis=0).astype(bf)
            start = half * r
            acc = acc + nn(spread, table[start : start + wide, :])
            dpt[:, start : start + wide] += tn(pqm, spread)
            dq_both.append(acc)
        att_ref[rows, :] = jnp.where(lane < HD, att_both[0], att_both[1])
        dq_ref[rows, :] = jnp.where(lane < HD, dq_both[0], dq_both[1]).astype(bf)
    for i, grad in enumerate((dkt, dvt)):
        for w in range(window):
            block = grad[:, w * tokens : (w + 1) * tokens].T
            if w == window - 1:
                own_ref[i] = block
            else:
                far_ref[window - 2 - w, i] = block.astype(bf)
    dist = dpt[:, tokens:].T.astype(bf)
    for d in range(slot_count):
        at = pl.multiple_of(owner_ref[d] * slot_rows, slot_rows)
        dpos_ref[pl.ds(at, slot_rows), :] = dist[d * slot_rows : (d + 1) * slot_rows, :]


def pair_call(owner, flags, q, kvs, slots, cb, pb, ga):
    tokens, features = q.shape
    pairs = features // 128
    rel = slots.shape[0]

    def col(rows):
        return pl.BlockSpec((rows, 128), lambda p, *_: (0, p))

    both = pl.BlockSpec((2, tokens, 128), lambda p, *_: (0, 0, p))
    bf = jnp.bfloat16
    return pl.pallas_call(
        pair_kernel,
        grid_spec=pltpu.PrefetchScalarGridSpec(
            num_scalar_prefetch=2,
            grid=(pairs,),
            in_specs=[col(tokens)] + [both] * 4 + [col(rel), col(1), col(1), col(tokens)],
            out_specs=[
                col(tokens),
                both,
                pl.BlockSpec((3, 2, tokens, 128), lambda p, *_: (0, 0, 0, p)),
                col(rel),
                col(tokens),
            ],
            scratch_shapes=[
                pltpu.VMEM((tokens + rel, 128), bf),
                pltpu.VMEM((tokens + rel, 128), bf),
                pltpu.VMEM((128, rel), jnp.float32),
                pltpu.VMEM((128, rel), jnp.float32),
                pltpu.VMEM((128, tokens + rel), jnp.float32),
            ],
        ),
        out_shape=[
            jax.ShapeDtypeStruct((tokens, features), bf),
            jax.ShapeDtypeStruct((2, tokens, features), jnp.float32),
            jax.ShapeDtypeStruct((3, 2, tokens, features), bf),
            jax.ShapeDtypeStruct((rel, features), bf),
            jax.ShapeDtypeStruct((tokens, features), bf),
        ],
        compiler_params=pltpu.CompilerParams(vmem_limit_bytes=56 << 20),
    )(owner, flags, q, *kvs, slots, cb, pb, ga)


def shifted(block, distance):
    count = lax.axis_size("ctx")
    return lax.ppermute(block, "ctx", [(i, (i + distance) % count) for i in range(count)])


def swapped(block, bit):
    return lax.ppermute(block, "head", [(i, i ^ bit) for i in range(lax.axis_size("head"))])


def body(
    query, key, value, pos_store, owner, block_mask, content_bias, pos_bias, out_weight, d_layer
):
    rows, features = query.shape
    window = block_mask.shape[1]
    slot_count = owner.shape[0]
    bf = jnp.bfloat16
    block_index = lax.axis_index("ctx")
    flags = block_mask[0] * (block_index >= jnp.arange(window)).astype(jnp.int32)

    own_pair = jnp.stack([key, value])
    lag1 = shifted(own_pair, 1)
    lag3 = shifted(own_pair, 3)
    slots = lax.all_to_all(
        jnp.broadcast_to(pos_store[None], (slot_count,) + pos_store.shape), "ctx", 0, 0
    ).reshape(-1, features)
    lag2 = shifted(lag1, 1)
    full_grad = lax.all_gather(d_layer, "head", axis=1, tiled=True)
    grad_attn = nt(full_grad, out_weight).astype(bf)

    grad_query, own, far, dist, attention = pair_call(
        owner, flags, query, [own_pair, lag1, lag2, lag3], slots,
        content_bias[None], pos_bias[None], grad_attn,
    )
    weight_term = tn(full_grad, attention).astype(bf)
    weight_parts = lax.all_to_all(weight_term.reshape(slot_count, -1, features), "ctx", 0, 0)
    pos_parts = lax.all_to_all(dist.reshape(slot_count, -1, features), "ctx", 0, 0)
    home3 = shifted(far[2], -3)
    step = (shifted(far[1], -1).astype(jnp.float32) + far[0].astype(jnp.float32)).astype(bf)
    home1 = shifted(step, -1)
    homed = own + home3.astype(jnp.float32) + home1.astype(jnp.float32)
    grad_pos = jnp.sum(pos_parts.astype(jnp.float32), axis=0).astype(bf)
    grad_weight = jnp.sum(weight_parts.astype(jnp.float32), axis=0).astype(bf).T
    return grad_query, homed[0].astype(bf), homed[1].astype(bf), grad_pos, grad_weight


def solution(mesh):
    spread = P("ctx", "head")
    return jax.shard_map(
        body,
        mesh=mesh,
        in_specs=(
            spread, spread, spread, spread, P(), P("ctx", None), P("head"), P("head"),
            P("head", None), spread,
        ),
        out_specs=(spread, spread, spread, spread, P("head", "ctx")),
        check_vma=False,
    )
```

time: 1840 us -> 227 us (0.12); the launches traced: 1810 us -> 224 us
  waiting for transfers between devices: 912 us -> 95.2 us
  local copies, waits for them, and re-layouts: 644 us -> 6.03 us
  matrix products: 175 us -> 3.81 us
  Pallas kernels: 0 us -> 35.5 us
  loops' own time: 28.2 us -> 0 us
  blocking collectives: 0 us -> 25.1 us
  starting transfers between devices: 13.6 us -> 38.7 us
    reduce_scatter x2 -> x0, waiting for transfers between devices: 558 us -> none  [the longest x1 315 us: body(): lax.psum_scatter(stored_grad, 'ctx', scatter_dimension=0, tiled=True)]
    rev x32 -> x0, local copies, waits for them, and re-layouts: 397 us -> none  [the longest x16 260 us: relative_shift(): flipped = wide_scores[:, ::-1].reshape(2 * length * length)]
    all_gather x1 -> x0, waiting for transfers between devices: 278 us -> none  [body(): gathered = lax.all_gather(pos_store, 'ctx', axis=0, tiled=True)]
    dot_general x146 -> x2, matrix products: 175 us -> 3.81 us  [the longest x1 2.41 us: nt(): lax.dot_general(a, b, (((1,), (1,)), ((), ())), preferred_element_type=jn...]
    reshape x49 -> x0, local copies, waits for them, and re-layouts: 107 us -> none  [the longest x16 57.5 us: relative_shift(): return kept.reshape(length, 2 * length - 1)[:, :length]]
    slice x49 -> x0, local copies, waits for them, and re-layouts: 51.8 us -> none  [the longest x28 23.8 us: relative_shift(): return kept.reshape(length, 2 * length - 1)[:, :length]]
    while x188 -> x0, local copies, waits for them, and re-layouts: 50.2 us -> none
    pallas_call x0 -> x1, Pallas kernels: none -> 35.5 us  [pair_call(): pl.pallas_call(pair_kernel, grid_spec=pltpu.PrefetchScalarGridSpec(num_sc...]
  transfers between devices with their start and end apart: 11 -> 9, of which waited for: 10 -> 5; matrix products, arithmetic and copies ran while one was open for 2% -> 4% of each run, Pallas kernels for 0% -> 0%
where the time goes in v1:
time: 227 us; the launch traced here: 224 us
  waiting for transfers between devices  95.2 us (42%)
  starting transfers between devices  38.7 us (17%)
  Pallas kernels  35.5 us (16%)
  blocking collectives  25.1 us (11%)
  between operations  14.2 us (6%)
  local copies, waits for them, and re-layouts  6.03 us (3%)
  other arithmetic  5.41 us (2%)
  matrix products  3.81 us (2%)
    ppermute x6, waiting for transfers between devices, shifted(): lax.ppermute(block, 'ctx', [(i, (i + distance) % count) for i in range(co...  87.4 us
    pallas_call x1, Pallas kernels, pair_call(): pl.pallas_call(pair_kernel, grid_spec=pltpu.PrefetchScalarGridSpec(num_sc...  35.5 us
    all_to_all x1, blocking collectives, body(): lax.all_to_all(weight_term.reshape(slot_count, -1, features), 'ctx', 0, 0)  25.1 us
    ppermute x6, starting transfers between devices, shifted(): lax.ppermute(block, 'ctx', [(i, (i + distance) % count) for i in range(co...  20.5 us
    all_to_all x1, starting transfers between devices, body(): lax.all_to_all(jnp.broadcast_to(pos_store[None], (slot_count,) + pos_stor...  12.8 us
    all_gather x1, waiting for transfers between devices, body(): full_grad = lax.all_gather(d_layer, 'head', axis=1, tiled=True)  7.19 us
    all_to_all x1, starting transfers between devices, body(): lax.all_to_all(dist.reshape(slot_count, -1, features), 'ctx', 0, 0)  5.35 us
  transfers between devices with their start and end apart: 9, of which 5 were waited for; matrix products, arithmetic and copies ran while one was open for 4% of the time, Pallas kernels for 0%

profile of v1, /device:TPU:16, one launch (start us, length us, event | category | flops | bytes accessed | tf_op | source)
XLA Modules:
  0.0 223.9 jit_solution(4087603754654807003)
XLA Ops:
  7.2 0.0 copy-start
  7.2 0.0 copy-start.7
  7.2 0.0 copy-start.8
  7.2 1.9 broadcast_in_dim.12
  9.1 0.0 copy-start.9
  9.1 12.8 %all-to-all-start = ((bf16[64,32,256]{2,1,0:T(8,128)(2,1)}), bf16[64,32,256]{2,1,0:T(8,128)(2,1)S(1)}, u32[]{:S(2)}, u32[]{:S(2)}) async-start(bf16[64,32,256]{2,1,0:T(8,128)(2,1)} %broadcast_in_dim.12), calls=%async_computation | async-start | bytes 2097152 | tf_op jit(solution)/shard_map/all_to_all | solution.py:195
  21.9 0.0 all-gather.2.cloned.1.call-start
  22.0 0.7 all-gather.2.cloned.1.call-update
  22.7 0.0 copy-done.7
  22.7 0.0 copy-done.8
  22.7 0.1 pad_maximum_fusion.kv0
  22.7 0.0 copy-start.2
  22.7 1.6 collective-permute-start
  24.4 2.7 %collective-permute-start.2 = (bf16[2,512,256]{2,1,0:T(8,128)(2,1)S(1)}, bf16[2,512,256]{2,1,0:T(8,128)(2,1)S(1)}, u32[]{:S(2)}, u32[]{:S(2)}) collective-permute-start(bf16[2,512,256]{2,1,0:T(8,128)(2,1)S(1)} %pad_maximum_fusion.kv0), channel_id=1, source_target_pairs={{0,12},{4,16},{8,20},{12,24},{16,28},{20,32},{24,36},{28,40},{32,4... | collective-permute-start | bytes 1572872 | tf_op jit(solution)/shard_map/ppermute | solution.py:175
  27.1 42.5 %collective-permute-done.kv1 = bf16[2,512,256]{2,1,0:T(8,128)(2,1)S(1)} collective-permute-done((bf16[2,512,256]{2,1,0:T(8,128)(2,1)S(1)}, bf16[2,512,256]{2,1,0:T(8,128)(2,1)S(1)}, u32[]{:S(2)}, u32[]{:S(2)}) %collective-permute-start) | collective-permute-done | bytes 524320 | tf_op jit(solution)/shard_map/ppermute | solution.py:175
  69.5 0.0 copy-start.5
  69.5 0.0 collective-permute-start.1
  69.5 0.0 copy-done.9
  69.5 0.6 compare_select_fusion.flag_ref
  70.1 7.2 %all-gather.2.cloned.1.call-done = bf16[512,1024]{1,0:T(8,128)(2,1)} async-done(((bf16[512,256]{1,0:T(8,128)(2,1)}), bf16[512,1024]{1,0:T(8,128)(2,1)}) %all-gather.2.cloned.1.call-update) | async-done | bytes 1048592 | tf_op jit(solution)/shard_map/all_gather | solution.py:199
  77.3 0.0 copy-done
  77.3 2.4 %convolution_convert_fusion.1.ga_ref = bf16[512,256]{1,0:T(8,128)(2,1)} fusion(bf16[512,1024]{1,0:T(8,128)(2,1)} %all-gather.2.cloned.1.call-done, bf16[256,1024]{1,0:T(8,128)(2,1)S(1)} %copy-done), kind=kOutput, calls=%fused_computation.2 | convolution fusion | flops 268566528 | bytes 1835008 | tf_op jit(solution)/shard_map/dot_general | solution.py:14
  79.7 0.0 collective-permute-done.2.kv3
  79.7 0.0 copy-start.6
  79.7 7.8 %collective-permute-done.1.kv2 = bf16[2,512,256]{2,1,0:T(8,128)(2,1)} collective-permute-done((bf16[2,512,256]{2,1,0:T(8,128)(2,1)S(1)}, bf16[2,512,256]{2,1,0:T(8,128)(2,1)}, u32[]{:S(2)}, u32[]{:S(2)}) %collective-permute-start.1) | collective-permute-done | bytes 524320 | tf_op jit(solution)/shard_map/ppermute | solution.py:175
  87.5 0.0 all-to-all-done
  87.5 0.0 copy-start.1
  87.5 0.0 copy-done.2
  87.5 0.0 copy-done.5
  87.5 0.0 copy-done.6
  87.6 1.0 copy-done.1
  88.5 0.0 copy-start.3
  88.5 35.5 %shard_map.137 = (bf16[512,256]{1,0:T(8,128)(2,1)}, f32[2,512,256]{2,1,0:T(8,128)}, bf16[3,2,512,256]{3,2,1,0:T(8,128)(2,1)}, bf16[2048,256]{1,0:T(8,128)(2,1)}, bf16[512,256]{1,0:T(8,128)(2,1)}) custom-call(s32[64]{0:T(128)} %owner_ref.1, s32[4]{0:T(128)} %compare_select_fusion.flag_ref, bf16[512,256]{1,0:T(8,128)(2,1)} %q_ref.1, ...), custom_call_target="tpu_custom_call" | custom-call | tf_op jit(solution)/shard_map/pallas_call | solution.py:141
  124.0 0.0 copy-done.3
  124.0 1.4 fusion
  125.4 0.2 copy.15
  125.7 25.1 %all_to_all.15 = bf16[64,16,256]{2,1,0:T(8,128)(2,1)S(1)} all-to-all(bf16[64,16,256]{2,1,0:T(8,128)(2,1)S(1)} %bitcast.28), channel_id=1, replica_groups=mesh['ctx'=64,'head'=4] {'ctx'}, dimensions={0} | all-to-all | bytes 1048576 | tf_op jit(solution)/shard_map/all_to_all | solution.py:207
  150.7 5.4 %all-to-all-start.1 = ((bf16[64,32,256]{2,1,0:T(8,128)(2,1)}), bf16[64,32,256]{2,1,0:T(8,128)(2,1)S(1)}, u32[]{:S(2)}, u32[]{:S(2)}) async-start(bf16[64,32,256]{2,1,0:T(8,128)(2,1)} %bitcast.11), calls=%async_computation.1 | async-start | bytes 2097152 | tf_op jit(solution)/shard_map/all_to_all | solution.py:208
  156.1 2.1 slice_bitcast_fusion.1
  158.2 0.0 copy-start.4
  158.2 6.1 %collective-permute-start.4 = (bf16[2,512,256]{2,1,0:T(8,128)(2,1)S(1)}, bf16[2,512,256]{2,1,0:T(8,128)(2,1)S(1)}, u32[]{:S(2)}, u32[]{:S(2)}) collective-permute-start(bf16[2,512,256]{2,1,0:T(8,128)(2,1)S(1)} %get-tuple-element.16), channel_id=1, source_target_pairs={{0,252},{4,0},{8,4},{12,8},{16,12},{20,16},{24,20},{28,24},{32,28}... | collective-permute-start | bytes 1572872 | tf_op jit(solution)/shard_map/ppermute | solution.py:175
  164.3 0.0 collective-permute-start.3
  164.3 28.5 %collective-permute-done.4 = bf16[2,512,256]{2,1,0:T(8,128)(2,1)S(1)} collective-permute-done((bf16[2,512,256]{2,1,0:T(8,128)(2,1)S(1)}, bf16[2,512,256]{2,1,0:T(8,128)(2,1)S(1)}, u32[]{:S(2)}, u32[]{:S(2)}) %collective-permute-start.4) | collective-permute-done | bytes 524320 | tf_op jit(solution)/shard_map/ppermute | solution.py:175
  192.8 2.0 fusion.1
  194.7 10.1 %collective-permute-start.5 = (bf16[2,512,256]{2,1,0:T(8,128)(2,1)}, bf16[2,512,256]{2,1,0:T(8,128)(2,1)}, u32[]{:S(2)}, u32[]{:S(2)}) collective-permute-start(bf16[2,512,256]{2,1,0:T(8,128)(2,1)} %fusion.1), channel_id=1, source_target_pairs={{0,252},{4,0},{8,4},{12,8},{16,12},{20,16},{24,20},{28,24},{32,28}... | collective-permute-start | bytes 1572872 | tf_op jit(solution)/shard_map/ppermute | solution.py:175
  204.8 0.7 reduce_sum.25
  205.5 0.0 collective-permute-done.3
  205.5 8.6 %collective-permute-done.5 = bf16[2,512,256]{2,1,0:T(8,128)(2,1)} collective-permute-done((bf16[2,512,256]{2,1,0:T(8,128)(2,1)}, bf16[2,512,256]{2,1,0:T(8,128)(2,1)}, u32[]{:S(2)}, u32[]{:S(2)}) %collective-permute-start.5) | collective-permute-done | bytes 524320 | tf_op jit(solution)/shard_map/ppermute | solution.py:175
  214.1 0.0 copy-done.4
  214.1 1.4 add_convert_fusion
  215.4 0.8 slice_bitcast_fusion.2
  216.2 0.0 all-to-all-done.1
  216.3 0.8 reduce_sum.24
Async XLA Ops:
  7.2 70.1 %copy-start = (bf16[256,1024]{1,0:T(8,128)(2,1)S(1)}, bf16[256,1024]{1,0:T(8,128)(2,1)}, u32[]{:S(2)}) copy-start(bf16[256,1024]{1,0:T(8,128)(2,1)} %param.18) | copy-start | bytes 1572868
  7.2 15.5 %copy-start.7 = (bf16[512,256]{1,0:T(8,128)(2,1)S(1)}, bf16[512,256]{1,0:T(8,128)(2,1)}, u32[]{:S(2)}) copy-start(bf16[512,256]{1,0:T(8,128)(2,1)} %param.12) | copy-start | bytes 786436
  7.2 15.5 %copy-start.8 = (bf16[512,256]{1,0:T(8,128)(2,1)S(1)}, bf16[512,256]{1,0:T(8,128)(2,1)}, u32[]{:S(2)}) copy-start(bf16[512,256]{1,0:T(8,128)(2,1)} %param.11) | copy-start | bytes 786436
  9.1 60.4 %copy-start.9 = (s32[1,4]{1,0:T(1,128)S(1)}, s32[1,4]{1,0:T(1,128)}, u32[]{:S(2)}) copy-start(s32[1,4]{1,0:T(1,128)} %param.15) | copy-start | bytes 52
  9.1 78.4 %all-to-all-start = ((bf16[64,32,256]{2,1,0:T(8,128)(2,1)}), bf16[64,32,256]{2,1,0:T(8,128)(2,1)S(1)}, u32[]{:S(2)}, u32[]{:S(2)}) async-start(bf16[64,32,256]{2,1,0:T(8,128)(2,1)} %broadcast_in_dim.12), calls=%async_computation | async-start | bytes 2097152 | tf_op jit(solution)/shard_map/all_to_all | solution.py:195
  21.9 55.4 %all-gather.2.cloned.1.call-start = ((), (), s32[]{:S(2)}) async-start(), calls=%async_computation.3 | async-start | bytes 1310720 | tf_op jit(solution)/shard_map/all_gather | solution.py:199
  22.7 64.8 %copy-start.2 = (bf16[2,512,256]{2,1,0:T(8,128)(2,1)}, bf16[2,512,256]{2,1,0:T(8,128)(2,1)S(1)}, u32[]{:S(2)}) copy-start(bf16[2,512,256]{2,1,0:T(8,128)(2,1)S(1)} %pad_maximum_fusion.kv0) | copy-start | bytes 1572868
  22.7 46.8 %collective-permute-start = (bf16[2,512,256]{2,1,0:T(8,128)(2,1)S(1)}, bf16[2,512,256]{2,1,0:T(8,128)(2,1)S(1)}, u32[]{:S(2)}, u32[]{:S(2)}) collective-permute-start(bf16[2,512,256]{2,1,0:T(8,128)(2,1)S(1)} %pad_maximum_fusion.kv0), channel_id=1, source_target_pairs={{0,4},{4,8},{8,12},{12,16},{16,20},{20,24},{24,28},{28,32},{32,36}... | collective-permute-start | bytes 1572872 | tf_op jit(solution)/shard_map/ppermute | solution.py:175
  24.4 55.3 %collective-permute-start.2 = (bf16[2,512,256]{2,1,0:T(8,128)(2,1)S(1)}, bf16[2,512,256]{2,1,0:T(8,128)(2,1)S(1)}, u32[]{:S(2)}, u32[]{:S(2)}) collective-permute-start(bf16[2,512,256]{2,1,0:T(8,128)(2,1)S(1)} %pad_maximum_fusion.kv0), channel_id=1, source_target_pairs={{0,12},{4,16},{8,20},{12,24},{16,28},{20,32},{24,36},{28,40},{32,4... | collective-permute-start | bytes 1572872 | tf_op jit(solution)/shard_map/ppermute | solution.py:175
  69.5 18.0 %copy-start.5 = (bf16[2,512,256]{2,1,0:T(8,128)(2,1)}, bf16[2,512,256]{2,1,0:T(8,128)(2,1)S(1)}, u32[]{:S(2)}) copy-start(bf16[2,512,256]{2,1,0:T(8,128)(2,1)S(1)} %collective-permute-done.kv1) | copy-start | bytes 1572868
  69.5 18.0 %collective-permute-start.1 = (bf16[2,512,256]{2,1,0:T(8,128)(2,1)S(1)}, bf16[2,512,256]{2,1,0:T(8,128)(2,1)}, u32[]{:S(2)}, u32[]{:S(2)}) collective-permute-start(bf16[2,512,256]{2,1,0:T(8,128)(2,1)S(1)} %collective-permute-done.kv1), channel_id=1, source_target_pairs={{0,4},{4,8},{8,12},{12,16},{16,20},{20,24},{24,28},{28,32},{32,36}... | collective-permute-start | bytes 1572872 | tf_op jit(solution)/shard_map/ppermute | solution.py:175
  79.7 7.8 %copy-start.6 = (bf16[2,512,256]{2,1,0:T(8,128)(2,1)}, bf16[2,512,256]{2,1,0:T(8,128)(2,1)S(1)}, u32[]{:S(2)}) copy-start(bf16[2,512,256]{2,1,0:T(8,128)(2,1)S(1)} %collective-permute-done.2.kv3) | copy-start | bytes 1572868
  87.5 1.0 copy-start.1
  88.5 35.5 %copy-start.3 = (bf16[512,1024]{1,0:T(8,128)(2,1)S(1)}, bf16[512,1024]{1,0:T(8,128)(2,1)}, u32[]{:S(2)}) copy-start(bf16[512,1024]{1,0:T(8,128)(2,1)} %all-gather.2.cloned.1.call-done) | copy-start | bytes 3145732
  150.7 65.5 %all-to-all-start.1 = ((bf16[64,32,256]{2,1,0:T(8,128)(2,1)}), bf16[64,32,256]{2,1,0:T(8,128)(2,1)S(1)}, u32[]{:S(2)}, u32[]{:S(2)}) async-start(bf16[64,32,256]{2,1,0:T(8,128)(2,1)} %bitcast.11), calls=%async_computation.1 | async-start | bytes 2097152 | tf_op jit(solution)/shard_map/all_to_all | solution.py:208
  158.2 55.9 %copy-start.4 = (f32[2,512,256]{2,1,0:T(8,128)S(1)}, f32[2,512,256]{2,1,0:T(8,128)}, u32[]{:S(2)}) copy-start(f32[2,512,256]{2,1,0:T(8,128)} %get-tuple-element.11) | copy-start | bytes 3145732
  158.2 34.6 %collective-permute-start.4 = (bf16[2,512,256]{2,1,0:T(8,128)(2,1)S(1)}, bf16[2,512,256]{2,1,0:T(8,128)(2,1)S(1)}, u32[]{:S(2)}, u32[]{:S(2)}) collective-permute-start(bf16[2,512,256]{2,1,0:T(8,128)(2,1)S(1)} %get-tuple-element.16), channel_id=1, source_target_pairs={{0,252},{4,0},{8,4},{12,8},{16,12},{20,16},{24,20},{28,24},{32,28}... | collective-permute-start | bytes 1572872 | tf_op jit(solution)/shard_map/ppermute | solution.py:175
  164.3 41.2 %collective-permute-start.3 = (bf16[2,512,256]{2,1,0:T(8,128)(2,1)}, bf16[2,512,256]{2,1,0:T(8,128)(2,1)}, u32[]{:S(2)}, u32[]{:S(2)}) collective-permute-start(bf16[2,512,256]{2,1,0:T(8,128)(2,1)} %get-tuple-element.15), channel_id=1, source_target_pairs={{0,244},{4,248},{8,252},{12,0},{16,4},{20,8},{24,12},{28,16},{32,2... | collective-permute-start | bytes 1572872 | tf_op jit(solution)/shard_map/ppermute | solution.py:175
  194.7 19.3 %collective-permute-start.5 = (bf16[2,512,256]{2,1,0:T(8,128)(2,1)}, bf16[2,512,256]{2,1,0:T(8,128)(2,1)}, u32[]{:S(2)}, u32[]{:S(2)}) collective-permute-start(bf16[2,512,256]{2,1,0:T(8,128)(2,1)} %fusion.1), channel_id=1, source_target_pairs={{0,252},{4,0},{8,4},{12,8},{16,12},{20,16},{24,20},{28,24},{32,28}... | collective-permute-start | bytes 1572872 | tf_op jit(solution)/shard_map/ppermute | solution.py:175
Sparse Core Ops, SparseCore 0:
  24.6 52.6 all-gather.1

commit v2 on v1

v2 whole, which is shorter than its diff:
```python
import functools

import jax
import jax.numpy as jnp
from jax import lax
from jax.experimental import pallas as pl
from jax.experimental.pallas import tpu as pltpu
from jax.sharding import PartitionSpec as P

HD = 64
LANES = 128
NEG = -1e30
ROW = 4
BF = jnp.bfloat16
F32 = jnp.float32


def nt(a, b):
    return lax.dot_general(a, b, (((1,), (1,)), ((), ())), preferred_element_type=F32)


def nn(a, b):
    return lax.dot_general(a, b, (((1,), (0,)), ((), ())), preferred_element_type=F32)


def tn(a, b):
    return lax.dot_general(a, b, (((0,), (0,)), ((), ())), preferred_element_type=F32)


def lanes():
    return lax.broadcasted_iota(jnp.int32, (1, LANES), 1)


def turned(block, shift=HD):
    return pltpu.roll(block.astype(F32), shift, 1)


def joined(low, high):
    return jnp.where(lanes() < HD, low.astype(F32), high.astype(F32))


def of_head(array, head):
    pair = array[:, head // 2 * LANES : (head // 2 + 1) * LANES]
    return turned(pair) if head % 2 else pair.astype(F32)


def halves(array, head):
    both = of_head(array, head)
    middle = both.shape[0] // 2
    return joined(both[:middle], turned(both[middle:]))


def whole_of(first, second):
    top = joined(first, turned(second))
    bottom = joined(turned(first), second)
    return jnp.concatenate([top, bottom], axis=0)


def anti_diagonal(size):
    row = lax.broadcasted_iota(jnp.int32, (size, size), 0)
    col = lax.broadcasted_iota(jnp.int32, (size, size), 1)
    return (row + col == size - 1).astype(F32).astype(BF)


def vmem_specs(count):
    return [pl.BlockSpec(memory_space=pltpu.VMEM)] * count


def smem_specs(count):
    return [pl.BlockSpec(memory_space=pltpu.SMEM)] * count


def any_specs(count):
    return [pl.BlockSpec(memory_space=pltpu.HBM)] * count


def whole_spec(shape):
    return pl.BlockSpec(shape, lambda *_: (0,) * len(shape))


def brought(pairs, sems):
    copies = [
        pltpu.make_async_copy(source, target, sems.at[i])
        for i, (source, target) in enumerate(pairs)
    ]
    for copy in copies:
        copy.start()
    for copy in copies:
        copy.wait()


def pack_kernel(mask_ref, q_in, k_in, v_in, pos_in, out_ref, q_ref, k_ref, v_ref, pos_ref, sems):
    brought([(q_in, q_ref), (k_in, k_ref), (v_in, v_ref), (pos_in, pos_ref)], sems)
    tokens = q_ref.shape[0]
    half = tokens // 2
    rows = pos_ref.shape[0] // 2
    flags = jnp.zeros((rows, LANES), F32)
    for lag in range(mask_ref.shape[1]):
        flags = jnp.where(lanes() == lag, mask_ref[0, lag].astype(F32), flags)
    for h in range(ROW):
        out_ref[h, :tokens, :] = joined(of_head(k_ref, h), turned(of_head(v_ref, h))).astype(BF)
        out_ref[h, tokens : tokens + half, :] = halves(q_ref, h).astype(BF)
        at = tokens + half
        out_ref[h, at : at + rows, :] = halves(pos_ref, h).astype(BF)
        out_ref[h, at + rows :, :] = flags.astype(BF)


def pack_call(mask, q, k, v, pos):
    tokens = q.shape[0]
    rows = tokens + tokens // 2 + pos.shape[0]
    return pl.pallas_call(
        pack_kernel,
        in_specs=smem_specs(1) + any_specs(4),
        out_shape=pltpu.HBM((ROW, rows, LANES), BF),
        scratch_shapes=[pltpu.VMEM(a.shape, BF) for a in (q, k, v, pos)]
        + [pltpu.SemaphoreType.DMA((4,))],
        compiler_params=pltpu.CompilerParams(vmem_limit_bytes=60 << 20),
    )(mask, q, k, v, pos)


def mix_kernel(
    place_ref, g0_in, g1_in, g2_in, g3_in, weight_in, out_ref, g0, g1, g2, g3, weight_ref, sems
):
    brought(
        [(g0_in, g0), (g1_in, g1), (g2_in, g2), (g3_in, g3), (weight_in, weight_ref)], sems
    )
    features = g0.shape[1]
    mixed = None
    for b, grad in enumerate((g0, g1, g2, g3)):
        at = pl.multiple_of((place_ref[0] ^ b) * features, features)
        part = nt(grad[...], weight_ref[:, pl.ds(at, features)])
        mixed = part if mixed is None else mixed + part
    mixed = mixed.astype(BF)
    for h in range(ROW):
        out_ref[h] = halves(mixed, h).astype(BF)


def mix_call(place, grads, out_weight):
    tokens = grads[0].shape[0]
    return pl.pallas_call(
        mix_kernel,
        in_specs=smem_specs(1) + any_specs(5),
        out_shape=pltpu.HBM((ROW, tokens // 2, LANES), BF),
        scratch_shapes=[pltpu.VMEM(a.shape, BF) for a in (*grads, out_weight)]
        + [pltpu.SemaphoreType.DMA((5,))],
        compiler_params=pltpu.CompilerParams(vmem_limit_bytes=60 << 20),
    )(place, *grads, out_weight)


def key_pairs(row_in, halo_in, keys, query, tokens):
    pairs = [(halo_in.at[b], keys.at[b * tokens : (b + 1) * tokens]) for b in range(ROW - 1)]
    for b in range(ROW):
        at = (ROW - 1 + b) * tokens
        pairs.append((row_in.at[b, 0:tokens], keys.at[at : at + tokens]))
        pairs.append((row_in.at[b, tokens : tokens + tokens // 2], query.at[b]))
    return pairs


def core_kernel(
    owner_ref, flag_ref, row_in, halo_in, slots_in, ga_in, cb_ref, pb_ref,
    near_ref, own_ref, far_ref, dpos_ref,
    keys, queries, slots_ref, ga_ref, table, flipped, grads, dist, sems,
):
    tokens = halo_in.shape[1]
    half = tokens // 2
    span = ROW * tokens
    wide = span + half
    block = pl.program_id(0)
    anti = anti_diagonal(half)

    @pl.when(block == 0)
    def _():
        pairs = key_pairs(row_in, halo_in, keys, queries, tokens)
        brought(pairs + [(slots_in, slots_ref), (ga_in, ga_ref)], sems)
        grads[...] = jnp.zeros_like(grads)
        dist[...] = jnp.zeros_like(dist)
        table[0:tokens, :] = jnp.zeros((tokens, LANES), BF)
        count, rows = slots_ref.shape[:2]
        for d in range(count):
            both = slots_ref[owner_ref[d]]
            at = tokens + 2 * d * rows
            table[at : at + rows, :] = both
            table[at + rows : at + 2 * rows, :] = turned(both).astype(BF)
        parts = (tokens + span) // half
        for i in range(parts):
            flipped[(parts - 1 - i) * half : (parts - i) * half, :] = nn(
                anti, table[i * half : (i + 1) * half, :]
            ).astype(BF)

    lane = lanes()
    low = lane < HD
    scale = jnp.asarray(0.125, BF)
    starts = [pl.multiple_of((block + w) * tokens, tokens) for w in range(ROW)]
    kept = []
    dqs = []
    for r in range(2):
        query = queries[block].astype(F32)
        ga = ga_ref[block].astype(F32)
        query = turned(query) if r == 1 else query
        ga = turned(ga) if r == 0 else ga
        ga = jnp.where(low, 0.0, ga)
        cq = jnp.where(low, query + cb_ref[...], 0.0).astype(BF)
        pq = jnp.where(low, query + pb_ref[...], 0.0).astype(BF)
        cqs = cq * scale
        pqs = pq * scale
        base = half * (1 - r)
        rel = nt(pqs, flipped[base : base + wide, :])
        rel = pltpu.roll(rel, span + 1, 1, stride=1, stride_axis=0)
        scores = []
        for w in range(ROW):
            s = nt(cqs, keys[pl.ds(starts[w], tokens), :]) + rel[:, w * tokens : (w + 1) * tokens]
            if w == ROW - 1:
                row = lax.broadcasted_iota(jnp.int32, (half, tokens), 0) + r * half
                col = lax.broadcasted_iota(jnp.int32, (half, tokens), 1)
                s = jnp.where(col <= row, s, NEG)
            else:
                s = jnp.where(flag_ref[block, ROW - 1 - w] == 1, s, NEG)
            scores.append(s)
        top = functools.reduce(jnp.maximum, [jnp.max(s, axis=1, keepdims=True) for s in scores])
        weights = [jnp.exp(s - top) for s in scores]
        total = functools.reduce(jnp.add, [jnp.sum(e, axis=1, keepdims=True) for e in weights])
        inv = 1.0 / total
        probs = [e * inv for e in weights]
        lows = [p.astype(BF) for p in probs]
        att = None
        for w in range(ROW):
            part = nn(lows[w], keys[pl.ds(starts[w], tokens), :])
            att = part if att is None else att + part
        att = att.astype(BF).astype(F32)
        kept.append(turned(att) if r == 0 else att)
        dot = jnp.sum(ga * att, axis=1, keepdims=True)
        ga = ga.astype(BF)
        flips = [None] * (2 * ROW)
        acc = None
        for w in range(ROW):
            window = keys[pl.ds(starts[w], tokens), :]
            ds = (0.125 * probs[w] * (nt(ga, window) - dot)).astype(BF)
            grads[:, pl.ds(starts[w], tokens)] += tn(cq, ds) + tn(ga, lows[w])
            part = nn(ds, window)
            acc = part if acc is None else acc + part
            for x in range(2):
                flips[2 * ROW - 1 - (2 * w + x)] = nn(ds[:, x * half : (x + 1) * half], anti)
        spread = jnp.concatenate(flips + [jnp.zeros((half, half), F32)], axis=1)
        spread = pltpu.roll(spread, 1, 1, stride=1, stride_axis=0).astype(BF)
        start = half * r
        acc = acc + nn(spread, table[start : start + wide, :])
        dist[:, start : start + wide] += tn(pq, spread)
        dqs.append(turned(acc) if r == 1 else acc)
    near_ref[block, :half, :] = joined(kept[0], kept[1]).astype(BF)
    near_ref[block, half:, :] = joined(dqs[0], dqs[1]).astype(BF)

    @pl.when(block == ROW - 1)
    def _():
        for b in range(ROW - 1):
            far_ref[b] = grads[:, b * tokens : (b + 1) * tokens].T.astype(BF)
        for b in range(ROW):
            at = (ROW - 1 + b) * tokens
            own_ref[b] = grads[:, at : at + tokens].T
        count, rows = dpos_ref.shape[:2]
        table_grad = dist[:, tokens:].T
        other = pltpu.roll(table_grad, HD, 1)
        for d in range(count):
            at = 2 * d * rows
            dpos_ref[owner_ref[d]] = joined(
                table_grad[at : at + rows], other[at + rows : at + 2 * rows]
            ).astype(BF)


def core_call(owner, flags, row, halo, slots, ga, cb, pb):
    tokens = halo.shape[1]
    half = tokens // 2
    slot_count, packed_rows = slots.shape[:2]
    rel = slot_count * packed_rows * 2
    shapes = [
        ((ROW, tokens, LANES), BF), ((ROW, tokens, LANES), F32), ((ROW - 1, tokens, LANES), BF),
        ((slot_count, packed_rows, LANES), BF),
    ]
    return pl.pallas_call(
        core_kernel,
        grid=(ROW,),
        in_specs=smem_specs(2) + any_specs(4) + vmem_specs(2),
        out_specs=[whole_spec(shape) for shape, _ in shapes],
        out_shape=[pltpu.HBM(shape, dtype) for shape, dtype in shapes],
        scratch_shapes=[
            pltpu.VMEM(((2 * ROW - 1) * tokens, LANES), BF),
            pltpu.VMEM((ROW, half, LANES), BF),
            pltpu.VMEM(slots.shape, BF),
            pltpu.VMEM((ROW, half, LANES), BF),
            pltpu.VMEM((tokens + rel, LANES), BF),
            pltpu.VMEM((tokens + rel, LANES), BF),
            pltpu.VMEM((LANES, (2 * ROW - 1) * tokens), F32),
            pltpu.VMEM((LANES, tokens + rel), F32),
            pltpu.SemaphoreType.DMA((3 * ROW + 1,)),
        ],
        compiler_params=pltpu.CompilerParams(vmem_limit_bytes=60 << 20),
        cost_estimate=pl.CostEstimate(
            flops=40_000_000_000, bytes_accessed=8_000_000, transcendentals=0
        ),
    )(owner, flags, row, halo, slots, ga, cb, pb)


def weight_kernel(
    place_ref, att_in, g0_in, g1_in, g2_in, g3_in, dpos_in, out_ref,
    att_ref, g0, g1, g2, g3, dpos_ref, sems,
):
    half = att_ref.shape[1]
    sources = [att_in.at[:, 0:half], g0_in, g1_in, g2_in, g3_in, dpos_in]
    brought(zip(sources, [att_ref, g0, g1, g2, g3, dpos_ref]), sems)
    rows = dpos_ref.shape[1]
    features = g0.shape[1]
    chunks = features // rows
    out_ref[:, :rows, :] = dpos_ref[...]
    for pair in range(features // LANES):
        att = whole_of(att_ref[2 * pair], att_ref[2 * pair + 1]).astype(BF)
        at = rows * (1 + pair)
        for b, grad in enumerate((g0, g1, g2, g3)):
            term = tn(att, grad[...]).T.astype(BF)
            out_ref[pl.ds((place_ref[0] ^ b) * chunks, chunks), at : at + rows, :] = term.reshape(
                chunks, rows, LANES
            )


def weight_call(place, att, grads, dpos):
    slot_count, rows = dpos.shape[:2]
    pairs = grads[0].shape[1] // LANES
    return pl.pallas_call(
        weight_kernel,
        in_specs=smem_specs(1) + any_specs(6),
        scratch_shapes=[pltpu.VMEM((ROW, grads[0].shape[0] // 2, LANES), BF)]
        + [pltpu.VMEM(a.shape, BF) for a in (*grads, dpos)]
        + [pltpu.SemaphoreType.DMA((6,))],
        out_shape=pltpu.HBM((slot_count, rows * (1 + pairs), LANES), BF),
        compiler_params=pltpu.CompilerParams(vmem_limit_bytes=60 << 20),
    )(place, att, *grads, dpos)


def meet_kernel(own_in, far_in, parts_in, out_ref, own_ref, far_ref, parts_ref, sems):
    sources = [own_in, far_in, parts_in]
    brought(zip(sources, [own_ref, far_ref, parts_ref]), sems)
    tokens = own_ref.shape[1]
    for b in range(ROW):
        grad = own_ref[b]
        if b > 0:
            grad = grad + far_ref[b - 1].astype(F32)
        out_ref[b, :tokens, :] = grad.astype(BF)
        total = parts_ref[0, b].astype(F32)
        for z in range(1, parts_ref.shape[0]):
            total = total + parts_ref[z, b].astype(F32)
        out_ref[b, tokens:, :] = total.astype(BF)


def meet_call(own, far, parts):
    rows = own.shape[1] + parts.shape[2]
    return pl.pallas_call(
        meet_kernel,
        in_specs=any_specs(3),
        out_shape=pltpu.HBM((ROW, rows, LANES), BF),
        scratch_shapes=[pltpu.VMEM(a.shape, a.dtype) for a in (own, far, parts)]
        + [pltpu.SemaphoreType.DMA((3,))],
        compiler_params=pltpu.CompilerParams(vmem_limit_bytes=60 << 20),
    )(own, far, parts)


def final_kernel(
    in_in, near_in, dq_ref, dk_ref, dv_ref, dpos_ref, dw_ref, in_ref, near_ref, sems
):
    tokens = dq_ref.shape[0]
    brought([(in_in, in_ref), (near_in.at[:, tokens // 2 :], near_ref)], sems)
    rows = dpos_ref.shape[0] // 2
    at = tokens
    for pair in range(ROW // 2):
        cols = slice(pair * LANES, (pair + 1) * LANES)
        dq_ref[:, cols] = whole_of(near_ref[2 * pair], near_ref[2 * pair + 1]).astype(BF)
        first, second = in_ref.at[2 * pair], in_ref.at[2 * pair + 1]
        a, b = first[:at, :], second[:at, :]
        dk_ref[:, cols] = joined(a, turned(b)).astype(BF)
        dv_ref[:, cols] = joined(turned(a), b).astype(BF)
        dpos_ref[:, cols] = whole_of(first[at : at + rows, :], second[at : at + rows, :]).astype(BF)
        lo = at + rows * (1 + pair)
        total = in_ref[0, lo : lo + rows, :].astype(F32)
        for x in range(1, ROW):
            total = total + in_ref[x, lo : lo + rows, :].astype(F32)
        dw_ref[:, cols] = total.astype(BF)


def final_call(arrived, near, features, slot_rows, out_rows):
    tokens = near.shape[1]
    shapes = [(tokens, features)] * 3 + [(slot_rows, features), (out_rows, features)]
    return pl.pallas_call(
        final_kernel,
        in_specs=any_specs(2),
        out_shape=[jax.ShapeDtypeStruct(shape, BF) for shape in shapes],
        scratch_shapes=[
            pltpu.VMEM(arrived.shape, BF),
            pltpu.VMEM((ROW, tokens // 2, LANES), BF),
            pltpu.SemaphoreType.DMA((2,)),
        ],
        compiler_params=pltpu.CompilerParams(vmem_limit_bytes=60 << 20),
    )(arrived, near)


def shifted(block, distance):
    count = lax.axis_size("ctx")
    return lax.ppermute(block, "ctx", [(i, (i + distance) % count) for i in range(count)])


def swapped(block, bit):
    return lax.ppermute(block, "head", [(i, i ^ bit) for i in range(lax.axis_size("head"))])


def in_row(block):
    count = lax.axis_size("ctx")
    groups = [list(range(r, r + ROW)) for r in range(0, count, ROW)]
    return lax.all_to_all(block, "ctx", 0, 0, axis_index_groups=groups)


def in_column(block):
    count = lax.axis_size("ctx")
    groups = [list(range(x, count, ROW)) for x in range(ROW)]
    return lax.all_to_all(block, "ctx", 0, 0, axis_index_groups=groups)


def body(
    query, key, value, pos_store, owner, block_mask, content_bias, pos_bias, out_weight, d_layer
):
    tokens, features = query.shape
    window = block_mask.shape[1]
    slot_count = owner.shape[0]
    slot_rows = pos_store.shape[0]
    half = tokens // 2
    block_index = lax.axis_index("ctx")
    place = lax.axis_index("head").astype(jnp.int32)[None]
    mine = block_index % ROW

    def bias_of(bias):
        part = lax.dynamic_slice_in_dim(bias, mine * HD, HD)
        return jnp.pad(part, (0, LANES - HD))[None]

    cb, pb = bias_of(content_bias), bias_of(pos_bias)
    across = swapped(d_layer, 2)
    row = in_row(pack_call(block_mask, query, key, value, pos_store))
    halo = shifted(row[1:, :tokens], ROW)
    at = tokens + half
    pos = row[:, at : at + slot_rows // 2]
    grads = [d_layer, swapped(d_layer, 1), across, swapped(across, 1)]
    mixed = mix_call(place, grads, out_weight)
    ga = in_row(mixed)
    pos, halo, ga = lax.optimization_barrier((pos, halo, ga))
    slots = in_column(jnp.broadcast_to(pos[None], (slot_count // ROW,) + pos.shape))
    slots = slots.reshape(slot_count, slot_rows // 2, LANES)
    flags = row[:, at + slot_rows // 2, :window].astype(jnp.int32)
    blocks = block_index - mine + jnp.arange(ROW)
    flags = flags * (blocks[:, None] >= jnp.arange(window)[None]).astype(jnp.int32)

    near, own, far, dpos = core_call(owner, flags, row, halo, slots, ga, cb, pb)
    back = shifted(far, -ROW)
    near = in_row(near)
    near, back = lax.optimization_barrier((near, back))
    sums = weight_call(place, near, grads, dpos)
    parts = in_column(sums.reshape((slot_count // ROW, ROW) + sums.shape[1:]))
    arrived = in_row(meet_call(own, back, parts))
    grad_query, grad_key, grad_value, grad_pos, grad_weight = final_call(
        arrived, near, features, slot_rows, slot_rows // 2
    )
    return grad_query, grad_key, grad_value, grad_pos, grad_weight.T


def solution(mesh):
    spread = P("ctx", "head")
    return jax.shard_map(
        body,
        mesh=mesh,
        in_specs=(
            spread, spread, spread, spread, P(), P("ctx", None), P("head"), P("head"),
            P("head", None), spread,
        ),
        out_specs=(spread, spread, spread, spread, P("head", "ctx")),
        check_vma=False,
    )
```

time: 227 us -> 150 us (0.66)
  waiting for transfers between devices: 95.2 us -> 33.8 us
  starting transfers between devices: 38.7 us -> 23.6 us
  Pallas kernels: 35.5 us -> 49 us
  between operations: 14.2 us -> 0.98 us
  blocking collectives: 25.1 us -> 35.5 us
  other arithmetic: 5.41 us -> 0.66 us
  matrix products: 3.81 us -> 0 us
    ppermute x6 -> x2, waiting for transfers between devices: 87.4 us -> 0.01 us  [shifted(): lax.ppermute(block, 'ctx', [(i, (i + distance) % count) for i in range(co...]
    all_to_all x2 -> x4, waiting for transfers between devices: 0.01 us -> 25.9 us  [the longest x3 15.8 us: in_row(): return lax.all_to_all(block, 'ctx', 0, 0, axis_index_groups=groups)]
    ppermute x6 -> x2, starting transfers between devices: 20.5 us -> 1.54 us  [shifted(): lax.ppermute(block, 'ctx', [(i, (i + distance) % count) for i in range(co...]
    pallas_call x1 -> x6, Pallas kernels: 35.5 us -> 49 us  [the longest x1 35.1 us: core_call(): pl.pallas_call(core_kernel, grid=(ROW,), in_specs=smem_specs(2) + any_spe...]
    all_to_all x1 -> x2, blocking collectives: 25.1 us -> 35.5 us  [the longest x1 22.9 us: in_column(): return lax.all_to_all(block, 'ctx', 0, 0, axis_index_groups=groups)]
    ppermute x0 -> x3, waiting for transfers between devices: none -> 7.9 us  [swapped(): lax.ppermute(block, 'head', [(i, i ^ bit) for i in range(lax.axis_size('h...]
    all_gather x1 -> x0, waiting for transfers between devices: 7.19 us -> none  [body(): full_grad = lax.all_gather(d_layer, 'head', axis=1, tiled=True)]
    dot_general x2 -> x0, matrix products: 3.81 us -> none  [the longest x1 2.41 us: nt(): lax.dot_general(a, b, (((1,), (1,)), ((), ())), preferred_element_type=jn...]
  transfers between devices with their start and end apart: 9 -> 9, of which waited for: 5 -> 5; matrix products, arithmetic and copies ran while one was open for 4% -> 1% of each run, Pallas kernels for 0% -> 2%
where the time goes in v2:
time: 150 us; the launch traced here: 149 us
  Pallas kernels  49 us (33%)
  blocking collectives  35.5 us (24%)
  waiting for transfers between devices  33.8 us (23%)
  starting transfers between devices  23.6 us (16%)
  local copies, waits for them, and re-layouts  5.31 us (4%)
    pallas_call x1, Pallas kernels, core_call(): pl.pallas_call(core_kernel, grid=(ROW,), in_specs=smem_specs(2) + any_spe...  35.1 us
    all_to_all x1, blocking collectives, in_column(): return lax.all_to_all(block, 'ctx', 0, 0, axis_index_groups=groups)  22.9 us
    all_to_all x3, waiting for transfers between devices, in_row(): return lax.all_to_all(block, 'ctx', 0, 0, axis_index_groups=groups)  15.8 us
    all_to_all x1, blocking collectives, in_row(): return lax.all_to_all(block, 'ctx', 0, 0, axis_index_groups=groups)  12.6 us
    all_to_all x3, starting transfers between devices, in_row(): return lax.all_to_all(block, 'ctx', 0, 0, axis_index_groups=groups)  11.5 us
    all_to_all x1, waiting for transfers between devices, in_column(): return lax.all_to_all(block, 'ctx', 0, 0, axis_index_groups=groups)  10.1 us
    all_to_all x1, starting transfers between devices, in_column(): return lax.all_to_all(block, 'ctx', 0, 0, axis_index_groups=groups)  9.22 us
    ppermute x3, waiting for transfers between devices, swapped(): lax.ppermute(block, 'head', [(i, i ^ bit) for i in range(lax.axis_size('h...  7.9 us
  transfers between devices with their start and end apart: 9, of which 5 were waited for; matrix products, arithmetic and copies ran while one was open for 1% of the time, Pallas kernels for 2%

profile of v2, /device:TPU:16, one launch (start us, length us, event | category | flops | bytes accessed | tf_op | source)
XLA Modules:
  0.0 148.9 jit_solution(10844242776802252604)
XLA Ops:
  0.6 3.4 %shard_map.137 = bf16[4,800,128]{2,1,0:T(8,128)(2,1)} custom-call(s32[1,4]{1,0:T(1,128)} %mask_ref.1, bf16[512,256]{1,0:T(8,128)(2,1)} %q_in.1, bf16[512,256]{1,0:T(8,128)(2,1)} %k_in.1, bf16[512,256]{1,0:T(8,128)(2,1)} %v_in.1, bf16[32,256]{1,0:T(8,128)(2,1)} %pos_in.1), custom_call_target="tpu_custom_call" | custom-call | tf_op jit(solution)/shard_map/pallas_call | solution.py:111
  4.1 0.0 copy-start.2
  4.1 4.4 %all-to-all-start = ((bf16[4,800,128]{2,1,0:T(8,128)(2,1)}), bf16[4,800,128]{2,1,0:T(8,128)(2,1)S(1)}, u32[]{:S(2)}, u32[]{:S(2)}) async-start(bf16[4,800,128]{2,1,0:T(8,128)(2,1)} %shard_map.137), calls=%async_computation | async-start | bytes 1638400 | tf_op jit(solution)/shard_map/all_to_all | solution.py:414
  8.5 0.0 copy-done.2
  8.5 1.4 collective-permute-start.2
  9.9 0.0 collective-permute-start.1
  9.9 7.9 %collective-permute-done.2.g2_in = bf16[512,256]{1,0:T(8,128)(2,1)S(1)} collective-permute-done((bf16[512,256]{1,0:T(8,128)(2,1)S(1)}, bf16[512,256]{1,0:T(8,128)(2,1)S(1)}, u32[]{:S(2)}, u32[]{:S(2)}) %collective-permute-start.2) | collective-permute-done | bytes 262176 | tf_op jit(solution)/shard_map/ppermute | solution.py:408
  17.8 0.0 copy-start.3
  17.8 0.0 collective-permute-start.3
  17.8 3.4 %all-to-all-done.row_in = bf16[4,800,128]{2,1,0:T(8,128)(2,1)S(1)} async-done(((bf16[4,800,128]{2,1,0:T(8,128)(2,1)}), bf16[4,800,128]{2,1,0:T(8,128)(2,1)S(1)}, u32[]{:S(2)}, u32[]{:S(2)}) %all-to-all-start) | async-done | bytes 819232 | tf_op jit(solution)/shard_map/all_to_all | solution.py:414
  21.2 0.0 copy-start.1
  21.2 0.0 copy-done.3
  21.2 1.4 collective-permute-start
  22.6 0.0 collective-permute-done.1.g1_in
  22.6 0.0 copy-start.4
  22.6 0.0 collective-permute-done.3.g3_in
  22.6 0.0 copy-start.5
  22.6 0.7 copy-done.4
  23.3 0.1 copy-done.5
  23.4 2.7 %shard_map.138 = bf16[4,256,128]{2,1,0:T(8,128)(2,1)} custom-call(s32[1]{0:T(128)} %bitcast.1.place_ref, bf16[512,256]{1,0:T(8,128)(2,1)} %g0_in.3, bf16[512,256]{1,0:T(8,128)(2,1)} %copy-done.4, bf16[512,256]{1,0:T(8,128)(2,1)} %copy-done.3, bf16[512,256]{1,0:T(8,128)(2,1)} %copy-done.5, bf16[256,1024]{1,0:T(8,128)(2,1)} %weight_in.1), custom_call_target="tpu_custom_call" | custom-call | tf_op jit(solution)/shard_map/pallas_call | solution.py:140
  26.1 3.4 %all-to-all-start.1 = ((bf16[4,256,128]{2,1,0:T(8,128)(2,1)}), bf16[4,256,128]{2,1,0:T(8,128)(2,1)S(1)}, u32[]{:S(2)}, u32[]{:S(2)}) async-start(bf16[4,256,128]{2,1,0:T(8,128)(2,1)} %shard_map.138), calls=%async_computation.1 | async-start | bytes 524288 | tf_op jit(solution)/shard_map/all_to_all | solution.py:414
  29.5 0.0 copy-start.11
  29.5 0.7 copy-done.11
  30.2 0.0 copy-start.12
  30.2 0.1 dynamic_slice.6
  30.3 0.6 copy-done.12
  30.9 0.1 dynamic_slice.7
  31.0 0.6 pad_bitcast_fusion
  31.6 4.6 %all-to-all-done.1.ga_in = bf16[4,256,128]{2,1,0:T(8,128)(2,1)S(1)} async-done(((bf16[4,256,128]{2,1,0:T(8,128)(2,1)}), bf16[4,256,128]{2,1,0:T(8,128)(2,1)S(1)}, u32[]{:S(2)}, u32[]{:S(2)}) %all-to-all-start.1) | async-done | bytes 262176 | tf_op jit(solution)/shard_map/all_to_all | solution.py:414
  36.2 0.0 copy-start.7
  36.2 0.0 collective-permute-done.halo_in
  36.2 0.0 copy-start.9
  36.2 0.8 broadcast_in_dim.18
  37.0 0.0 copy-done.7
  37.0 0.1 copy-done.9
  37.1 9.2 %all-to-all-start.2 = ((bf16[16,4,16,128]{3,2,1,0:T(8,128)(2,1)}), bf16[16,4,16,128]{3,2,1,0:T(8,128)(2,1)S(1)}, u32[]{:S(2)}, u32[]{:S(2)}) async-start(bf16[16,4,16,128]{3,2,1,0:T(8,128)(2,1)} %broadcast_in_dim.18), calls=%async_computation.2 | async-start | bytes 524288 | tf_op jit(solution)/shard_map/all_to_all | solution.py:420
  46.4 0.0 copy-done.1
  46.4 0.6 fusion.flag_ref
  47.0 10.1 %all-to-all-done.2 = bf16[16,4,16,128]{3,2,1,0:T(8,128)(2,1)S(1)} async-done(((bf16[16,4,16,128]{3,2,1,0:T(8,128)(2,1)}), bf16[16,4,16,128]{3,2,1,0:T(8,128)(2,1)S(1)}, u32[]{:S(2)}, u32[]{:S(2)}) %all-to-all-start.2) | async-done | bytes 262176 | tf_op jit(solution)/shard_map/all_to_all | solution.py:420
  57.1 0.0 copy-start.8
  57.1 0.7 copy-done.8
  57.8 35.1 %shard_map.139 = (bf16[4,512,128]{2,1,0:T(8,128)(2,1)}, f32[4,512,128]{2,1,0:T(8,128)}, bf16[3,512,128]{2,1,0:T(8,128)(2,1)}, bf16[64,16,128]{2,1,0:T(8,128)(2,1)}) custom-call(s32[64]{0:T(128)} %owner_ref.1, s32[4,4]{1,0:T(4,128)} %fusion.flag_ref, bf16[4,800,128]{2,1,0:T(8,128)(2,1)} %copy-done.1, bf16[3,512,128]{2,1,0:T(8,128)(2,1)} %copy-done.9, ...), custom_call_target="tpu_custom_call" | custom-call | flops 40000000000 | bytes 8000000 | tf_op jit(solution)/shard_map/pallas_call | solution.py:278
  92.9 0.0 copy-start.10
  93.0 3.6 %all-to-all-start.3 = ((bf16[4,512,128]{2,1,0:T(8,128)(2,1)}), bf16[4,512,128]{2,1,0:T(8,128)(2,1)S(1)}, u32[]{:S(2)}, u32[]{:S(2)}) async-start(bf16[4,512,128]{2,1,0:T(8,128)(2,1)} %get-tuple-element.23), calls=%async_computation.3 | async-start | bytes 1048576 | tf_op jit(solution)/shard_map/all_to_all | solution.py:414
  96.6 0.0 copy-done.10
  96.6 0.2 collective-permute-start.4
  96.8 7.9 %all-to-all-done.3.att_in.near_in = bf16[4,512,128]{2,1,0:T(8,128)(2,1)S(1)} async-done(((bf16[4,512,128]{2,1,0:T(8,128)(2,1)}), bf16[4,512,128]{2,1,0:T(8,128)(2,1)S(1)}, u32[]{:S(2)}, u32[]{:S(2)}) %all-to-all-start.3) | async-done | bytes 524320 | tf_op jit(solution)/shard_map/all_to_all | solution.py:414
  104.6 0.0 copy-start
  104.6 0.0 collective-permute-done.4.far_in
  104.6 0.0 copy-start.6
  104.6 0.8 copy-done
  105.4 2.9 %shard_map.140 = bf16[64,48,128]{2,1,0:T(8,128)(2,1)} custom-call(s32[1]{0:T(128)} %bitcast.1.place_ref, bf16[4,512,128]{2,1,0:T(8,128)(2,1)} %copy-done, bf16[512,256]{1,0:T(8,128)(2,1)} %g0_in.3, bf16[512,256]{1,0:T(8,128)(2,1)} %copy-done.4, bf16[512,256]{1,0:T(8,128)(2,1)} %copy-done.3, bf16[512,256]{1,0:T(8,128)(2,1)} %copy-done.5, ...), custom_call_target="tpu_custom_call" | custom-call | tf_op jit(solution)/shard_map/pallas_call | solution.py:326
  108.4 0.0 copy-done.6
  108.4 22.9 %all_to_all.30.parts_in = bf16[16,4,48,128]{3,2,1,0:T(8,128)(2,1)} all-to-all(bf16[16,4,48,128]{3,2,1,0:T(8,128)(2,1)} %bitcast.9), channel_id=1, replica_groups={{0,16,32,48,64,80,96,112,128,144,160,176,192,208,224,240},{4,20,36,52,6..., dimensions={0} | all-to-all | bytes 1572864 | tf_op jit(solution)/shard_map/all_to_all | solution.py:420
  131.3 2.6 %shard_map.141 = bf16[4,560,128]{2,1,0:T(8,128)(2,1)} custom-call(f32[4,512,128]{2,1,0:T(8,128)} %get-tuple-element.22.own_in, bf16[3,512,128]{2,1,0:T(8,128)(2,1)} %copy-done.6, bf16[16,4,48,128]{3,2,1,0:T(8,128)(2,1)} %all_to_all.30.parts_in), custom_call_target="tpu_custom_call" | custom-call | tf_op jit(solution)/shard_map/pallas_call | solution.py:354
  133.9 12.6 %all_to_all.31.in_in = bf16[4,560,128]{2,1,0:T(8,128)(2,1)} all-to-all(bf16[4,560,128]{2,1,0:T(8,128)(2,1)} %shard_map.141), channel_id=1, replica_groups={{0,4,8,12},{16,20,24,28},{32,36,40,44},{48,52,56,60},{64,68,72,76},{80,..., dimensions={0} | all-to-all | bytes 1146880 | tf_op jit(solution)/shard_map/all_to_all | solution.py:414
  146.5 2.2 %shard_map.142 = (bf16[512,256]{1,0:T(8,128)(2,1)}, bf16[512,256]{1,0:T(8,128)(2,1)}, bf16[512,256]{1,0:T(8,128)(2,1)}, bf16[32,256]{1,0:T(8,128)(2,1)}, bf16[16,256]{1,0:T(8,128)(2,1)}) custom-call(bf16[4,560,128]{2,1,0:T(8,128)(2,1)} %all_to_all.31.in_in, bf16[4,512,128]{2,1,0:T(8,128)(2,1)} %copy-done), custom_call_target="tpu_custom_call" | custom-call | tf_op jit(solution)/shard_map/pallas_call | solution.py:389
  (4 shorter events, 0.0 us)
Async XLA Ops:
  4.1 4.5 %copy-start.2 = (bf16[512,256]{1,0:T(8,128)(2,1)S(1)}, bf16[512,256]{1,0:T(8,128)(2,1)}, u32[]{:S(2)}) copy-start(bf16[512,256]{1,0:T(8,128)(2,1)} %g0_in.3) | copy-start | bytes 786436
  4.1 17.1 %all-to-all-start = ((bf16[4,800,128]{2,1,0:T(8,128)(2,1)}), bf16[4,800,128]{2,1,0:T(8,128)(2,1)S(1)}, u32[]{:S(2)}, u32[]{:S(2)}) async-start(bf16[4,800,128]{2,1,0:T(8,128)(2,1)} %shard_map.137), calls=%async_computation | async-start | bytes 1638400 | tf_op jit(solution)/shard_map/all_to_all | solution.py:414
  8.5 9.3 %collective-permute-start.2 = (bf16[512,256]{1,0:T(8,128)(2,1)S(1)}, bf16[512,256]{1,0:T(8,128)(2,1)S(1)}, u32[]{:S(2)}, u32[]{:S(2)}) collective-permute-start(bf16[512,256]{1,0:T(8,128)(2,1)S(1)} %copy-done.2), channel_id=1, source_target_pairs={{0,2},{1,3},{2,0},{3,1},{4,6},{5,7},{6,4},{7,5},{8,10},{9,11},{10,... | collective-permute-start | bytes 786440 | tf_op jit(solution)/shard_map/ppermute | solution.py:408
  9.9 12.7 %collective-permute-start.1 = (bf16[512,256]{1,0:T(8,128)(2,1)S(1)}, bf16[512,256]{1,0:T(8,128)(2,1)S(1)}, u32[]{:S(2)}, u32[]{:S(2)}) collective-permute-start(bf16[512,256]{1,0:T(8,128)(2,1)S(1)} %copy-done.2), channel_id=1, source_target_pairs={{0,1},{1,0},{2,3},{3,2},{4,5},{5,4},{6,7},{7,6},{8,9},{9,8},{10,11... | collective-permute-start | bytes 786440 | tf_op jit(solution)/shard_map/ppermute | solution.py:408
  17.8 3.4 %copy-start.3 = (bf16[512,256]{1,0:T(8,128)(2,1)}, bf16[512,256]{1,0:T(8,128)(2,1)S(1)}, u32[]{:S(2)}) copy-start(bf16[512,256]{1,0:T(8,128)(2,1)S(1)} %collective-permute-done.2.g2_in) | copy-start | bytes 786436
  17.8 4.8 %collective-permute-start.3 = (bf16[512,256]{1,0:T(8,128)(2,1)S(1)}, bf16[512,256]{1,0:T(8,128)(2,1)S(1)}, u32[]{:S(2)}, u32[]{:S(2)}) collective-permute-start(bf16[512,256]{1,0:T(8,128)(2,1)S(1)} %collective-permute-done.2.g2_in), channel_id=1, source_target_pairs={{0,1},{1,0},{2,3},{3,2},{4,5},{5,4},{6,7},{7,6},{8,9},{9,8},{10,11... | collective-permute-start | bytes 786440 | tf_op jit(solution)/shard_map/ppermute | solution.py:408
  21.2 25.2 %copy-start.1 = (bf16[4,800,128]{2,1,0:T(8,128)(2,1)}, bf16[4,800,128]{2,1,0:T(8,128)(2,1)S(1)}, u32[]{:S(2)}) copy-start(bf16[4,800,128]{2,1,0:T(8,128)(2,1)S(1)} %all-to-all-done.row_in) | copy-start | bytes 2457604
  21.2 14.9 %collective-permute-start = (bf16[3,512,128]{2,1,0:T(8,128)(2,1)S(1)}, bf16[3,512,128]{2,1,0:T(8,128)(2,1)S(1)}, u32[]{:S(2)}, u32[]{:S(2)}) collective-permute-start(bf16[3,512,128]{2,1,0:T(8,128)(2,1)S(1)} %slice.14), channel_id=1, source_target_pairs={{0,16},{4,20},{8,24},{12,28},{16,32},{20,36},{24,40},{28,44},{32,4... | collective-permute-start | bytes 1179656 | tf_op jit(solution)/shard_map/ppermute | solution.py:404
  22.6 0.7 copy-start.4
  22.6 0.8 copy-start.5
  26.1 10.1 %all-to-all-start.1 = ((bf16[4,256,128]{2,1,0:T(8,128)(2,1)}), bf16[4,256,128]{2,1,0:T(8,128)(2,1)S(1)}, u32[]{:S(2)}, u32[]{:S(2)}) async-start(bf16[4,256,128]{2,1,0:T(8,128)(2,1)} %shard_map.138), calls=%async_computation.1 | async-start | bytes 524288 | tf_op jit(solution)/shard_map/all_to_all | solution.py:414
  29.5 0.7 copy-start.11
  30.2 0.7 copy-start.12
  36.2 0.8 copy-start.7
  36.2 1.0 copy-start.9
  37.1 20.0 %all-to-all-start.2 = ((bf16[16,4,16,128]{3,2,1,0:T(8,128)(2,1)}), bf16[16,4,16,128]{3,2,1,0:T(8,128)(2,1)S(1)}, u32[]{:S(2)}, u32[]{:S(2)}) async-start(bf16[16,4,16,128]{3,2,1,0:T(8,128)(2,1)} %broadcast_in_dim.18), calls=%async_computation.2 | async-start | bytes 524288 | tf_op jit(solution)/shard_map/all_to_all | solution.py:420
  57.1 0.7 copy-start.8
  92.9 3.6 %copy-start.10 = (bf16[3,512,128]{2,1,0:T(8,128)(2,1)S(1)}, bf16[3,512,128]{2,1,0:T(8,128)(2,1)}, u32[]{:S(2)}) copy-start(bf16[3,512,128]{2,1,0:T(8,128)(2,1)} %get-tuple-element.24) | copy-start | bytes 1179652
  93.0 11.7 %all-to-all-start.3 = ((bf16[4,512,128]{2,1,0:T(8,128)(2,1)}), bf16[4,512,128]{2,1,0:T(8,128)(2,1)S(1)}, u32[]{:S(2)}, u32[]{:S(2)}) async-start(bf16[4,512,128]{2,1,0:T(8,128)(2,1)} %get-tuple-element.23), calls=%async_computation.3 | async-start | bytes 1048576 | tf_op jit(solution)/shard_map/all_to_all | solution.py:414
  96.6 8.0 %collective-permute-start.4 = (bf16[3,512,128]{2,1,0:T(8,128)(2,1)S(1)}, bf16[3,512,128]{2,1,0:T(8,128)(2,1)S(1)}, u32[]{:S(2)}, u32[]{:S(2)}) collective-permute-start(bf16[3,512,128]{2,1,0:T(8,128)(2,1)S(1)} %copy-done.10), channel_id=1, source_target_pairs={{0,240},{4,244},{8,248},{12,252},{16,0},{20,4},{24,8},{28,12},{32,... | collective-permute-start | bytes 1179656 | tf_op jit(solution)/shard_map/ppermute | solution.py:404
  104.6 0.8 copy-start
  104.6 3.7 %copy-start.6 = (bf16[3,512,128]{2,1,0:T(8,128)(2,1)}, bf16[3,512,128]{2,1,0:T(8,128)(2,1)S(1)}, u32[]{:S(2)}) copy-start(bf16[3,512,128]{2,1,0:T(8,128)(2,1)S(1)} %collective-permute-done.4.far_in) | copy-start | bytes 1179652

commit v3 on v2

--- a/solution.py
+++ b/solution.py
@@ -71,6 +71,10 @@
 
 
 def any_specs(count):
+    return [pl.BlockSpec(memory_space=pl.ANY)] * count
+
+
+def hbm_specs(count):
     return [pl.BlockSpec(memory_space=pltpu.HBM)] * count
 
 
@@ -110,7 +114,7 @@
     rows = tokens + tokens // 2 + pos.shape[0]
     return pl.pallas_call(
         pack_kernel,
-        in_specs=smem_specs(1) + any_specs(4),
+        in_specs=smem_specs(1) + hbm_specs(4),
         out_shape=pltpu.HBM((ROW, rows, LANES), BF),
         scratch_shapes=[pltpu.VMEM(a.shape, BF) for a in (q, k, v, pos)]
         + [pltpu.SemaphoreType.DMA((4,))],
@@ -119,7 +123,7 @@
 
 
 def mix_kernel(
-    place_ref, g0_in, g1_in, g2_in, g3_in, weight_in, out_ref, g0, g1, g2, g3, weight_ref, sems
+    g0_in, g1_in, g2_in, g3_in, weight_in, out_ref, g0, g1, g2, g3, weight_ref, sems
 ):
     brought(
         [(g0_in, g0), (g1_in, g1), (g2_in, g2), (g3_in, g3), (weight_in, weight_ref)], sems
@@ -127,7 +131,7 @@
     features = g0.shape[1]
     mixed = None
     for b, grad in enumerate((g0, g1, g2, g3)):
-        at = pl.multiple_of((place_ref[0] ^ b) * features, features)
+        at = pl.multiple_of((lax.axis_index("head") ^ b) * features, features)
         part = nt(grad[...], weight_ref[:, pl.ds(at, features)])
         mixed = part if mixed is None else mixed + part
     mixed = mixed.astype(BF)
@@ -135,16 +139,16 @@
         out_ref[h] = halves(mixed, h).astype(BF)
 
 
-def mix_call(place, grads, out_weight):
+def mix_call(grads, out_weight):
     tokens = grads[0].shape[0]
     return pl.pallas_call(
         mix_kernel,
-        in_specs=smem_specs(1) + any_specs(5),
+        in_specs=any_specs(5),
         out_shape=pltpu.HBM((ROW, tokens // 2, LANES), BF),
         scratch_shapes=[pltpu.VMEM(a.shape, BF) for a in (*grads, out_weight)]
         + [pltpu.SemaphoreType.DMA((5,))],
-        compiler_params=pltpu.CompilerParams(vmem_limit_bytes=60 << 20),
-    )(place, *grads, out_weight)
+        compiler_params=pltpu.CompilerParams(vmem_limit_bytes=16 << 20),
+    )(*grads, out_weight)
 
 
 def key_pairs(row_in, halo_in, keys, query, tokens):
@@ -157,9 +161,10 @@
 
 
 def core_kernel(
-    owner_ref, flag_ref, row_in, halo_in, slots_in, ga_in, cb_ref, pb_ref,
+    owner_ref, row_in, halo_in, s0_in, s1_in, s2_in, s3_in, ga_in, cb_in, pb_in,
     near_ref, own_ref, far_ref, dpos_ref,
-    keys, queries, slots_ref, ga_ref, table, flipped, grads, dist, sems,
+    keys, queries, slots_ref, ga_ref, table, flipped, grads, dist,
+    score_ref, rel_ref, low_ref, ds_ref, spread_ref, dot_ref, flag_ref, cb_ref, pb_ref, sems,
 ):
     tokens = halo_in.shape[1]
     half = tokens // 2
@@ -171,13 +176,22 @@
     @pl.when(block == 0)
     def _():
         pairs = key_pairs(row_in, halo_in, keys, queries, tokens)
-        brought(pairs + [(slots_in, slots_ref), (ga_in, ga_ref)], sems)
+        pairs += [(part, slots_ref.at[i]) for i, part in enumerate((s0_in, s1_in, s2_in, s3_in))]
+        at = tokens + half + slots_ref.shape[3]
+        pairs += [(ga_in, ga_ref), (row_in.at[:, at : at + 16], flag_ref)]
+        brought(pairs, sems)
+        turn = (ROW - (lax.axis_index("ctx") & 3)) * HD % cb_in.shape[1]
+        for bias_in, bias_ref in ((cb_in, cb_ref), (pb_in, pb_ref)):
+            bias = jnp.broadcast_to(bias_in[...], (8, bias_in.shape[1]))
+            bias_ref[...] = pltpu.roll(bias, turn, 1)[0:1, :LANES]
         grads[...] = jnp.zeros_like(grads)
         dist[...] = jnp.zeros_like(dist)
         table[0:tokens, :] = jnp.zeros((tokens, LANES), BF)
-        count, rows = slots_ref.shape[:2]
+        count, rows = owner_ref.shape[0], slots_ref.shape[3]
         for d in range(count):
-            both = slots_ref[owner_ref[d]]
+            slot = owner_ref[d]
+            apart = (slot >> 2) ^ (lax.axis_index("ctx") >> 2)
+            both = slots_ref[apart & 3, apart >> 2, slot & 3]
             at = tokens + 2 * d * rows
             table[at : at + rows, :] = both
             table[at + rows : at + 2 * rows, :] = turned(both).astype(BF)
@@ -193,7 +207,16 @@
     starts = [pl.multiple_of((block + w) * tokens, tokens) for w in range(ROW)]
     kept = []
     dqs = []
-    for r in range(2):
+    chunk = 16
+    groups = [slice(c, c + chunk) for c in range(0, half, chunk)]
+    barred = []
+    for lag in range(ROW - 1, 0, -1):
+        there = (lax.axis_index("ctx") & ~3) + block >= lag
+        flag = flag_ref[block, 0:1, lag : lag + 1].astype(F32)
+        barred.append(jnp.where(there & (flag > 0.5), 0.0, NEG))
+    state = [{}, {}]
+
+    def first(r):
         query = queries[block].astype(F32)
         ga = ga_ref[block].astype(F32)
         query = turned(query) if r == 1 else query
@@ -201,51 +224,105 @@
         ga = jnp.where(low, 0.0, ga)
         cq = jnp.where(low, query + cb_ref[...], 0.0).astype(BF)
         pq = jnp.where(low, query + pb_ref[...], 0.0).astype(BF)
+        state[r].update(ga=ga, gal=ga.astype(BF), cq=cq, pq=pq)
+        base = half * (1 - r)
+        rel_ref[r] = nt(pq * scale, flipped[base : base + wide, :])
         cqs = cq * scale
-        pqs = pq * scale
-        base = half * (1 - r)
-        rel = nt(pqs, flipped[base : base + wide, :])
-        rel = pltpu.roll(rel, span + 1, 1, stride=1, stride_axis=0)
-        scores = []
         for w in range(ROW):
-            s = nt(cqs, keys[pl.ds(starts[w], tokens), :]) + rel[:, w * tokens : (w + 1) * tokens]
-            if w == ROW - 1:
-                row = lax.broadcasted_iota(jnp.int32, (half, tokens), 0) + r * half
-                col = lax.broadcasted_iota(jnp.int32, (half, tokens), 1)
-                s = jnp.where(col <= row, s, NEG)
-            else:
-                s = jnp.where(flag_ref[block, ROW - 1 - w] == 1, s, NEG)
-            scores.append(s)
-        top = functools.reduce(jnp.maximum, [jnp.max(s, axis=1, keepdims=True) for s in scores])
-        weights = [jnp.exp(s - top) for s in scores]
-        total = functools.reduce(jnp.add, [jnp.sum(e, axis=1, keepdims=True) for e in weights])
-        inv = 1.0 / total
-        probs = [e * inv for e in weights]
-        lows = [p.astype(BF) for p in probs]
+            score_ref[r, :, w * tokens : (w + 1) * tokens] = nt(
+                cqs, keys[pl.ds(starts[w], tokens), :]
+            )
+
+    def soften(r):
+        for g in groups:
+            moved = pltpu.roll(
+                rel_ref[r, g, :], (span + 1 + g.start) % wide, 1, stride=1, stride_axis=0
+            )
+            scores = []
+            for w in range(ROW):
+                cols = slice(w * tokens, (w + 1) * tokens)
+                s = score_ref[r, g, cols] + moved[:, cols]
+                if w == ROW - 1:
+                    row = lax.broadcasted_iota(jnp.int32, (chunk, tokens), 0) + r * half + g.start
+                    col = lax.broadcasted_iota(jnp.int32, (chunk, tokens), 1)
+                    s = jnp.where(col <= row, s, NEG)
+                else:
+                    s = s + barred[w]
+                scores.append(s)
+            top = functools.reduce(jnp.maximum, scores)
+            top = jnp.max(top, axis=1, keepdims=True)
+            weights = [jnp.exp(s - top) for s in scores]
+            total = functools.reduce(jnp.add, weights)
+            inv = 1.0 / jnp.sum(total, axis=1, keepdims=True)
+            for w in range(ROW):
+                cols = slice(w * tokens, (w + 1) * tokens)
+                p = weights[w] * inv
+                score_ref[r, g, cols] = p
+                low_ref[r, g, cols] = p.astype(BF)
+
+    def second(r):
         att = None
         for w in range(ROW):
-            part = nn(lows[w], keys[pl.ds(starts[w], tokens), :])
+            cols = slice(w * tokens, (w + 1) * tokens)
+            part = nn(low_ref[r, :, cols], keys[pl.ds(starts[w], tokens), :])
             att = part if att is None else att + part
         att = att.astype(BF).astype(F32)
-        kept.append(turned(att) if r == 0 else att)
-        dot = jnp.sum(ga * att, axis=1, keepdims=True)
-        ga = ga.astype(BF)
-        flips = [None] * (2 * ROW)
+        state[r]["att"] = turned(att) if r == 0 else att
+        dot = jnp.sum(state[r]["ga"] * att, axis=1, keepdims=True)
+        dot_ref[r] = jnp.broadcast_to(dot, (half, LANES))
+        for w in range(ROW):
+            cols = slice(w * tokens, (w + 1) * tokens)
+            rel_ref[r, :, cols] = nt(state[r]["gal"], keys[pl.ds(starts[w], tokens), :])
+
+    def steepen(r):
+        for g in groups:
+            dot = dot_ref[r, g, 0:1]
+            for w in range(ROW):
+                cols = slice(w * tokens, (w + 1) * tokens)
+                ds = 0.125 * score_ref[r, g, cols] * (rel_ref[r, g, cols] - dot)
+                ds_ref[r, g, cols] = ds.astype(BF)
+
+    def third(r):
         acc = None
         for w in range(ROW):
-            window = keys[pl.ds(starts[w], tokens), :]
-            ds = (0.125 * probs[w] * (nt(ga, window) - dot)).astype(BF)
-            grads[:, pl.ds(starts[w], tokens)] += tn(cq, ds) + tn(ga, lows[w])
-            part = nn(ds, window)
+            cols = slice(w * tokens, (w + 1) * tokens)
+            ds = ds_ref[r, :, cols]
+            for x in range(2):
+                at = (2 * ROW - 1 - (2 * w + x)) * half
+                rel_ref[r, :, at : at + half] = nn(ds[:, x * half : (x + 1) * half], anti)
+        rel_ref[r, :, span:] = jnp.zeros((half, wide - span), F32)
+        for w in range(ROW):
+            cols = slice(w * tokens, (w + 1) * tokens)
+            ds = ds_ref[r, :, cols]
+            grads[:, pl.ds(starts[w], tokens)] += tn(state[r]["cq"], ds) + tn(
+                state[r]["gal"], low_ref[r, :, cols]
+            )
+            part = nn(ds, keys[pl.ds(starts[w], tokens), :])
             acc = part if acc is None else acc + part
-            for x in range(2):
-                flips[2 * ROW - 1 - (2 * w + x)] = nn(ds[:, x * half : (x + 1) * half], anti)
-        spread = jnp.concatenate(flips + [jnp.zeros((half, half), F32)], axis=1)
-        spread = pltpu.roll(spread, 1, 1, stride=1, stride_axis=0).astype(BF)
+        state[r]["acc"] = acc
+
+    def slant(r):
+        for g in groups:
+            spread_ref[r, g, :] = pltpu.roll(
+                rel_ref[r, g, :], 1 + g.start, 1, stride=1, stride_axis=0
+            ).astype(BF)
+
+    def fourth(r):
         start = half * r
-        acc = acc + nn(spread, table[start : start + wide, :])
-        dist[:, start : start + wide] += tn(pq, spread)
-        dqs.append(turned(acc) if r == 1 else acc)
+        acc = state[r]["acc"] + nn(spread_ref[r], table[start : start + wide, :])
+        dist[:, start : start + wide] += tn(state[r]["pq"], spread_ref[r])
+        state[r]["acc"] = turned(acc) if r == 1 else acc
+
+    first(0)
+    for stage, other in (
+        (soften, first), (second, soften), (steepen, second), (third, steepen), (slant, third),
+        (fourth, slant),
+    ):
+        stage(0)
+        other(1)
+    fourth(1)
+    kept = [part["att"] for part in state]
+    dqs = [part["acc"] for part in state]
     near_ref[block, :half, :] = joined(kept[0], kept[1]).astype(BF)
     near_ref[block, half:, :] = joined(dqs[0], dqs[1]).astype(BF)
 
@@ -266,10 +343,11 @@
             ).astype(BF)
 
 
-def core_call(owner, flags, row, halo, slots, ga, cb, pb):
+def core_call(owner, row, halo, slots, ga, cb, pb):
     tokens = halo.shape[1]
     half = tokens // 2
-    slot_count, packed_rows = slots.shape[:2]
+    slot_count = owner.shape[0]
+    packed_rows = slots[0].shape[2]
     rel = slot_count * packed_rows * 2
     shapes = [
         ((ROW, tokens, LANES), BF), ((ROW, tokens, LANES), F32), ((ROW - 1, tokens, LANES), BF),
@@ -278,29 +356,38 @@
     return pl.pallas_call(
         core_kernel,
         grid=(ROW,),
-        in_specs=smem_specs(2) + any_specs(4) + vmem_specs(2),
+        in_specs=smem_specs(1) + any_specs(7) + vmem_specs(2),
         out_specs=[whole_spec(shape) for shape, _ in shapes],
         out_shape=[pltpu.HBM(shape, dtype) for shape, dtype in shapes],
         scratch_shapes=[
             pltpu.VMEM(((2 * ROW - 1) * tokens, LANES), BF),
             pltpu.VMEM((ROW, half, LANES), BF),
-            pltpu.VMEM(slots.shape, BF),
+            pltpu.VMEM((4,) + slots[0].shape, BF),
             pltpu.VMEM((ROW, half, LANES), BF),
             pltpu.VMEM((tokens + rel, LANES), BF),
             pltpu.VMEM((tokens + rel, LANES), BF),
             pltpu.VMEM((LANES, (2 * ROW - 1) * tokens), F32),
             pltpu.VMEM((LANES, tokens + rel), F32),
-            pltpu.SemaphoreType.DMA((3 * ROW + 1,)),
+            pltpu.VMEM((2, half, ROW * tokens), F32),
+            pltpu.VMEM((2, half, ROW * tokens + half), F32),
+            pltpu.VMEM((2, half, ROW * tokens), BF),
+            pltpu.VMEM((2, half, ROW * tokens), BF),
+            pltpu.VMEM((2, half, ROW * tokens + half), BF),
+            pltpu.VMEM((2, half, LANES), F32),
+            pltpu.VMEM((ROW, 16, LANES), BF),
+            pltpu.VMEM((1, LANES), F32),
+            pltpu.VMEM((1, LANES), F32),
+            pltpu.SemaphoreType.DMA((3 * ROW + 5,)),
         ],
         compiler_params=pltpu.CompilerParams(vmem_limit_bytes=60 << 20),
         cost_estimate=pl.CostEstimate(
             flops=40_000_000_000, bytes_accessed=8_000_000, transcendentals=0
         ),
-    )(owner, flags, row, halo, slots, ga, cb, pb)
+    )(owner, row, halo, *slots, ga, cb, pb)
 
 
 def weight_kernel(
-    place_ref, att_in, g0_in, g1_in, g2_in, g3_in, dpos_in, out_ref,
+    att_in, g0_in, g1_in, g2_in, g3_in, dpos_in, out_ref,
     att_ref, g0, g1, g2, g3, dpos_ref, sems,
 ):
     half = att_ref.shape[1]
@@ -315,23 +402,23 @@
         at = rows * (1 + pair)
         for b, grad in enumerate((g0, g1, g2, g3)):
             term = tn(att, grad[...]).T.astype(BF)
-            out_ref[pl.ds((place_ref[0] ^ b) * chunks, chunks), at : at + rows, :] = term.reshape(
+            out_ref[pl.ds((lax.axis_index("head") ^ b) * chunks, chunks), at : at + rows, :] = term.reshape(
                 chunks, rows, LANES
             )
 
 
-def weight_call(place, att, grads, dpos):
+def weight_call(att, grads, dpos):
     slot_count, rows = dpos.shape[:2]
     pairs = grads[0].shape[1] // LANES
     return pl.pallas_call(
         weight_kernel,
-        in_specs=smem_specs(1) + any_specs(6),
+        in_specs=any_specs(6),
         scratch_shapes=[pltpu.VMEM((ROW, grads[0].shape[0] // 2, LANES), BF)]
         + [pltpu.VMEM(a.shape, BF) for a in (*grads, dpos)]
         + [pltpu.SemaphoreType.DMA((6,))],
         out_shape=pltpu.HBM((slot_count, rows * (1 + pairs), LANES), BF),
-        compiler_params=pltpu.CompilerParams(vmem_limit_bytes=60 << 20),
-    )(place, att, *grads, dpos)
+        compiler_params=pltpu.CompilerParams(vmem_limit_bytes=16 << 20),
+    )(att, *grads, dpos)
 
 
 def meet_kernel(own_in, far_in, parts_in, out_ref, own_ref, far_ref, parts_ref, sems):
@@ -357,7 +444,7 @@
         out_shape=pltpu.HBM((ROW, rows, LANES), BF),
         scratch_shapes=[pltpu.VMEM(a.shape, a.dtype) for a in (own, far, parts)]
         + [pltpu.SemaphoreType.DMA((3,))],
-        compiler_params=pltpu.CompilerParams(vmem_limit_bytes=60 << 20),
+        compiler_params=pltpu.CompilerParams(vmem_limit_bytes=16 << 20),
     )(own, far, parts)
 
 
@@ -395,7 +482,7 @@
             pltpu.VMEM((ROW, tokens // 2, LANES), BF),
             pltpu.SemaphoreType.DMA((2,)),
         ],
-        compiler_params=pltpu.CompilerParams(vmem_limit_bytes=60 << 20),
+        compiler_params=pltpu.CompilerParams(vmem_limit_bytes=16 << 20),
     )(arrived, near)
 
 
@@ -420,43 +507,34 @@
     return lax.all_to_all(block, "ctx", 0, 0, axis_index_groups=groups)
 
 
+def masked(block, mask):
+    return lax.ppermute(block, "ctx", [(i, i ^ mask) for i in range(lax.axis_size("ctx"))])
+
+
 def body(
     query, key, value, pos_store, owner, block_mask, content_bias, pos_bias, out_weight, d_layer
 ):
     tokens, features = query.shape
-    window = block_mask.shape[1]
     slot_count = owner.shape[0]
     slot_rows = pos_store.shape[0]
     half = tokens // 2
-    block_index = lax.axis_index("ctx")
-    place = lax.axis_index("head").astype(jnp.int32)[None]
-    mine = block_index % ROW
-
-    def bias_of(bias):
-        part = lax.dynamic_slice_in_dim(bias, mine * HD, HD)
-        return jnp.pad(part, (0, LANES - HD))[None]
-
-    cb, pb = bias_of(content_bias), bias_of(pos_bias)
     across = swapped(d_layer, 2)
     row = in_row(pack_call(block_mask, query, key, value, pos_store))
     halo = shifted(row[1:, :tokens], ROW)
     at = tokens + half
     pos = row[:, at : at + slot_rows // 2]
+    far_pos = [pos] + [masked(pos, ROW * 4 * j) for j in range(1, 4)]
+    far_pos = jnp.stack(far_pos)
+    slots = [far_pos] + [masked(far_pos, ROW * j) for j in range(1, 4)]
     grads = [d_layer, swapped(d_layer, 1), across, swapped(across, 1)]
-    mixed = mix_call(place, grads, out_weight)
-    ga = in_row(mixed)
-    pos, halo, ga = lax.optimization_barrier((pos, halo, ga))
-    slots = in_column(jnp.broadcast_to(pos[None], (slot_count // ROW,) + pos.shape))
-    slots = slots.reshape(slot_count, slot_rows // 2, LANES)
-    flags = row[:, at + slot_rows // 2, :window].astype(jnp.int32)
-    blocks = block_index - mine + jnp.arange(ROW)
-    flags = flags * (blocks[:, None] >= jnp.arange(window)[None]).astype(jnp.int32)
-
-    near, own, far, dpos = core_call(owner, flags, row, halo, slots, ga, cb, pb)
+    ga = in_row(mix_call(grads, out_weight))
+    near, own, far, dpos = core_call(
+        owner, row, halo, slots, ga, content_bias[None], pos_bias[None]
+    )
     back = shifted(far, -ROW)
     near = in_row(near)
     near, back = lax.optimization_barrier((near, back))
-    sums = weight_call(place, near, grads, dpos)
+    sums = weight_call(near, grads, dpos)
     parts = in_column(sums.reshape((slot_count // ROW, ROW) + sums.shape[1:]))
     arrived = in_row(meet_call(own, back, parts))
     grad_query, grad_key, grad_value, grad_pos, grad_weight = final_call(

time: 150 us -> 136 us (0.907)
  Pallas kernels: 49 us -> 38.7 us
  starting transfers between devices: 23.6 us -> 29.7 us
  waiting for transfers between devices: 33.8 us -> 27.9 us
  local copies, waits for them, and re-layouts: 5.31 us -> 0.88 us
  blocking collectives: 35.5 us -> 37.4 us
    ppermute x0 -> x6, starting transfers between devices: none -> 13.7 us  [masked(): lax.ppermute(block, 'ctx', [(i, i ^ mask) for i in range(lax.axis_size('c...]
    ppermute x0 -> x6, waiting for transfers between devices: none -> 10.1 us  [masked(): lax.ppermute(block, 'ctx', [(i, i ^ mask) for i in range(lax.axis_size('c...]
    all_to_all x1 -> x0, waiting for transfers between devices: 10.1 us -> none  [in_column(): return lax.all_to_all(block, 'ctx', 0, 0, axis_index_groups=groups)]
    all_to_all x1 -> x0, starting transfers between devices: 9.22 us -> none  [in_column(): return lax.all_to_all(block, 'ctx', 0, 0, axis_index_groups=groups)]
    pallas_call x4, Pallas kernels: 44.2 us -> 36.1 us  [the longest x1 29.5 us: core_call(): pl.pallas_call(core_kernel, grid=(ROW,), in_specs=smem_specs(1) + any_spe...]
    all_to_all x3, waiting for transfers between devices: 15.8 us -> 8.41 us  [in_row(): return lax.all_to_all(block, 'ctx', 0, 0, axis_index_groups=groups)]
    unnamed x26 -> x24, local copies, waits for them, and re-layouts: 3.72 us -> 0.85 us
    all_to_all x1, blocking collectives: 22.9 us -> 25 us  [in_column(): return lax.all_to_all(block, 'ctx', 0, 0, axis_index_groups=groups)]
  transfers between devices with their start and end apart: 9 -> 14, of which waited for: 5 -> 10; matrix products, arithmetic and copies ran while one was open for 1% -> 0% of each run, Pallas kernels for 2% -> 1%
where the time goes in v3:
time: 136 us
  Pallas kernels  38.7 us (28%)
  blocking collectives  37.4 us (28%)
  starting transfers between devices  29.7 us (22%)
  waiting for transfers between devices  27.9 us (21%)
    pallas_call x1, Pallas kernels, core_call(): pl.pallas_call(core_kernel, grid=(ROW,), in_specs=smem_specs(1) + any_spe...  29.5 us
    all_to_all x1, blocking collectives, in_column(): return lax.all_to_all(block, 'ctx', 0, 0, axis_index_groups=groups)  25 us
    ppermute x6, starting transfers between devices, masked(): lax.ppermute(block, 'ctx', [(i, i ^ mask) for i in range(lax.axis_size('c...  13.7 us
    all_to_all x3, starting transfers between devices, in_row(): return lax.all_to_all(block, 'ctx', 0, 0, axis_index_groups=groups)  13.3 us
    all_to_all x1, blocking collectives, in_row(): return lax.all_to_all(block, 'ctx', 0, 0, axis_index_groups=groups)  12.4 us
    ppermute x6, waiting for transfers between devices, masked(): lax.ppermute(block, 'ctx', [(i, i ^ mask) for i in range(lax.axis_size('c...  10.1 us
    ppermute x3, waiting for transfers between devices, swapped(): lax.ppermute(block, 'head', [(i, i ^ bit) for i in range(lax.axis_size('h...  9.42 us
    all_to_all x3, waiting for transfers between devices, in_row(): return lax.all_to_all(block, 'ctx', 0, 0, axis_index_groups=groups)  8.41 us
  transfers between devices with their start and end apart: 14, of which 10 were waited for; matrix products, arithmetic and copies ran while one was open for 0% of the time, Pallas kernels for 1%

profile of v3, /device:TPU:16, one launch (start us, length us, event | category | flops | bytes accessed | tf_op | source)
XLA Modules:
  0.0 135.6 jit_solution(3533210755589291154)
XLA Ops:
  0.6 3.4 %shard_map.137 = bf16[4,800,128]{2,1,0:T(8,128)(2,1)} custom-call(s32[1,4]{1,0:T(1,128)} %mask_ref.1, bf16[512,256]{1,0:T(8,128)(2,1)} %q_in.1, bf16[512,256]{1,0:T(8,128)(2,1)} %k_in.1, bf16[512,256]{1,0:T(8,128)(2,1)} %v_in.1, bf16[32,256]{1,0:T(8,128)(2,1)} %pos_in.1), custom_call_target="tpu_custom_call" | custom-call | tf_op jit(solution)/shard_map/pallas_call | solution.py:115
  4.1 0.0 copy-start
  4.1 0.0 copy-start.2
  4.1 4.4 %all-to-all-start = ((bf16[4,800,128]{2,1,0:T(8,128)(2,1)}), bf16[4,800,128]{2,1,0:T(8,128)(2,1)S(1)}, u32[]{:S(2)}, u32[]{:S(2)}) async-start(bf16[4,800,128]{2,1,0:T(8,128)(2,1)} %shard_map.137), calls=%async_computation | async-start | bytes 1638400 | tf_op jit(solution)/shard_map/all_to_all | solution.py:501
  8.5 0.0 copy-done
  8.5 1.4 %collective-permute-start.8 = (bf16[512,256]{1,0:T(8,128)(2,1)S(1)}, bf16[512,256]{1,0:T(8,128)(2,1)S(1)}, u32[]{:S(2)}, u32[]{:S(2)}) collective-permute-start(bf16[512,256]{1,0:T(8,128)(2,1)S(1)} %copy-done), channel_id=1, source_target_pairs={{0,2},{1,3},{2,0},{3,1},{4,6},{5,7},{6,4},{7,5},{8,10},{9,11},{10,... | collective-permute-start | bytes 786440 | tf_op jit(solution)/shard_map/ppermute | solution.py:495
  9.9 0.0 collective-permute-start.7
  9.9 7.9 %collective-permute-done.8.g2_in = bf16[512,256]{1,0:T(8,128)(2,1)S(1)} collective-permute-done((bf16[512,256]{1,0:T(8,128)(2,1)S(1)}, bf16[512,256]{1,0:T(8,128)(2,1)S(1)}, u32[]{:S(2)}, u32[]{:S(2)}) %collective-permute-start.8) | collective-permute-done | bytes 262176 | tf_op jit(solution)/shard_map/ppermute | solution.py:495
  17.8 0.0 collective-permute-start.9
  17.8 0.0 collective-permute-done.7.g1_in
  17.8 1.5 %collective-permute-done.9.g3_in = bf16[512,256]{1,0:T(8,128)(2,1)S(1)} collective-permute-done((bf16[512,256]{1,0:T(8,128)(2,1)S(1)}, bf16[512,256]{1,0:T(8,128)(2,1)S(1)}, u32[]{:S(2)}, u32[]{:S(2)}) %collective-permute-start.9) | collective-permute-done | bytes 262176 | tf_op jit(solution)/shard_map/ppermute | solution.py:495
  19.4 0.0 copy-done.2
  19.4 1.5 %shard_map.138 = bf16[4,256,128]{2,1,0:T(8,128)(2,1)} custom-call(bf16[512,256]{1,0:T(8,128)(2,1)S(1)} %copy-done, bf16[512,256]{1,0:T(8,128)(2,1)S(1)} %collective-permute-done.7.g1_in, bf16[512,256]{1,0:T(8,128)(2,1)S(1)} %collective-permute-done.8.g2_in, bf16[512,256]{1,0:T(8,128)(2,1)S(1)} %collective-permute-done.9.g3_in, bf16[256,1024]{1,0:T(8,128)(2,1)S(1)} %copy-done.2), custom_call_target="tpu_custom_call" | custom-call | tf_op jit(solution)/shard_map/pallas_call | solution.py:144
  20.8 0.3 all-to-all-done.row_in
  21.2 0.0 copy-start.4
  21.2 4.2 %all-to-all-start.1 = ((bf16[4,256,128]{2,1,0:T(8,128)(2,1)}), bf16[4,256,128]{2,1,0:T(8,128)(2,1)S(1)}, u32[]{:S(2)}, u32[]{:S(2)}) async-start(bf16[4,256,128]{2,1,0:T(8,128)(2,1)} %shard_map.138), calls=%async_computation.1 | async-start | bytes 524288 | tf_op jit(solution)/shard_map/all_to_all | solution.py:501
  25.4 1.4 %collective-permute-start = (bf16[3,512,128]{2,1,0:T(8,128)(2,1)S(1)}, bf16[3,512,128]{2,1,0:T(8,128)(2,1)S(1)}, u32[]{:S(2)}, u32[]{:S(2)}) collective-permute-start(bf16[3,512,128]{2,1,0:T(8,128)(2,1)S(1)} %slice.8), channel_id=1, source_target_pairs={{0,16},{4,20},{8,24},{12,28},{16,32},{20,36},{24,40},{28,44},{32,4... | collective-permute-start | bytes 1179656 | tf_op jit(solution)/shard_map/ppermute | solution.py:491
  26.8 7.2 %collective-permute-start.2 = (bf16[4,16,128]{2,1,0:T(8,128)(2,1)S(1)}, bf16[4,16,128]{2,1,0:T(8,128)(2,1)S(1)}, u32[]{:S(2)}, u32[]{:S(2)}) collective-permute-start(bf16[4,16,128]{2,1,0:T(8,128)(2,1)S(1)} %get-tuple-element.28), channel_id=1, source_target_pairs={{0,128},{4,132},{8,136},{12,140},{16,144},{20,148},{24,152},{28,15... | collective-permute-start | bytes 49160 | tf_op jit(solution)/shard_map/ppermute | solution.py:511
  34.0 1.5 %collective-permute-start.1 = (bf16[4,16,128]{2,1,0:T(8,128)(2,1)S(1)}, bf16[4,16,128]{2,1,0:T(8,128)(2,1)S(1)}, u32[]{:S(2)}, u32[]{:S(2)}) collective-permute-start(bf16[4,16,128]{2,1,0:T(8,128)(2,1)S(1)} %get-tuple-element.28), channel_id=1, source_target_pairs={{0,64},{4,68},{8,72},{12,76},{16,80},{20,84},{24,88},{28,92},{32,9... | collective-permute-start | bytes 49160 | tf_op jit(solution)/shard_map/ppermute | solution.py:511
  35.5 0.0 collective-permute-start.3
  35.5 0.2 collective-permute-done.2
  35.7 2.9 %collective-permute-done.1 = bf16[4,16,128]{2,1,0:T(8,128)(2,1)S(1)} collective-permute-done((bf16[4,16,128]{2,1,0:T(8,128)(2,1)S(1)}, bf16[4,16,128]{2,1,0:T(8,128)(2,1)S(1)}, u32[]{:S(2)}, u32[]{:S(2)}) %collective-permute-start.1) | collective-permute-done | bytes 16416 | tf_op jit(solution)/shard_map/ppermute | solution.py:511
  38.6 2.7 %collective-permute-done.3 = bf16[4,16,128]{2,1,0:T(8,128)(2,1)S(1)} collective-permute-done((bf16[4,16,128]{2,1,0:T(8,128)(2,1)S(1)}, bf16[4,16,128]{2,1,0:T(8,128)(2,1)S(1)}, u32[]{:S(2)}, u32[]{:S(2)}) %collective-permute-start.3) | collective-permute-done | bytes 16416 | tf_op jit(solution)/shard_map/ppermute | solution.py:511
  41.3 0.0 copy-start.6
  41.3 1.9 %collective-permute-start.6 = (bf16[4,4,16,128]{3,2,1,0:T(8,128)(2,1)S(1)}, bf16[4,4,16,128]{3,2,1,0:T(8,128)(2,1)S(1)}, u32[]{:S(2)}, u32[]{:S(2)}) collective-permute-start(bf16[4,4,16,128]{3,2,1,0:T(8,128)(2,1)S(1)} %pad_maximum_fusion.s0_in), channel_id=1, source_target_pairs={{0,48},{4,52},{8,56},{12,60},{16,32},{20,36},{24,40},{28,44},{32,1... | collective-permute-start | bytes 196616 | tf_op jit(solution)/shard_map/ppermute | solution.py:511
  43.3 3.0 %collective-permute-start.5 = (bf16[4,4,16,128]{3,2,1,0:T(8,128)(2,1)S(1)}, bf16[4,4,16,128]{3,2,1,0:T(8,128)(2,1)S(1)}, u32[]{:S(2)}, u32[]{:S(2)}) collective-permute-start(bf16[4,4,16,128]{3,2,1,0:T(8,128)(2,1)S(1)} %pad_maximum_fusion.s0_in), channel_id=1, source_target_pairs={{0,32},{4,36},{8,40},{12,44},{16,48},{20,52},{24,56},{28,60},{32,0... | collective-permute-start | bytes 196616 | tf_op jit(solution)/shard_map/ppermute | solution.py:511
  46.3 0.0 collective-permute-start.4
  46.3 0.5 collective-permute-done.6.s3_in
  46.8 0.0 copy-start.9
  46.8 2.4 %collective-permute-done.5.s2_in = bf16[4,4,16,128]{3,2,1,0:T(8,128)(2,1)S(1)} collective-permute-done((bf16[4,4,16,128]{3,2,1,0:T(8,128)(2,1)S(1)}, bf16[4,4,16,128]{3,2,1,0:T(8,128)(2,1)S(1)}, u32[]{:S(2)}, u32[]{:S(2)}) %collective-permute-start.5) | collective-permute-done | bytes 65568 | tf_op jit(solution)/shard_map/ppermute | solution.py:511
  49.3 0.0 copy-start.10
  49.3 1.3 collective-permute-done.4.s1_in
  50.6 0.0 copy-start.11
  50.6 0.0 all-to-all-done.1.ga_in
  50.6 0.0 copy-start.5
  50.6 0.0 collective-permute-done.halo_in
  50.6 0.0 copy-start.7
  50.6 0.0 copy-done.4
  50.6 0.0 copy-done.6
  50.6 0.0 copy-done.9
  50.6 0.0 copy-done.10
  50.6 0.6 copy-done.11
  51.2 0.1 copy-done.5
  51.3 0.1 copy-done.7
  51.4 29.5 %shard_map.139 = (bf16[4,512,128]{2,1,0:T(8,128)(2,1)}, f32[4,512,128]{2,1,0:T(8,128)}, bf16[3,512,128]{2,1,0:T(8,128)(2,1)}, bf16[64,16,128]{2,1,0:T(8,128)(2,1)}) custom-call(s32[64]{0:T(128)} %owner_ref.1, bf16[4,800,128]{2,1,0:T(8,128)(2,1)} %copy-done.4, bf16[3,512,128]{2,1,0:T(8,128)(2,1)} %copy-done.7, bf16[4,4,16,128]{3,2,1,0:T(8,128)(2,1)} %copy-done.6, ...), custom_call_target="tpu_custom_call" | custom-call | flops 40000000000 | bytes 8000000 | tf_op jit(solution)/shard_map/pallas_call | solution.py:356
  80.9 0.0 copy-start.8
  81.0 0.0 copy-start.3
  81.0 4.7 %all-to-all-start.2 = ((bf16[4,512,128]{2,1,0:T(8,128)(2,1)}), bf16[4,512,128]{2,1,0:T(8,128)(2,1)S(1)}, u32[]{:S(2)}, u32[]{:S(2)}) async-start(bf16[4,512,128]{2,1,0:T(8,128)(2,1)} %get-tuple-element.17), calls=%async_computation.2 | async-start | bytes 1048576 | tf_op jit(solution)/shard_map/all_to_all | solution.py:501
  85.6 0.0 copy-done.8
  85.6 0.0 collective-permute-start.10
  85.6 8.1 %all-to-all-done.2.att_in.near_in = bf16[4,512,128]{2,1,0:T(8,128)(2,1)S(1)} async-done(((bf16[4,512,128]{2,1,0:T(8,128)(2,1)}), bf16[4,512,128]{2,1,0:T(8,128)(2,1)S(1)}, u32[]{:S(2)}, u32[]{:S(2)}) %all-to-all-start.2) | async-done | bytes 524320 | tf_op jit(solution)/shard_map/all_to_all | solution.py:501
  93.7 0.0 collective-permute-done.10.far_in
  93.7 0.0 copy-done.3
  93.7 1.7 %shard_map.140 = bf16[64,48,128]{2,1,0:T(8,128)(2,1)} custom-call(bf16[4,512,128]{2,1,0:T(8,128)(2,1)S(1)} %all-to-all-done.2.att_in.near_in, bf16[512,256]{1,0:T(8,128)(2,1)S(1)} %copy-done, bf16[512,256]{1,0:T(8,128)(2,1)S(1)} %collective-permute-done.7.g1_in, bf16[512,256]{1,0:T(8,128)(2,1)S(1)} %collective-permute-done.8.g2_in, ...), custom_call_target="tpu_custom_call" | custom-call | tf_op jit(solution)/shard_map/pallas_call | solution.py:413
  95.4 0.0 copy-start.1
  95.4 25.0 %all_to_all.25.parts_in = bf16[16,4,48,128]{3,2,1,0:T(8,128)(2,1)S(1)} all-to-all(bf16[16,4,48,128]{3,2,1,0:T(8,128)(2,1)} %bitcast.9), channel_id=1, replica_groups={{0,16,32,48,64,80,96,112,128,144,160,176,192,208,224,240},{4,20,36,52,6..., dimensions={0} | all-to-all | bytes 1572864 | tf_op jit(solution)/shard_map/all_to_all | solution.py:507
  120.5 0.0 copy-done.1
  120.5 1.3 shard_map.141
  121.8 12.4 %all_to_all.26.in_in = bf16[4,560,128]{2,1,0:T(8,128)(2,1)S(1)} all-to-all(bf16[4,560,128]{2,1,0:T(8,128)(2,1)} %shard_map.141), channel_id=1, replica_groups={{0,4,8,12},{16,20,24,28},{32,36,40,44},{48,52,56,60},{64,68,72,76},{80,..., dimensions={0} | all-to-all | bytes 1146880 | tf_op jit(solution)/shard_map/all_to_all | solution.py:501
  134.1 1.2 shard_map.142
  (3 shorter events, 0.0 us)
Async XLA Ops:
  4.1 4.5 %copy-start = (bf16[512,256]{1,0:T(8,128)(2,1)S(1)}, bf16[512,256]{1,0:T(8,128)(2,1)}, u32[]{:S(2)}) copy-start(bf16[512,256]{1,0:T(8,128)(2,1)} %g0_in.3) | copy-start | bytes 786436
  4.1 15.3 %copy-start.2 = (bf16[256,1024]{1,0:T(8,128)(2,1)S(1)}, bf16[256,1024]{1,0:T(8,128)(2,1)}, u32[]{:S(2)}) copy-start(bf16[256,1024]{1,0:T(8,128)(2,1)} %weight_in.1) | copy-start | bytes 1572868
  4.1 17.1 %all-to-all-start = ((bf16[4,800,128]{2,1,0:T(8,128)(2,1)}), bf16[4,800,128]{2,1,0:T(8,128)(2,1)S(1)}, u32[]{:S(2)}, u32[]{:S(2)}) async-start(bf16[4,800,128]{2,1,0:T(8,128)(2,1)} %shard_map.137), calls=%async_computation | async-start | bytes 1638400 | tf_op jit(solution)/shard_map/all_to_all | solution.py:501
  8.5 9.3 %collective-permute-start.8 = (bf16[512,256]{1,0:T(8,128)(2,1)S(1)}, bf16[512,256]{1,0:T(8,128)(2,1)S(1)}, u32[]{:S(2)}, u32[]{:S(2)}) collective-permute-start(bf16[512,256]{1,0:T(8,128)(2,1)S(1)} %copy-done), channel_id=1, source_target_pairs={{0,2},{1,3},{2,0},{3,1},{4,6},{5,7},{6,4},{7,5},{8,10},{9,11},{10,... | collective-permute-start | bytes 786440 | tf_op jit(solution)/shard_map/ppermute | solution.py:495
  9.9 7.9 %collective-permute-start.7 = (bf16[512,256]{1,0:T(8,128)(2,1)S(1)}, bf16[512,256]{1,0:T(8,128)(2,1)S(1)}, u32[]{:S(2)}, u32[]{:S(2)}) collective-permute-start(bf16[512,256]{1,0:T(8,128)(2,1)S(1)} %copy-done), channel_id=1, source_target_pairs={{0,1},{1,0},{2,3},{3,2},{4,5},{5,4},{6,7},{7,6},{8,9},{9,8},{10,11... | collective-permute-start | bytes 786440 | tf_op jit(solution)/shard_map/ppermute | solution.py:495
  17.8 1.5 %collective-permute-start.9 = (bf16[512,256]{1,0:T(8,128)(2,1)S(1)}, bf16[512,256]{1,0:T(8,128)(2,1)S(1)}, u32[]{:S(2)}, u32[]{:S(2)}) collective-permute-start(bf16[512,256]{1,0:T(8,128)(2,1)S(1)} %collective-permute-done.8.g2_in), channel_id=1, source_target_pairs={{0,1},{1,0},{2,3},{3,2},{4,5},{5,4},{6,7},{7,6},{8,9},{9,8},{10,11... | collective-permute-start | bytes 786440 | tf_op jit(solution)/shard_map/ppermute | solution.py:495
  21.2 29.4 %copy-start.4 = (bf16[4,800,128]{2,1,0:T(8,128)(2,1)}, bf16[4,800,128]{2,1,0:T(8,128)(2,1)S(1)}, u32[]{:S(2)}) copy-start(bf16[4,800,128]{2,1,0:T(8,128)(2,1)S(1)} %all-to-all-done.row_in) | copy-start | bytes 2457604
  21.2 29.4 %all-to-all-start.1 = ((bf16[4,256,128]{2,1,0:T(8,128)(2,1)}), bf16[4,256,128]{2,1,0:T(8,128)(2,1)S(1)}, u32[]{:S(2)}, u32[]{:S(2)}) async-start(bf16[4,256,128]{2,1,0:T(8,128)(2,1)} %shard_map.138), calls=%async_computation.1 | async-start | bytes 524288 | tf_op jit(solution)/shard_map/all_to_all | solution.py:501
  25.4 25.2 %collective-permute-start = (bf16[3,512,128]{2,1,0:T(8,128)(2,1)S(1)}, bf16[3,512,128]{2,1,0:T(8,128)(2,1)S(1)}, u32[]{:S(2)}, u32[]{:S(2)}) collective-permute-start(bf16[3,512,128]{2,1,0:T(8,128)(2,1)S(1)} %slice.8), channel_id=1, source_target_pairs={{0,16},{4,20},{8,24},{12,28},{16,32},{20,36},{24,40},{28,44},{32,4... | collective-permute-start | bytes 1179656 | tf_op jit(solution)/shard_map/ppermute | solution.py:491
  26.8 8.9 %collective-permute-start.2 = (bf16[4,16,128]{2,1,0:T(8,128)(2,1)S(1)}, bf16[4,16,128]{2,1,0:T(8,128)(2,1)S(1)}, u32[]{:S(2)}, u32[]{:S(2)}) collective-permute-start(bf16[4,16,128]{2,1,0:T(8,128)(2,1)S(1)} %get-tuple-element.28), channel_id=1, source_target_pairs={{0,128},{4,132},{8,136},{12,140},{16,144},{20,148},{24,152},{28,15... | collective-permute-start | bytes 49160 | tf_op jit(solution)/shard_map/ppermute | solution.py:511
  34.0 4.6 %collective-permute-start.1 = (bf16[4,16,128]{2,1,0:T(8,128)(2,1)S(1)}, bf16[4,16,128]{2,1,0:T(8,128)(2,1)S(1)}, u32[]{:S(2)}, u32[]{:S(2)}) collective-permute-start(bf16[4,16,128]{2,1,0:T(8,128)(2,1)S(1)} %get-tuple-element.28), channel_id=1, source_target_pairs={{0,64},{4,68},{8,72},{12,76},{16,80},{20,84},{24,88},{28,92},{32,9... | collective-permute-start | bytes 49160 | tf_op jit(solution)/shard_map/ppermute | solution.py:511
  35.5 5.8 %collective-permute-start.3 = (bf16[4,16,128]{2,1,0:T(8,128)(2,1)S(1)}, bf16[4,16,128]{2,1,0:T(8,128)(2,1)S(1)}, u32[]{:S(2)}, u32[]{:S(2)}) collective-permute-start(bf16[4,16,128]{2,1,0:T(8,128)(2,1)S(1)} %get-tuple-element.28), channel_id=1, source_target_pairs={{0,192},{4,196},{8,200},{12,204},{16,208},{20,212},{24,216},{28,22... | collective-permute-start | bytes 49160 | tf_op jit(solution)/shard_map/ppermute | solution.py:511
  41.3 9.3 %copy-start.6 = (bf16[4,4,16,128]{3,2,1,0:T(8,128)(2,1)}, bf16[4,4,16,128]{3,2,1,0:T(8,128)(2,1)S(1)}, u32[]{:S(2)}) copy-start(bf16[4,4,16,128]{3,2,1,0:T(8,128)(2,1)S(1)} %pad_maximum_fusion.s0_in) | copy-start | bytes 196612
  41.3 5.5 %collective-permute-start.6 = (bf16[4,4,16,128]{3,2,1,0:T(8,128)(2,1)S(1)}, bf16[4,4,16,128]{3,2,1,0:T(8,128)(2,1)S(1)}, u32[]{:S(2)}, u32[]{:S(2)}) collective-permute-start(bf16[4,4,16,128]{3,2,1,0:T(8,128)(2,1)S(1)} %pad_maximum_fusion.s0_in), channel_id=1, source_target_pairs={{0,48},{4,52},{8,56},{12,60},{16,32},{20,36},{24,40},{28,44},{32,1... | collective-permute-start | bytes 196616 | tf_op jit(solution)/shard_map/ppermute | solution.py:511
  43.3 6.0 %collective-permute-start.5 = (bf16[4,4,16,128]{3,2,1,0:T(8,128)(2,1)S(1)}, bf16[4,4,16,128]{3,2,1,0:T(8,128)(2,1)S(1)}, u32[]{:S(2)}, u32[]{:S(2)}) collective-permute-start(bf16[4,4,16,128]{3,2,1,0:T(8,128)(2,1)S(1)} %pad_maximum_fusion.s0_in), channel_id=1, source_target_pairs={{0,32},{4,36},{8,40},{12,44},{16,48},{20,52},{24,56},{28,60},{32,0... | collective-permute-start | bytes 196616 | tf_op jit(solution)/shard_map/ppermute | solution.py:511
  46.3 4.3 %collective-permute-start.4 = (bf16[4,4,16,128]{3,2,1,0:T(8,128)(2,1)S(1)}, bf16[4,4,16,128]{3,2,1,0:T(8,128)(2,1)S(1)}, u32[]{:S(2)}, u32[]{:S(2)}) collective-permute-start(bf16[4,4,16,128]{3,2,1,0:T(8,128)(2,1)S(1)} %pad_maximum_fusion.s0_in), channel_id=1, source_target_pairs={{0,16},{4,20},{8,24},{12,28},{16,0},{20,4},{24,8},{28,12},{32,48},... | collective-permute-start | bytes 196616 | tf_op jit(solution)/shard_map/ppermute | solution.py:511
  46.8 3.8 %copy-start.9 = (bf16[4,4,16,128]{3,2,1,0:T(8,128)(2,1)}, bf16[4,4,16,128]{3,2,1,0:T(8,128)(2,1)S(1)}, u32[]{:S(2)}) copy-start(bf16[4,4,16,128]{3,2,1,0:T(8,128)(2,1)S(1)} %collective-permute-done.6.s3_in) | copy-start | bytes 196612
  49.3 1.4 %copy-start.10 = (bf16[4,4,16,128]{3,2,1,0:T(8,128)(2,1)}, bf16[4,4,16,128]{3,2,1,0:T(8,128)(2,1)S(1)}, u32[]{:S(2)}) copy-start(bf16[4,4,16,128]{3,2,1,0:T(8,128)(2,1)S(1)} %collective-permute-done.5.s2_in) | copy-start | bytes 196612
  50.6 0.6 copy-start.11
  50.6 0.7 copy-start.5
  50.6 0.9 copy-start.7
  80.9 4.7 %copy-start.8 = (bf16[3,512,128]{2,1,0:T(8,128)(2,1)S(1)}, bf16[3,512,128]{2,1,0:T(8,128)(2,1)}, u32[]{:S(2)}) copy-start(bf16[3,512,128]{2,1,0:T(8,128)(2,1)} %get-tuple-element.18) | copy-start | bytes 1179652
  81.0 12.8 %copy-start.3 = (bf16[64,16,128]{2,1,0:T(8,128)(2,1)S(1)}, bf16[64,16,128]{2,1,0:T(8,128)(2,1)}, u32[]{:S(2)}) copy-start(bf16[64,16,128]{2,1,0:T(8,128)(2,1)} %get-tuple-element.21.dpos_in) | copy-start | bytes 786436
  81.0 12.7 %all-to-all-start.2 = ((bf16[4,512,128]{2,1,0:T(8,128)(2,1)}), bf16[4,512,128]{2,1,0:T(8,128)(2,1)S(1)}, u32[]{:S(2)}, u32[]{:S(2)}) async-start(bf16[4,512,128]{2,1,0:T(8,128)(2,1)} %get-tuple-element.17), calls=%async_computation.2 | async-start | bytes 1048576 | tf_op jit(solution)/shard_map/all_to_all | solution.py:501
  85.6 8.1 %collective-permute-start.10 = (bf16[3,512,128]{2,1,0:T(8,128)(2,1)S(1)}, bf16[3,512,128]{2,1,0:T(8,128)(2,1)S(1)}, u32[]{:S(2)}, u32[]{:S(2)}) collective-permute-start(bf16[3,512,128]{2,1,0:T(8,128)(2,1)S(1)} %copy-done.8), channel_id=1, source_target_pairs={{0,240},{4,244},{8,248},{12,252},{16,0},{20,4},{24,8},{28,12},{32,... | collective-permute-start | bytes 1179656 | tf_op jit(solution)/shard_map/ppermute | solution.py:491
  95.4 25.0 %copy-start.1 = (f32[4,512,128]{2,1,0:T(8,128)S(1)}, f32[4,512,128]{2,1,0:T(8,128)}, u32[]{:S(2)}) copy-start(f32[4,512,128]{2,1,0:T(8,128)} %get-tuple-element.16.own_in) | copy-start | bytes 3145732

commit v4 on v3

--- a/solution.py
+++ b/solution.py
@@ -93,42 +93,42 @@
         copy.wait()
 
 
-def pack_kernel(mask_ref, q_in, k_in, v_in, pos_in, out_ref, q_ref, k_ref, v_ref, pos_ref, sems):
-    brought([(q_in, q_ref), (k_in, k_ref), (v_in, v_ref), (pos_in, pos_ref)], sems)
+def pack_kernel(mask_ref, q_in, k_in, v_in, out_ref, q_ref, k_ref, v_ref, sems):
+    brought([(q_in, q_ref), (k_in, k_ref), (v_in, v_ref)], sems)
     tokens = q_ref.shape[0]
     half = tokens // 2
-    rows = pos_ref.shape[0] // 2
-    flags = jnp.zeros((rows, LANES), F32)
+    flags = jnp.zeros((16, LANES), F32)
     for lag in range(mask_ref.shape[1]):
         flags = jnp.where(lanes() == lag, mask_ref[0, lag].astype(F32), flags)
     for h in range(ROW):
         out_ref[h, :tokens, :] = joined(of_head(k_ref, h), turned(of_head(v_ref, h))).astype(BF)
         out_ref[h, tokens : tokens + half, :] = halves(q_ref, h).astype(BF)
-        at = tokens + half
-        out_ref[h, at : at + rows, :] = halves(pos_ref, h).astype(BF)
-        out_ref[h, at + rows :, :] = flags.astype(BF)
-
-
-def pack_call(mask, q, k, v, pos):
+        out_ref[h, tokens + half :, :] = flags.astype(BF)
+
+
+def pack_call(mask, q, k, v):
     tokens = q.shape[0]
-    rows = tokens + tokens // 2 + pos.shape[0]
+    rows = tokens + tokens // 2 + 16
     return pl.pallas_call(
         pack_kernel,
-        in_specs=smem_specs(1) + hbm_specs(4),
+        in_specs=smem_specs(1) + hbm_specs(3),
         out_shape=pltpu.HBM((ROW, rows, LANES), BF),
-        scratch_shapes=[pltpu.VMEM(a.shape, BF) for a in (q, k, v, pos)]
-        + [pltpu.SemaphoreType.DMA((4,))],
+        scratch_shapes=[pltpu.VMEM(a.shape, BF) for a in (q, k, v)]
+        + [pltpu.SemaphoreType.DMA((3,))],
         compiler_params=pltpu.CompilerParams(vmem_limit_bytes=60 << 20),
-    )(mask, q, k, v, pos)
+    )(mask, q, k, v)
 
 
 def mix_kernel(
-    g0_in, g1_in, g2_in, g3_in, weight_in, out_ref, g0, g1, g2, g3, weight_ref, sems
+    g0_in, g1_in, g2_in, g3_in, weight_in, s0_in, s1_in, s2_in, s3_in, out_ref,
+    g0, g1, g2, g3, weight_ref, pos_ref, sems,
 ):
-    brought(
-        [(g0_in, g0), (g1_in, g1), (g2_in, g2), (g3_in, g3), (weight_in, weight_ref)], sems
-    )
-    features = g0.shape[1]
+    rows = s0_in.shape[0]
+    pairs = [(g0_in, g0), (g1_in, g1), (g2_in, g2), (g3_in, g3), (weight_in, weight_ref)]
+    for i, part in enumerate((s0_in, s1_in, s2_in, s3_in)):
+        pairs.append((part, pos_ref.at[i * rows : (i + 1) * rows]))
+    brought(pairs, sems)
+    tokens, features = g0.shape
     mixed = None
     for b, grad in enumerate((g0, g1, g2, g3)):
         at = pl.multiple_of((lax.axis_index("head") ^ b) * features, features)
@@ -136,19 +136,21 @@
         mixed = part if mixed is None else mixed + part
     mixed = mixed.astype(BF)
     for h in range(ROW):
-        out_ref[h] = halves(mixed, h).astype(BF)
-
-
-def mix_call(grads, out_weight):
-    tokens = grads[0].shape[0]
+        out_ref[h, : tokens // 2, :] = halves(mixed, h).astype(BF)
+        out_ref[h, tokens // 2 :, :] = halves(pos_ref, h).astype(BF)
+
+
+def mix_call(grads, out_weight, slots):
+    tokens, features = grads[0].shape
+    rows = 4 * slots[0].shape[0]
     return pl.pallas_call(
         mix_kernel,
-        in_specs=any_specs(5),
-        out_shape=pltpu.HBM((ROW, tokens // 2, LANES), BF),
+        in_specs=any_specs(9),
+        out_shape=pltpu.HBM((ROW, (tokens + rows) // 2, LANES), BF),
         scratch_shapes=[pltpu.VMEM(a.shape, BF) for a in (*grads, out_weight)]
-        + [pltpu.SemaphoreType.DMA((5,))],
+        + [pltpu.VMEM((rows, features), BF), pltpu.SemaphoreType.DMA((9,))],
         compiler_params=pltpu.CompilerParams(vmem_limit_bytes=16 << 20),
-    )(*grads, out_weight)
+    )(*grads, out_weight, *slots)
 
 
 def key_pairs(row_in, halo_in, keys, query, tokens):
@@ -161,9 +163,9 @@
 
 
 def core_kernel(
-    owner_ref, row_in, halo_in, s0_in, s1_in, s2_in, s3_in, ga_in, cb_in, pb_in,
-    near_ref, own_ref, far_ref, dpos_ref,
-    keys, queries, slots_ref, ga_ref, table, flipped, grads, dist,
+    owner_ref, row_in, halo_in, ga_in, cb_in, pb_in,
+    near_ref, own_ref, far_ref,
+    keys, queries, pos_ref, ga_ref, dist_out, table, flipped, grads, dist,
     score_ref, rel_ref, low_ref, ds_ref, spread_ref, dot_ref, flag_ref, cb_ref, pb_ref, sems,
 ):
     tokens = halo_in.shape[1]
@@ -176,10 +178,14 @@
     @pl.when(block == 0)
     def _():
         pairs = key_pairs(row_in, halo_in, keys, queries, tokens)
-        pairs += [(part, slots_ref.at[i]) for i, part in enumerate((s0_in, s1_in, s2_in, s3_in))]
-        at = tokens + half + slots_ref.shape[3]
-        pairs += [(ga_in, ga_ref), (row_in.at[:, at : at + 16], flag_ref)]
+        count = owner_ref.shape[0]
+        packed = pos_ref.shape[2]
+        rows = 2 * packed * ROW // count
+        pairs += [(ga_in.at[:, 0:half], ga_ref), (ga_in.at[:, half : half + packed], pos_ref.at[0])]
+        pairs.append((row_in.at[:, tokens + half : tokens + half + 16], flag_ref))
         brought(pairs, sems)
+        for b in range(ROW):
+            pos_ref[1, b] = turned(pos_ref[0, b]).astype(BF)
         turn = (ROW - (lax.axis_index("ctx") & 3)) * HD % cb_in.shape[1]
         for bias_in, bias_ref in ((cb_in, cb_ref), (pb_in, pb_ref)):
             bias = jnp.broadcast_to(bias_in[...], (8, bias_in.shape[1]))
@@ -187,14 +193,13 @@
         grads[...] = jnp.zeros_like(grads)
         dist[...] = jnp.zeros_like(dist)
         table[0:tokens, :] = jnp.zeros((tokens, LANES), BF)
-        count, rows = owner_ref.shape[0], slots_ref.shape[3]
         for d in range(count):
             slot = owner_ref[d]
             apart = (slot >> 2) ^ (lax.axis_index("ctx") >> 2)
-            both = slots_ref[apart & 3, apart >> 2, slot & 3]
-            at = tokens + 2 * d * rows
-            table[at : at + rows, :] = both
-            table[at + rows : at + 2 * rows, :] = turned(both).astype(BF)
+            place = (apart & 3) * 4 + (apart >> 2)
+            at = pl.multiple_of((place & 7) * rows, rows)
+            both = pos_ref[place >> 3, slot & 3, pl.ds(at, rows), :]
+            table[tokens + d * rows : tokens + (d + 1) * rows, :] = both
         parts = (tokens + span) // half
         for i in range(parts):
             flipped[(parts - 1 - i) * half : (parts - i) * half, :] = nn(
@@ -324,7 +329,7 @@
     kept = [part["att"] for part in state]
     dqs = [part["acc"] for part in state]
     near_ref[block, :half, :] = joined(kept[0], kept[1]).astype(BF)
-    near_ref[block, half:, :] = joined(dqs[0], dqs[1]).astype(BF)
+    near_ref[block, half:tokens, :] = joined(dqs[0], dqs[1]).astype(BF)
 
     @pl.when(block == ROW - 1)
     def _():
@@ -333,37 +338,41 @@
         for b in range(ROW):
             at = (ROW - 1 + b) * tokens
             own_ref[b] = grads[:, at : at + tokens].T
-        count, rows = dpos_ref.shape[:2]
-        table_grad = dist[:, tokens:].T
-        other = pltpu.roll(table_grad, HD, 1)
+        count = owner_ref.shape[0]
+        packed = pos_ref.shape[2]
+        rows = 2 * packed * ROW // count
+        dist_out[...] = dist[:, tokens:].T
         for d in range(count):
-            at = 2 * d * rows
-            dpos_ref[owner_ref[d]] = joined(
-                table_grad[at : at + rows], other[at + rows : at + 2 * rows]
-            ).astype(BF)
-
-
-def core_call(owner, row, halo, slots, ga, cb, pb):
+            slot = owner_ref[d]
+            part = dist_out[d * rows : (d + 1) * rows, :].astype(BF)
+            place = slot >> 2
+            at = pl.multiple_of((place & 7) * rows, rows)
+            pos_ref[place >> 3, slot & 3, pl.ds(at, rows), :] = part
+        for b in range(ROW):
+            near_ref[b, tokens:, :] = joined(pos_ref[0, b], turned(pos_ref[1, b])).astype(BF)
+
+
+def core_call(owner, row, halo, ga, cb, pb):
     tokens = halo.shape[1]
     half = tokens // 2
-    slot_count = owner.shape[0]
-    packed_rows = slots[0].shape[2]
-    rel = slot_count * packed_rows * 2
+    packed = ga.shape[1] - half
+    rel = ROW * packed * 2
     shapes = [
-        ((ROW, tokens, LANES), BF), ((ROW, tokens, LANES), F32), ((ROW - 1, tokens, LANES), BF),
-        ((slot_count, packed_rows, LANES), BF),
+        ((ROW, tokens + packed, LANES), BF), ((ROW, tokens, LANES), F32),
+        ((ROW - 1, tokens, LANES), BF),
     ]
     return pl.pallas_call(
         core_kernel,
         grid=(ROW,),
-        in_specs=smem_specs(1) + any_specs(7) + vmem_specs(2),
+        in_specs=smem_specs(1) + any_specs(3) + vmem_specs(2),
         out_specs=[whole_spec(shape) for shape, _ in shapes],
         out_shape=[pltpu.HBM(shape, dtype) for shape, dtype in shapes],
         scratch_shapes=[
             pltpu.VMEM(((2 * ROW - 1) * tokens, LANES), BF),
             pltpu.VMEM((ROW, half, LANES), BF),
-            pltpu.VMEM((4,) + slots[0].shape, BF),
+            pltpu.VMEM((2, ROW, packed, LANES), BF),
             pltpu.VMEM((ROW, half, LANES), BF),
+            pltpu.VMEM((rel, LANES), F32),
             pltpu.VMEM((tokens + rel, LANES), BF),
             pltpu.VMEM((tokens + rel, LANES), BF),
             pltpu.VMEM((LANES, (2 * ROW - 1) * tokens), F32),
@@ -377,113 +386,138 @@
             pltpu.VMEM((ROW, 16, LANES), BF),
             pltpu.VMEM((1, LANES), F32),
             pltpu.VMEM((1, LANES), F32),
-            pltpu.SemaphoreType.DMA((3 * ROW + 5,)),
+            pltpu.SemaphoreType.DMA((3 * ROW + 2,)),
         ],
         compiler_params=pltpu.CompilerParams(vmem_limit_bytes=60 << 20),
         cost_estimate=pl.CostEstimate(
             flops=40_000_000_000, bytes_accessed=8_000_000, transcendentals=0
         ),
-    )(owner, row, halo, *slots, ga, cb, pb)
+    )(owner, row, halo, ga, cb, pb)
 
 
 def weight_kernel(
-    att_in, g0_in, g1_in, g2_in, g3_in, dpos_in, out_ref,
-    att_ref, g0, g1, g2, g3, dpos_ref, sems,
+    att_in, g0_in, g1_in, g2_in, g3_in, own_in, far_in, out_ref,
+    att_ref, g0, g1, g2, g3, own_ref, far_ref, sems,
 ):
     half = att_ref.shape[1]
-    sources = [att_in.at[:, 0:half], g0_in, g1_in, g2_in, g3_in, dpos_in]
-    brought(zip(sources, [att_ref, g0, g1, g2, g3, dpos_ref]), sems)
-    rows = dpos_ref.shape[1]
-    features = g0.shape[1]
-    chunks = features // rows
-    out_ref[:, :rows, :] = dpos_ref[...]
-    for pair in range(features // LANES):
-        att = whole_of(att_ref[2 * pair], att_ref[2 * pair + 1]).astype(BF)
-        at = rows * (1 + pair)
-        for b, grad in enumerate((g0, g1, g2, g3)):
-            term = tn(att, grad[...]).T.astype(BF)
-            out_ref[pl.ds((lax.axis_index("head") ^ b) * chunks, chunks), at : at + rows, :] = term.reshape(
-                chunks, rows, LANES
-            )
-
-
-def weight_call(att, grads, dpos):
-    slot_count, rows = dpos.shape[:2]
-    pairs = grads[0].shape[1] // LANES
-    return pl.pallas_call(
-        weight_kernel,
-        in_specs=any_specs(6),
-        scratch_shapes=[pltpu.VMEM((ROW, grads[0].shape[0] // 2, LANES), BF)]
-        + [pltpu.VMEM(a.shape, BF) for a in (*grads, dpos)]
-        + [pltpu.SemaphoreType.DMA((6,))],
-        out_shape=pltpu.HBM((slot_count, rows * (1 + pairs), LANES), BF),
-        compiler_params=pltpu.CompilerParams(vmem_limit_bytes=16 << 20),
-    )(att, *grads, dpos)
-
-
-def meet_kernel(own_in, far_in, parts_in, out_ref, own_ref, far_ref, parts_ref, sems):
-    sources = [own_in, far_in, parts_in]
-    brought(zip(sources, [own_ref, far_ref, parts_ref]), sems)
-    tokens = own_ref.shape[1]
+    tokens, features = g0.shape
+    sources = [att_in.at[:, 0:half], g0_in, g1_in, g2_in, g3_in, own_in, far_in]
+    brought(zip(sources, [att_ref, g0, g1, g2, g3, own_ref, far_ref]), sems)
     for b in range(ROW):
         grad = own_ref[b]
         if b > 0:
             grad = grad + far_ref[b - 1].astype(F32)
         out_ref[b, :tokens, :] = grad.astype(BF)
-        total = parts_ref[0, b].astype(F32)
-        for z in range(1, parts_ref.shape[0]):
-            total = total + parts_ref[z, b].astype(F32)
-        out_ref[b, tokens:, :] = total.astype(BF)
-
-
-def meet_call(own, far, parts):
-    rows = own.shape[1] + parts.shape[2]
-    return pl.pallas_call(
-        meet_kernel,
-        in_specs=any_specs(3),
+    rows = 16
+    chunks = features // rows
+    column = 4 * features // (ROW * rows)
+    for pair in range(features // LANES):
+        att = whole_of(att_ref[2 * pair], att_ref[2 * pair + 1]).astype(BF)
+        for b, grad in enumerate((g0, g1, g2, g3)):
+            term = tn(att, grad[...]).T.astype(BF)
+            first = (lax.axis_index("head") ^ b) * (chunks // ROW)
+            for c in range(chunks):
+                at = tokens + (pair * column + first + c // ROW) * rows
+                out_ref[c % ROW, pl.ds(pl.multiple_of(at, rows), rows), :] = term[
+                    c * rows : (c + 1) * rows
+                ]
+
+
+def weight_call(near, grads, own, far):
+    tokens, features = grads[0].shape
+    rows = tokens + 4 * features // ROW * (features // LANES)
+    return pl.pallas_call(
+        weight_kernel,
+        in_specs=any_specs(7),
         out_shape=pltpu.HBM((ROW, rows, LANES), BF),
-        scratch_shapes=[pltpu.VMEM(a.shape, a.dtype) for a in (own, far, parts)]
-        + [pltpu.SemaphoreType.DMA((3,))],
+        scratch_shapes=[pltpu.VMEM((ROW, tokens // 2, LANES), BF)]
+        + [pltpu.VMEM(a.shape, a.dtype) for a in (*grads, own, far)]
+        + [pltpu.SemaphoreType.DMA((7,))],
         compiler_params=pltpu.CompilerParams(vmem_limit_bytes=16 << 20),
-    )(own, far, parts)
-
-
-def final_kernel(
-    in_in, near_in, dq_ref, dk_ref, dv_ref, dpos_ref, dw_ref, in_ref, near_ref, sems
-):
+    )(near, *grads, own, far)
+
+
+def sum_kernel(row_in, near_in, out_ref, row_ref, near_ref, sems):
+    column, rows, features = out_ref.shape
+    weight_rows = 16
+    pos_rows = rows - weight_rows
+    tokens = row_in.shape[1] - column * weight_rows * (features // LANES)
+    near_rows = near_in.shape[1]
+    sources = [row_in.at[:, tokens:], near_in.at[:, tokens:near_rows]]
+    brought(zip(sources, [row_ref, near_ref]), sems)
+    for pair in range(features // LANES):
+        cols = slice(pair * LANES, (pair + 1) * LANES)
+        pos = whole_of(near_ref[2 * pair], near_ref[2 * pair + 1]).astype(BF)
+        part = slice(pair * column * weight_rows, (pair + 1) * column * weight_rows)
+        total = row_ref[0, part, :].astype(F32)
+        for x in range(1, ROW):
+            total = total + row_ref[x, part, :].astype(F32)
+        total = total.astype(BF)
+        for z in range(column):
+            out_ref[z, :pos_rows, cols] = pos[z * pos_rows : (z + 1) * pos_rows]
+            out_ref[z, pos_rows:, cols] = total[z * weight_rows : (z + 1) * weight_rows]
+
+
+def sum_call(row, near, column, pos_rows, features, tokens):
+    return pl.pallas_call(
+        sum_kernel,
+        in_specs=any_specs(2),
+        out_shape=pltpu.HBM((column, pos_rows + 16, features), BF),
+        scratch_shapes=[
+            pltpu.VMEM((ROW, row.shape[1] - tokens, LANES), BF),
+            pltpu.VMEM((ROW, near.shape[1] - tokens, LANES), BF),
+            pltpu.SemaphoreType.DMA((2,)),
+        ],
+        compiler_params=pltpu.CompilerParams(vmem_limit_bytes=16 << 20),
+    )(row, near)
+
+
+def grads_kernel(row_in, near_in, dq_ref, dk_ref, dv_ref, row_ref, near_ref, sems):
     tokens = dq_ref.shape[0]
-    brought([(in_in, in_ref), (near_in.at[:, tokens // 2 :], near_ref)], sems)
-    rows = dpos_ref.shape[0] // 2
-    at = tokens
+    sources = [row_in.at[:, 0:tokens], near_in.at[:, tokens // 2 : tokens]]
+    brought(zip(sources, [row_ref, near_ref]), sems)
     for pair in range(ROW // 2):
         cols = slice(pair * LANES, (pair + 1) * LANES)
         dq_ref[:, cols] = whole_of(near_ref[2 * pair], near_ref[2 * pair + 1]).astype(BF)
-        first, second = in_ref.at[2 * pair], in_ref.at[2 * pair + 1]
-        a, b = first[:at, :], second[:at, :]
+        a, b = row_ref[2 * pair], row_ref[2 * pair + 1]
         dk_ref[:, cols] = joined(a, turned(b)).astype(BF)
         dv_ref[:, cols] = joined(turned(a), b).astype(BF)
-        dpos_ref[:, cols] = whole_of(first[at : at + rows, :], second[at : at + rows, :]).astype(BF)
-        lo = at + rows * (1 + pair)
-        total = in_ref[0, lo : lo + rows, :].astype(F32)
-        for x in range(1, ROW):
-            total = total + in_ref[x, lo : lo + rows, :].astype(F32)
-        dw_ref[:, cols] = total.astype(BF)
-
-
-def final_call(arrived, near, features, slot_rows, out_rows):
-    tokens = near.shape[1]
-    shapes = [(tokens, features)] * 3 + [(slot_rows, features), (out_rows, features)]
-    return pl.pallas_call(
-        final_kernel,
+
+
+def grads_call(row, near, tokens, features):
+    return pl.pallas_call(
+        grads_kernel,
         in_specs=any_specs(2),
-        out_shape=[jax.ShapeDtypeStruct(shape, BF) for shape in shapes],
+        out_shape=[jax.ShapeDtypeStruct((tokens, features), BF)] * 3,
         scratch_shapes=[
-            pltpu.VMEM(arrived.shape, BF),
+            pltpu.VMEM((ROW, tokens, LANES), BF),
             pltpu.VMEM((ROW, tokens // 2, LANES), BF),
             pltpu.SemaphoreType.DMA((2,)),
         ],
         compiler_params=pltpu.CompilerParams(vmem_limit_bytes=16 << 20),
-    )(arrived, near)
+    )(row, near)
+
+
+def final_kernel(parts_in, dpos_ref, dw_ref, parts_ref, sems):
+    brought([(parts_in, parts_ref)], sems)
+    cut = dpos_ref.shape[0]
+    total = parts_ref[0].astype(F32)
+    for z in range(1, parts_ref.shape[0]):
+        total = total + parts_ref[z].astype(F32)
+    dpos_ref[...] = total[:cut].astype(BF)
+    dw_ref[...] = total[cut:].astype(BF)
+
+
+def final_call(parts, pos_rows):
+    rows, features = parts.shape[1:]
+    shapes = [(pos_rows, features), (rows - pos_rows, features)]
+    return pl.pallas_call(
+        final_kernel,
+        in_specs=any_specs(1),
+        out_shape=[jax.ShapeDtypeStruct(shape, BF) for shape in shapes],
+        scratch_shapes=[pltpu.VMEM(parts.shape, BF), pltpu.SemaphoreType.DMA((1,))],
+        compiler_params=pltpu.CompilerParams(vmem_limit_bytes=16 << 20),
+    )(parts)
 
 
 def shifted(block, distance):
@@ -517,29 +551,25 @@
     tokens, features = query.shape
     slot_count = owner.shape[0]
     slot_rows = pos_store.shape[0]
-    half = tokens // 2
+    column = slot_count // ROW
     across = swapped(d_layer, 2)
-    row = in_row(pack_call(block_mask, query, key, value, pos_store))
+    far_pos = [pos_store] + [masked(pos_store, ROW * 4 * j) for j in range(1, 4)]
+    packed = pack_call(block_mask, query, key, value)
+    packed, across, *far_pos = lax.optimization_barrier((packed, across, *far_pos))
+    far_pos = jnp.concatenate(far_pos, axis=0)
+    slots = [far_pos] + [masked(far_pos, ROW * j) for j in range(1, 4)]
+    row = in_row(packed)
     halo = shifted(row[1:, :tokens], ROW)
-    at = tokens + half
-    pos = row[:, at : at + slot_rows // 2]
-    far_pos = [pos] + [masked(pos, ROW * 4 * j) for j in range(1, 4)]
-    far_pos = jnp.stack(far_pos)
-    slots = [far_pos] + [masked(far_pos, ROW * j) for j in range(1, 4)]
     grads = [d_layer, swapped(d_layer, 1), across, swapped(across, 1)]
-    ga = in_row(mix_call(grads, out_weight))
-    near, own, far, dpos = core_call(
-        owner, row, halo, slots, ga, content_bias[None], pos_bias[None]
-    )
+    ga = in_row(mix_call(grads, out_weight, slots))
+    near, own, far = core_call(owner, row, halo, ga, content_bias[None], pos_bias[None])
     back = shifted(far, -ROW)
     near = in_row(near)
     near, back = lax.optimization_barrier((near, back))
-    sums = weight_call(near, grads, dpos)
-    parts = in_column(sums.reshape((slot_count // ROW, ROW) + sums.shape[1:]))
-    arrived = in_row(meet_call(own, back, parts))
-    grad_query, grad_key, grad_value, grad_pos, grad_weight = final_call(
-        arrived, near, features, slot_rows, slot_rows // 2
-    )
+    met = in_row(weight_call(near, grads, own, back))
+    parts = in_column(sum_call(met, near, column, slot_rows, features, tokens))
+    grad_query, grad_key, grad_value = grads_call(met, near, tokens, features)
+    grad_pos, grad_weight = final_call(parts, slot_rows)
     return grad_query, grad_key, grad_value, grad_pos, grad_weight.T
 
 

time: 136 us -> 128 us (0.941)
  blocking collectives: 37.4 us -> 14.7 us
  waiting for transfers between devices: 27.9 us -> 37.9 us
  starting transfers between devices: 29.7 us -> 33.2 us
  Pallas kernels: 38.7 us -> 40.1 us
    all_to_all x1 -> x0, blocking collectives: 25 us -> none  [in_column(): return lax.all_to_all(block, 'ctx', 0, 0, axis_index_groups=groups)]
    ppermute x2, waiting for transfers between devices: 0.01 us -> 11.6 us  [shifted(): lax.ppermute(block, 'ctx', [(i, (i + distance) % count) for i in range(co...]
    all_to_all x0 -> x1, waiting for transfers between devices: none -> 10.7 us  [in_column(): return lax.all_to_all(block, 'ctx', 0, 0, axis_index_groups=groups)]
    ppermute x3, waiting for transfers between devices: 9.42 us -> 0.01 us  [swapped(): lax.ppermute(block, 'head', [(i, i ^ bit) for i in range(lax.axis_size('h...]
    all_to_all x0 -> x1, starting transfers between devices: none -> 5.02 us  [in_column(): return lax.all_to_all(block, 'ctx', 0, 0, axis_index_groups=groups)]
    ppermute x6, waiting for transfers between devices: 10.1 us -> 6.9 us  [masked(): lax.ppermute(block, 'ctx', [(i, i ^ mask) for i in range(lax.axis_size('c...]
    ppermute x6, starting transfers between devices: 13.7 us -> 10.7 us  [masked(): lax.ppermute(block, 'ctx', [(i, i ^ mask) for i in range(lax.axis_size('c...]
    all_to_all x1, blocking collectives: 12.4 us -> 14.7 us  [in_row(): return lax.all_to_all(block, 'ctx', 0, 0, axis_index_groups=groups)]
  transfers between devices with their start and end apart: 14 -> 15, of which waited for: 10 -> 9; matrix products, arithmetic and copies ran while one was open for 0% -> 0% of each run, Pallas kernels for 1% -> 5%
where the time goes in v4:
time: 128 us
  Pallas kernels  40.1 us (31%)
  waiting for transfers between devices  37.9 us (30%)
  starting transfers between devices  33.2 us (26%)
  blocking collectives  14.7 us (11%)
    pallas_call x1, Pallas kernels, core_call(): pl.pallas_call(core_kernel, grid=(ROW,), in_specs=smem_specs(1) + any_spe...  29.7 us
    all_to_all x1, blocking collectives, in_row(): return lax.all_to_all(block, 'ctx', 0, 0, axis_index_groups=groups)  14.7 us
    all_to_all x3, starting transfers between devices, in_row(): return lax.all_to_all(block, 'ctx', 0, 0, axis_index_groups=groups)  13.8 us
    ppermute x2, waiting for transfers between devices, shifted(): lax.ppermute(block, 'ctx', [(i, (i + distance) % count) for i in range(co...  11.6 us
    all_to_all x1, waiting for transfers between devices, in_column(): return lax.all_to_all(block, 'ctx', 0, 0, axis_index_groups=groups)  10.7 us
    ppermute x6, starting transfers between devices, masked(): lax.ppermute(block, 'ctx', [(i, i ^ mask) for i in range(lax.axis_size('c...  10.7 us
    all_to_all x3, waiting for transfers between devices, in_row(): return lax.all_to_all(block, 'ctx', 0, 0, axis_index_groups=groups)  8.7 us
    ppermute x6, waiting for transfers between devices, masked(): lax.ppermute(block, 'ctx', [(i, i ^ mask) for i in range(lax.axis_size('c...  6.9 us
  transfers between devices with their start and end apart: 15, of which 9 were waited for; matrix products, arithmetic and copies ran while one was open for 0% of the time, Pallas kernels for 5%

profile of v4, /device:TPU:16, one launch (start us, length us, event | category | flops | bytes accessed | tf_op | source)
XLA Modules:
  0.0 127.7 jit_solution(522200242630592077)
XLA Ops:
  0.6 2.2 %collective-permute-start = (bf16[512,256]{1,0:T(8,128)(2,1)}, bf16[512,256]{1,0:T(8,128)(2,1)S(1)}, u32[]{:S(2)}, u32[]{:S(2)}) collective-permute-start(bf16[512,256]{1,0:T(8,128)(2,1)} %g0_in.3), channel_id=1, source_target_pairs={{0,2},{1,3},{2,0},{3,1},{4,6},{5,7},{6,4},{7,5},{8,10},{9,11},{10,... | collective-permute-start | bytes 786440 | tf_op jit(solution)/shard_map/ppermute | solution.py:529
  2.8 5.5 %collective-permute-start.2 = (bf16[32,256]{1,0:T(8,128)(2,1)}, bf16[32,256]{1,0:T(8,128)(2,1)S(1)}, u32[]{:S(2)}, u32[]{:S(2)}) collective-permute-start(bf16[32,256]{1,0:T(8,128)(2,1)} %param.13), channel_id=1, source_target_pairs={{0,128},{4,132},{8,136},{12,140},{16,144},{20,148},{24,152},{28,15... | collective-permute-start | bytes 49160 | tf_op jit(solution)/shard_map/ppermute | solution.py:545
  8.2 1.5 %collective-permute-start.1 = (bf16[32,256]{1,0:T(8,128)(2,1)}, bf16[32,256]{1,0:T(8,128)(2,1)S(1)}, u32[]{:S(2)}, u32[]{:S(2)}) collective-permute-start(bf16[32,256]{1,0:T(8,128)(2,1)} %param.13), channel_id=1, source_target_pairs={{0,64},{4,68},{8,72},{12,76},{16,80},{20,84},{24,88},{28,92},{32,9... | collective-permute-start | bytes 49160 | tf_op jit(solution)/shard_map/ppermute | solution.py:545
  9.7 0.0 collective-permute-start.3
  9.7 3.4 %shard_map.137 = bf16[4,784,128]{2,1,0:T(8,128)(2,1)} custom-call(s32[1,4]{1,0:T(1,128)} %mask_ref.1, bf16[512,256]{1,0:T(8,128)(2,1)} %q_in.1, bf16[512,256]{1,0:T(8,128)(2,1)} %k_in.1, bf16[512,256]{1,0:T(8,128)(2,1)} %v_in.1), custom_call_target="tpu_custom_call" | custom-call | tf_op jit(solution)/shard_map/pallas_call | solution.py:112
  13.1 0.0 copy-start
  13.1 0.0 copy-start.5
  13.1 0.0 copy-start.2
  13.1 0.0 collective-permute-done.2
  13.1 0.0 collective-permute-done.1
  13.1 2.6 %collective-permute-done.3 = bf16[32,256]{1,0:T(8,128)(2,1)S(1)} collective-permute-done((bf16[32,256]{1,0:T(8,128)(2,1)}, bf16[32,256]{1,0:T(8,128)(2,1)S(1)}, u32[]{:S(2)}, u32[]{:S(2)}) %collective-permute-start.3) | collective-permute-done | bytes 16416 | tf_op jit(solution)/shard_map/ppermute | solution.py:545
  15.8 0.0 collective-permute-done.g2_in
  15.8 4.3 %all-to-all-start = ((bf16[4,784,128]{2,1,0:T(8,128)(2,1)}), bf16[4,784,128]{2,1,0:T(8,128)(2,1)S(1)}, u32[]{:S(2)}, u32[]{:S(2)}) async-start(bf16[4,784,128]{2,1,0:T(8,128)(2,1)} %shard_map.137), calls=%async_computation | async-start | bytes 1605632 | tf_op jit(solution)/shard_map/all_to_all | solution.py:535
  20.1 0.0 copy-done
  20.1 0.0 collective-permute-start.5
  20.1 0.5 collective-permute-start.6
  20.6 0.0 copy-done.5
  20.6 2.7 %collective-permute-start.9 = (bf16[128,256]{1,0:T(8,128)(2,1)S(1)}, bf16[128,256]{1,0:T(8,128)(2,1)S(1)}, u32[]{:S(2)}, u32[]{:S(2)}) collective-permute-start(bf16[128,256]{1,0:T(8,128)(2,1)S(1)} %constant_dynamic-update-slice_fusion.s0_in), channel_id=1, source_target_pairs={{0,48},{4,52},{8,56},{12,60},{16,32},{20,36},{24,40},{28,44},{32,1... | collective-permute-start | bytes 196616 | tf_op jit(solution)/shard_map/ppermute | solution.py:545
  23.3 1.0 collective-permute-start.8
  24.3 0.0 collective-permute-start.7
  24.4 0.0 collective-permute-done.5.g1_in
  24.4 2.2 %collective-permute-done.9.s3_in = bf16[128,256]{1,0:T(8,128)(2,1)S(1)} collective-permute-done((bf16[128,256]{1,0:T(8,128)(2,1)S(1)}, bf16[128,256]{1,0:T(8,128)(2,1)S(1)}, u32[]{:S(2)}, u32[]{:S(2)}) %collective-permute-start.9) | collective-permute-done | bytes 65568 | tf_op jit(solution)/shard_map/ppermute | solution.py:545
  26.5 1.3 %collective-permute-done.8.s2_in = bf16[128,256]{1,0:T(8,128)(2,1)S(1)} collective-permute-done((bf16[128,256]{1,0:T(8,128)(2,1)S(1)}, bf16[128,256]{1,0:T(8,128)(2,1)S(1)}, u32[]{:S(2)}, u32[]{:S(2)}) %collective-permute-start.8) | collective-permute-done | bytes 65568 | tf_op jit(solution)/shard_map/ppermute | solution.py:545
  27.9 0.8 collective-permute-done.7.s1_in
  28.6 0.0 collective-permute-done.6.g3_in
  28.6 0.0 copy-done.2
  28.6 2.0 %shard_map.138 = bf16[4,512,128]{2,1,0:T(8,128)(2,1)} custom-call(bf16[512,256]{1,0:T(8,128)(2,1)S(1)} %copy-done, bf16[512,256]{1,0:T(8,128)(2,1)S(1)} %collective-permute-done.5.g1_in, bf16[512,256]{1,0:T(8,128)(2,1)S(1)} %collective-permute-done.g2_in, bf16[512,256]{1,0:T(8,128)(2,1)S(1)} %collective-permute-done.6.g3_in, ...), custom_call_target="tpu_custom_call" | custom-call | tf_op jit(solution)/shard_map/pallas_call | solution.py:146
  30.6 0.0 all-to-all-done.row_in
  30.6 0.0 copy-start.3
  30.6 4.8 %all-to-all-start.1 = ((bf16[4,512,128]{2,1,0:T(8,128)(2,1)}), bf16[4,512,128]{2,1,0:T(8,128)(2,1)S(1)}, u32[]{:S(2)}, u32[]{:S(2)}) async-start(bf16[4,512,128]{2,1,0:T(8,128)(2,1)} %shard_map.138), calls=%async_computation.1 | async-start | bytes 1048576 | tf_op jit(solution)/shard_map/all_to_all | solution.py:535
  35.5 0.0 copy-done.3
  35.5 1.0 collective-permute-start.4
  36.5 7.2 %all-to-all-done.1.ga_in = bf16[4,512,128]{2,1,0:T(8,128)(2,1)S(1)} async-done(((bf16[4,512,128]{2,1,0:T(8,128)(2,1)}), bf16[4,512,128]{2,1,0:T(8,128)(2,1)S(1)}, u32[]{:S(2)}, u32[]{:S(2)}) %all-to-all-start.1) | async-done | bytes 524320 | tf_op jit(solution)/shard_map/all_to_all | solution.py:535
  43.7 0.0 copy-start.4
  43.7 3.5 %collective-permute-done.4.halo_in = bf16[3,512,128]{2,1,0:T(8,128)(2,1)S(1)} collective-permute-done((bf16[3,512,128]{2,1,0:T(8,128)(2,1)S(1)}, bf16[3,512,128]{2,1,0:T(8,128)(2,1)S(1)}, u32[]{:S(2)}, u32[]{:S(2)}) %collective-permute-start.4) | collective-permute-done | bytes 393248 | tf_op jit(solution)/shard_map/ppermute | solution.py:525
  47.2 0.0 copy-start.6
  47.2 0.0 copy-done.4
  47.2 0.7 copy-done.6
  48.0 29.7 %shard_map.139 = (bf16[4,768,128]{2,1,0:T(8,128)(2,1)}, f32[4,512,128]{2,1,0:T(8,128)}, bf16[3,512,128]{2,1,0:T(8,128)(2,1)}) custom-call(s32[64]{0:T(128)} %owner_ref.1, bf16[4,784,128]{2,1,0:T(8,128)(2,1)} %copy-done.3, bf16[3,512,128]{2,1,0:T(8,128)(2,1)} %copy-done.6, bf16[4,512,128]{2,1,0:T(8,128)(2,1)} %copy-done.4, f32[1,256]{1,0:T(1,128)} %bitcast.4, ...), custom_call_target="tpu_custom_call" | custom-call | flops 40000000000 | bytes 8000000 | tf_op jit(solution)/shard_map/pallas_call | solution.py:364
  77.6 0.0 copy-start.1
  77.7 4.7 %all-to-all-start.2 = ((bf16[4,768,128]{2,1,0:T(8,128)(2,1)}), bf16[4,768,128]{2,1,0:T(8,128)(2,1)S(1)}, u32[]{:S(2)}, u32[]{:S(2)}) async-start(bf16[4,768,128]{2,1,0:T(8,128)(2,1)} %get-tuple-element.27), calls=%async_computation.2 | async-start | bytes 1572864 | tf_op jit(solution)/shard_map/all_to_all | solution.py:535
  82.3 0.0 collective-permute-start.10
  82.3 8.1 %collective-permute-done.10.far_in = bf16[3,512,128]{2,1,0:T(8,128)(2,1)S(1)} collective-permute-done((bf16[3,512,128]{2,1,0:T(8,128)(2,1)}, bf16[3,512,128]{2,1,0:T(8,128)(2,1)S(1)}, u32[]{:S(2)}, u32[]{:S(2)}) %collective-permute-start.10) | collective-permute-done | bytes 393248 | tf_op jit(solution)/shard_map/ppermute | solution.py:525
  90.4 1.5 %all-to-all-done.2.att_in.near_in = bf16[4,768,128]{2,1,0:T(8,128)(2,1)S(1)} async-done(((bf16[4,768,128]{2,1,0:T(8,128)(2,1)}), bf16[4,768,128]{2,1,0:T(8,128)(2,1)S(1)}, u32[]{:S(2)}, u32[]{:S(2)}) %all-to-all-start.2) | async-done | bytes 786464 | tf_op jit(solution)/shard_map/all_to_all | solution.py:535
  91.9 0.0 copy-done.1
  91.9 2.1 %shard_map.140 = bf16[4,1024,128]{2,1,0:T(8,128)(2,1)} custom-call(bf16[4,768,128]{2,1,0:T(8,128)(2,1)S(1)} %all-to-all-done.2.att_in.near_in, bf16[512,256]{1,0:T(8,128)(2,1)S(1)} %copy-done, bf16[512,256]{1,0:T(8,128)(2,1)S(1)} %collective-permute-done.5.g1_in, bf16[512,256]{1,0:T(8,128)(2,1)S(1)} %collective-permute-done.g2_in, ...), custom_call_target="tpu_custom_call" | custom-call | tf_op jit(solution)/shard_map/pallas_call | solution.py:429
  94.0 14.7 %all_to_all.25.row_in = bf16[4,1024,128]{2,1,0:T(8,128)(2,1)S(1)} all-to-all(bf16[4,1024,128]{2,1,0:T(8,128)(2,1)} %shard_map.140), channel_id=1, replica_groups={{0,4,8,12},{16,20,24,28},{32,36,40,44},{48,52,56,60},{64,68,72,76},{80,..., dimensions={0} | all-to-all | bytes 2097152 | tf_op jit(solution)/shard_map/all_to_all | solution.py:535
  108.7 1.0 shard_map.142
  109.7 5.0 %all-to-all-start.4 = ((bf16[16,48,256]{2,1,0:T(8,128)(2,1)}), bf16[16,48,256]{2,1,0:T(8,128)(2,1)S(1)}, u32[]{:S(2)}, u32[]{:S(2)}) async-start(bf16[16,48,256]{2,1,0:T(8,128)(2,1)} %shard_map.142), calls=%async_computation.4 | async-start | bytes 786432 | tf_op jit(solution)/shard_map/all_to_all | solution.py:541
  114.8 1.2 shard_map.141
  115.9 10.7 %all-to-all-done.4.parts_in = bf16[16,48,256]{2,1,0:T(8,128)(2,1)S(1)} async-done(((bf16[16,48,256]{2,1,0:T(8,128)(2,1)}), bf16[16,48,256]{2,1,0:T(8,128)(2,1)S(1)}, u32[]{:S(2)}, u32[]{:S(2)}) %all-to-all-start.4) | async-done | bytes 393248 | tf_op jit(solution)/shard_map/all_to_all | solution.py:541
  126.7 0.8 shard_map.143
  (5 shorter events, 0.0 us)
Async XLA Ops:
  0.6 15.1 %collective-permute-start = (bf16[512,256]{1,0:T(8,128)(2,1)}, bf16[512,256]{1,0:T(8,128)(2,1)S(1)}, u32[]{:S(2)}, u32[]{:S(2)}) collective-permute-start(bf16[512,256]{1,0:T(8,128)(2,1)} %g0_in.3), channel_id=1, source_target_pairs={{0,2},{1,3},{2,0},{3,1},{4,6},{5,7},{6,4},{7,5},{8,10},{9,11},{10,... | collective-permute-start | bytes 786440 | tf_op jit(solution)/shard_map/ppermute | solution.py:529
  2.8 10.3 %collective-permute-start.2 = (bf16[32,256]{1,0:T(8,128)(2,1)}, bf16[32,256]{1,0:T(8,128)(2,1)S(1)}, u32[]{:S(2)}, u32[]{:S(2)}) collective-permute-start(bf16[32,256]{1,0:T(8,128)(2,1)} %param.13), channel_id=1, source_target_pairs={{0,128},{4,132},{8,136},{12,140},{16,144},{20,148},{24,152},{28,15... | collective-permute-start | bytes 49160 | tf_op jit(solution)/shard_map/ppermute | solution.py:545
  8.2 4.9 %collective-permute-start.1 = (bf16[32,256]{1,0:T(8,128)(2,1)}, bf16[32,256]{1,0:T(8,128)(2,1)S(1)}, u32[]{:S(2)}, u32[]{:S(2)}) collective-permute-start(bf16[32,256]{1,0:T(8,128)(2,1)} %param.13), channel_id=1, source_target_pairs={{0,64},{4,68},{8,72},{12,76},{16,80},{20,84},{24,88},{28,92},{32,9... | collective-permute-start | bytes 49160 | tf_op jit(solution)/shard_map/ppermute | solution.py:545
  9.7 6.1 %collective-permute-start.3 = (bf16[32,256]{1,0:T(8,128)(2,1)}, bf16[32,256]{1,0:T(8,128)(2,1)S(1)}, u32[]{:S(2)}, u32[]{:S(2)}) collective-permute-start(bf16[32,256]{1,0:T(8,128)(2,1)} %param.13), channel_id=1, source_target_pairs={{0,192},{4,196},{8,200},{12,204},{16,208},{20,212},{24,216},{28,22... | collective-permute-start | bytes 49160 | tf_op jit(solution)/shard_map/ppermute | solution.py:545
  13.1 7.0 %copy-start = (bf16[512,256]{1,0:T(8,128)(2,1)S(1)}, bf16[512,256]{1,0:T(8,128)(2,1)}, u32[]{:S(2)}) copy-start(bf16[512,256]{1,0:T(8,128)(2,1)} %g0_in.3) | copy-start | bytes 786436
  13.1 7.5 %copy-start.5 = (bf16[32,256]{1,0:T(8,128)(2,1)S(1)}, bf16[32,256]{1,0:T(8,128)(2,1)}, u32[]{:S(2)}) copy-start(bf16[32,256]{1,0:T(8,128)(2,1)} %param.13) | copy-start | bytes 49156
  13.1 15.5 %copy-start.2 = (bf16[256,1024]{1,0:T(8,128)(2,1)S(1)}, bf16[256,1024]{1,0:T(8,128)(2,1)}, u32[]{:S(2)}) copy-start(bf16[256,1024]{1,0:T(8,128)(2,1)} %weight_in.1) | copy-start | bytes 1572868
  15.8 14.8 %all-to-all-start = ((bf16[4,784,128]{2,1,0:T(8,128)(2,1)}), bf16[4,784,128]{2,1,0:T(8,128)(2,1)S(1)}, u32[]{:S(2)}, u32[]{:S(2)}) async-start(bf16[4,784,128]{2,1,0:T(8,128)(2,1)} %shard_map.137), calls=%async_computation | async-start | bytes 1605632 | tf_op jit(solution)/shard_map/all_to_all | solution.py:535
  20.1 4.3 %collective-permute-start.5 = (bf16[512,256]{1,0:T(8,128)(2,1)S(1)}, bf16[512,256]{1,0:T(8,128)(2,1)S(1)}, u32[]{:S(2)}, u32[]{:S(2)}) collective-permute-start(bf16[512,256]{1,0:T(8,128)(2,1)S(1)} %copy-done), channel_id=1, source_target_pairs={{0,1},{1,0},{2,3},{3,2},{4,5},{5,4},{6,7},{7,6},{8,9},{9,8},{10,11... | collective-permute-start | bytes 786440 | tf_op jit(solution)/shard_map/ppermute | solution.py:529
  20.1 8.5 %collective-permute-start.6 = (bf16[512,256]{1,0:T(8,128)(2,1)S(1)}, bf16[512,256]{1,0:T(8,128)(2,1)S(1)}, u32[]{:S(2)}, u32[]{:S(2)}) collective-permute-start(bf16[512,256]{1,0:T(8,128)(2,1)S(1)} %collective-permute-done.g2_in), channel_id=1, source_target_pairs={{0,1},{1,0},{2,3},{3,2},{4,5},{5,4},{6,7},{7,6},{8,9},{9,8},{10,11... | collective-permute-start | bytes 786440 | tf_op jit(solution)/shard_map/ppermute | solution.py:529
  20.6 5.9 %collective-permute-start.9 = (bf16[128,256]{1,0:T(8,128)(2,1)S(1)}, bf16[128,256]{1,0:T(8,128)(2,1)S(1)}, u32[]{:S(2)}, u32[]{:S(2)}) collective-permute-start(bf16[128,256]{1,0:T(8,128)(2,1)S(1)} %constant_dynamic-update-slice_fusion.s0_in), channel_id=1, source_target_pairs={{0,48},{4,52},{8,56},{12,60},{16,32},{20,36},{24,40},{28,44},{32,1... | collective-permute-start | bytes 196616 | tf_op jit(solution)/shard_map/ppermute | solution.py:545
  23.3 4.5 %collective-permute-start.8 = (bf16[128,256]{1,0:T(8,128)(2,1)S(1)}, bf16[128,256]{1,0:T(8,128)(2,1)S(1)}, u32[]{:S(2)}, u32[]{:S(2)}) collective-permute-start(bf16[128,256]{1,0:T(8,128)(2,1)S(1)} %constant_dynamic-update-slice_fusion.s0_in), channel_id=1, source_target_pairs={{0,32},{4,36},{8,40},{12,44},{16,48},{20,52},{24,56},{28,60},{32,0... | collective-permute-start | bytes 196616 | tf_op jit(solution)/shard_map/ppermute | solution.py:545
  24.3 4.3 %collective-permute-start.7 = (bf16[128,256]{1,0:T(8,128)(2,1)S(1)}, bf16[128,256]{1,0:T(8,128)(2,1)S(1)}, u32[]{:S(2)}, u32[]{:S(2)}) collective-permute-start(bf16[128,256]{1,0:T(8,128)(2,1)S(1)} %constant_dynamic-update-slice_fusion.s0_in), channel_id=1, source_target_pairs={{0,16},{4,20},{8,24},{12,28},{16,0},{20,4},{24,8},{28,12},{32,48},... | collective-permute-start | bytes 196616 | tf_op jit(solution)/shard_map/ppermute | solution.py:545
  30.6 4.9 %copy-start.3 = (bf16[4,784,128]{2,1,0:T(8,128)(2,1)}, bf16[4,784,128]{2,1,0:T(8,128)(2,1)S(1)}, u32[]{:S(2)}) copy-start(bf16[4,784,128]{2,1,0:T(8,128)(2,1)S(1)} %all-to-all-done.row_in) | copy-start | bytes 2408452
  30.6 13.1 %all-to-all-start.1 = ((bf16[4,512,128]{2,1,0:T(8,128)(2,1)}), bf16[4,512,128]{2,1,0:T(8,128)(2,1)S(1)}, u32[]{:S(2)}, u32[]{:S(2)}) async-start(bf16[4,512,128]{2,1,0:T(8,128)(2,1)} %shard_map.138), calls=%async_computation.1 | async-start | bytes 1048576 | tf_op jit(solution)/shard_map/all_to_all | solution.py:535
  35.5 11.8 %collective-permute-start.4 = (bf16[3,512,128]{2,1,0:T(8,128)(2,1)S(1)}, bf16[3,512,128]{2,1,0:T(8,128)(2,1)S(1)}, u32[]{:S(2)}, u32[]{:S(2)}) collective-permute-start(bf16[3,512,128]{2,1,0:T(8,128)(2,1)S(1)} %slice.4), channel_id=1, source_target_pairs={{0,16},{4,20},{8,24},{12,28},{16,32},{20,36},{24,40},{28,44},{32,4... | collective-permute-start | bytes 1179656 | tf_op jit(solution)/shard_map/ppermute | solution.py:525
  43.7 3.5 %copy-start.4 = (bf16[4,512,128]{2,1,0:T(8,128)(2,1)}, bf16[4,512,128]{2,1,0:T(8,128)(2,1)S(1)}, u32[]{:S(2)}) copy-start(bf16[4,512,128]{2,1,0:T(8,128)(2,1)S(1)} %all-to-all-done.1.ga_in) | copy-start | bytes 1572868
  47.2 0.7 copy-start.6
  77.6 14.3 %copy-start.1 = (f32[4,512,128]{2,1,0:T(8,128)S(1)}, f32[4,512,128]{2,1,0:T(8,128)}, u32[]{:S(2)}) copy-start(f32[4,512,128]{2,1,0:T(8,128)} %get-tuple-element.30.own_in) | copy-start | bytes 3145732
  77.7 14.3 %all-to-all-start.2 = ((bf16[4,768,128]{2,1,0:T(8,128)(2,1)}), bf16[4,768,128]{2,1,0:T(8,128)(2,1)S(1)}, u32[]{:S(2)}, u32[]{:S(2)}) async-start(bf16[4,768,128]{2,1,0:T(8,128)(2,1)} %get-tuple-element.27), calls=%async_computation.2 | async-start | bytes 1572864 | tf_op jit(solution)/shard_map/all_to_all | solution.py:535
  82.3 8.1 %collective-permute-start.10 = (bf16[3,512,128]{2,1,0:T(8,128)(2,1)}, bf16[3,512,128]{2,1,0:T(8,128)(2,1)S(1)}, u32[]{:S(2)}, u32[]{:S(2)}) collective-permute-start(bf16[3,512,128]{2,1,0:T(8,128)(2,1)} %get-tuple-element.28), channel_id=1, source_target_pairs={{0,240},{4,244},{8,248},{12,252},{16,0},{20,4},{24,8},{28,12},{32,... | collective-permute-start | bytes 1179656 | tf_op jit(solution)/shard_map/ppermute | solution.py:525
  109.7 16.9 %all-to-all-start.4 = ((bf16[16,48,256]{2,1,0:T(8,128)(2,1)}), bf16[16,48,256]{2,1,0:T(8,128)(2,1)S(1)}, u32[]{:S(2)}, u32[]{:S(2)}) async-start(bf16[16,48,256]{2,1,0:T(8,128)(2,1)} %shard_map.142), calls=%async_computation.4 | async-start | bytes 786432 | tf_op jit(solution)/shard_map/all_to_all | solution.py:541

commit v5 on v4

--- a/solution.py
+++ b/solution.py
@@ -82,13 +82,14 @@
     return pl.BlockSpec(shape, lambda *_: (0,) * len(shape))
 
 
-def brought(pairs, sems):
+def brought(pairs, sems, meanwhile=lambda: None):
     copies = [
         pltpu.make_async_copy(source, target, sems.at[i])
         for i, (source, target) in enumerate(pairs)
     ]
     for copy in copies:
         copy.start()
+    meanwhile()
     for copy in copies:
         copy.wait()
 
@@ -183,16 +184,19 @@
         rows = 2 * packed * ROW // count
         pairs += [(ga_in.at[:, 0:half], ga_ref), (ga_in.at[:, half : half + packed], pos_ref.at[0])]
         pairs.append((row_in.at[:, tokens + half : tokens + half + 16], flag_ref))
-        brought(pairs, sems)
+
+        def clear():
+            grads[...] = jnp.zeros_like(grads)
+            dist[...] = jnp.zeros_like(dist)
+            table[0:tokens, :] = jnp.zeros((tokens, LANES), BF)
+
+        brought(pairs, sems, clear)
         for b in range(ROW):
             pos_ref[1, b] = turned(pos_ref[0, b]).astype(BF)
         turn = (ROW - (lax.axis_index("ctx") & 3)) * HD % cb_in.shape[1]
         for bias_in, bias_ref in ((cb_in, cb_ref), (pb_in, pb_ref)):
             bias = jnp.broadcast_to(bias_in[...], (8, bias_in.shape[1]))
             bias_ref[...] = pltpu.roll(bias, turn, 1)[0:1, :LANES]
-        grads[...] = jnp.zeros_like(grads)
-        dist[...] = jnp.zeros_like(dist)
-        table[0:tokens, :] = jnp.zeros((tokens, LANES), BF)
         for d in range(count):
             slot = owner_ref[d]
             apart = (slot >> 2) ^ (lax.axis_index("ctx") >> 2)
@@ -221,6 +225,10 @@
         barred.append(jnp.where(there & (flag > 0.5), 0.0, NEG))
     state = [{}, {}]
 
+    def cols_of(w, r):
+        width = half if r == 0 and w == ROW - 1 else tokens
+        return width, slice(w * tokens, w * tokens + width)
+
     def first(r):
         query = queries[block].astype(F32)
         ga = ga_ref[block].astype(F32)
@@ -231,12 +239,12 @@
         pq = jnp.where(low, query + pb_ref[...], 0.0).astype(BF)
         state[r].update(ga=ga, gal=ga.astype(BF), cq=cq, pq=pq)
         base = half * (1 - r)
-        rel_ref[r] = nt(pq * scale, flipped[base : base + wide, :])
+        width = span if r == 0 else wide
+        rel_ref[r, :, :width] = nt(pq * scale, flipped[base : base + width, :])
         cqs = cq * scale
         for w in range(ROW):
-            score_ref[r, :, w * tokens : (w + 1) * tokens] = nt(
-                cqs, keys[pl.ds(starts[w], tokens), :]
-            )
+            width, cols = cols_of(w, r)
+            score_ref[r, :, cols] = nt(cqs, keys[pl.ds(starts[w], width), :])
 
     def soften(r):
         for g in groups:
@@ -245,22 +253,24 @@
             )
             scores = []
             for w in range(ROW):
-                cols = slice(w * tokens, (w + 1) * tokens)
+                width, cols = cols_of(w, r)
                 s = score_ref[r, g, cols] + moved[:, cols]
                 if w == ROW - 1:
-                    row = lax.broadcasted_iota(jnp.int32, (chunk, tokens), 0) + r * half + g.start
-                    col = lax.broadcasted_iota(jnp.int32, (chunk, tokens), 1)
+                    row = lax.broadcasted_iota(jnp.int32, (chunk, width), 0) + r * half + g.start
+                    col = lax.broadcasted_iota(jnp.int32, (chunk, width), 1)
                     s = jnp.where(col <= row, s, NEG)
                 else:
                     s = s + barred[w]
                 scores.append(s)
-            top = functools.reduce(jnp.maximum, scores)
+            parts = [s[:, x : x + half] for s in scores for x in range(0, s.shape[1], half)]
+            top = functools.reduce(jnp.maximum, parts)
             top = jnp.max(top, axis=1, keepdims=True)
             weights = [jnp.exp(s - top) for s in scores]
-            total = functools.reduce(jnp.add, weights)
+            parts = [e[:, x : x + half] for e in weights for x in range(0, e.shape[1], half)]
+            total = functools.reduce(jnp.add, parts)
             inv = 1.0 / jnp.sum(total, axis=1, keepdims=True)
             for w in range(ROW):
-                cols = slice(w * tokens, (w + 1) * tokens)
+                _, cols = cols_of(w, r)
                 p = weights[w] * inv
                 score_ref[r, g, cols] = p
                 low_ref[r, g, cols] = p.astype(BF)
@@ -268,41 +278,43 @@
     def second(r):
         att = None
         for w in range(ROW):
-            cols = slice(w * tokens, (w + 1) * tokens)
-            part = nn(low_ref[r, :, cols], keys[pl.ds(starts[w], tokens), :])
+            width, cols = cols_of(w, r)
+            part = nn(low_ref[r, :, cols], keys[pl.ds(starts[w], width), :])
             att = part if att is None else att + part
         att = att.astype(BF).astype(F32)
         state[r]["att"] = turned(att) if r == 0 else att
         dot = jnp.sum(state[r]["ga"] * att, axis=1, keepdims=True)
         dot_ref[r] = jnp.broadcast_to(dot, (half, LANES))
         for w in range(ROW):
-            cols = slice(w * tokens, (w + 1) * tokens)
-            rel_ref[r, :, cols] = nt(state[r]["gal"], keys[pl.ds(starts[w], tokens), :])
+            width, cols = cols_of(w, r)
+            rel_ref[r, :, cols] = nt(state[r]["gal"], keys[pl.ds(starts[w], width), :])
 
     def steepen(r):
         for g in groups:
             dot = dot_ref[r, g, 0:1]
             for w in range(ROW):
-                cols = slice(w * tokens, (w + 1) * tokens)
+                _, cols = cols_of(w, r)
                 ds = 0.125 * score_ref[r, g, cols] * (rel_ref[r, g, cols] - dot)
                 ds_ref[r, g, cols] = ds.astype(BF)
 
     def third(r):
         acc = None
         for w in range(ROW):
-            cols = slice(w * tokens, (w + 1) * tokens)
+            width, cols = cols_of(w, r)
             ds = ds_ref[r, :, cols]
-            for x in range(2):
+            for x in range(width // half):
                 at = (2 * ROW - 1 - (2 * w + x)) * half
                 rel_ref[r, :, at : at + half] = nn(ds[:, x * half : (x + 1) * half], anti)
+        if r == 0:
+            rel_ref[r, :, :half] = jnp.zeros((half, half), F32)
         rel_ref[r, :, span:] = jnp.zeros((half, wide - span), F32)
         for w in range(ROW):
-            cols = slice(w * tokens, (w + 1) * tokens)
+            width, cols = cols_of(w, r)
             ds = ds_ref[r, :, cols]
-            grads[:, pl.ds(starts[w], tokens)] += tn(state[r]["cq"], ds) + tn(
+            grads[:, pl.ds(starts[w], width)] += tn(state[r]["cq"], ds) + tn(
                 state[r]["gal"], low_ref[r, :, cols]
             )
-            part = nn(ds, keys[pl.ds(starts[w], tokens), :])
+            part = nn(ds, keys[pl.ds(starts[w], width), :])
             acc = part if acc is None else acc + part
         state[r]["acc"] = acc
 
@@ -313,9 +325,11 @@
             ).astype(BF)
 
     def fourth(r):
-        start = half * r
-        acc = state[r]["acc"] + nn(spread_ref[r], table[start : start + wide, :])
-        dist[:, start : start + wide] += tn(state[r]["pq"], spread_ref[r])
+        skip = half if r == 0 else 0
+        start, stop = half * r + skip, half * r + wide
+        spread = spread_ref[r, :, skip:]
+        acc = state[r]["acc"] + nn(spread, table[start:stop, :])
+        dist[:, start:stop] += tn(state[r]["pq"], spread)
         state[r]["acc"] = turned(acc) if r == 1 else acc
 
     first(0)

time: 128 us -> 127 us (level)
  Pallas kernels: 40.1 us -> 38.7 us
    pallas_call x1, Pallas kernels: 29.7 us -> 28.3 us  [core_call(): pl.pallas_call(core_kernel, grid=(ROW,), in_specs=smem_specs(1) + any_spe...]
where the time goes in v5:
time: 127 us; the launch traced here: 126 us
  Pallas kernels  38.7 us (30%)
  waiting for transfers between devices  37.9 us (30%)
  starting transfers between devices  33.2 us (26%)
  blocking collectives  14.7 us (12%)
    pallas_call x1, Pallas kernels, core_call(): pl.pallas_call(core_kernel, grid=(ROW,), in_specs=smem_specs(1) + any_spe...  28.3 us
    all_to_all x1, blocking collectives, in_row(): return lax.all_to_all(block, 'ctx', 0, 0, axis_index_groups=groups)  14.7 us
    all_to_all x3, starting transfers between devices, in_row(): return lax.all_to_all(block, 'ctx', 0, 0, axis_index_groups=groups)  13.8 us
    ppermute x2, waiting for transfers between devices, shifted(): lax.ppermute(block, 'ctx', [(i, (i + distance) % count) for i in range(co...  11.6 us
    all_to_all x1, waiting for transfers between devices, in_column(): return lax.all_to_all(block, 'ctx', 0, 0, axis_index_groups=groups)  10.7 us
    ppermute x6, starting transfers between devices, masked(): lax.ppermute(block, 'ctx', [(i, i ^ mask) for i in range(lax.axis_size('c...  10.7 us
    all_to_all x3, waiting for transfers between devices, in_row(): return lax.all_to_all(block, 'ctx', 0, 0, axis_index_groups=groups)  8.7 us
    ppermute x6, waiting for transfers between devices, masked(): lax.ppermute(block, 'ctx', [(i, i ^ mask) for i in range(lax.axis_size('c...  6.9 us
  transfers between devices with their start and end apart: 15, of which 9 were waited for; matrix products, arithmetic and copies ran while one was open for 0% of the time, Pallas kernels for 5%

profile of v5, /device:TPU:16, one launch (start us, length us, event | category | flops | bytes accessed | tf_op | source)
XLA Modules:
  0.0 126.3 jit_solution(3037202410132066423)
XLA Ops:
  0.6 2.2 %collective-permute-start = (bf16[512,256]{1,0:T(8,128)(2,1)}, bf16[512,256]{1,0:T(8,128)(2,1)S(1)}, u32[]{:S(2)}, u32[]{:S(2)}) collective-permute-start(bf16[512,256]{1,0:T(8,128)(2,1)} %g0_in.3), channel_id=1, source_target_pairs={{0,2},{1,3},{2,0},{3,1},{4,6},{5,7},{6,4},{7,5},{8,10},{9,11},{10,... | collective-permute-start | bytes 786440 | tf_op jit(solution)/shard_map/ppermute | solution.py:543
  2.8 5.5 %collective-permute-start.2 = (bf16[32,256]{1,0:T(8,128)(2,1)}, bf16[32,256]{1,0:T(8,128)(2,1)S(1)}, u32[]{:S(2)}, u32[]{:S(2)}) collective-permute-start(bf16[32,256]{1,0:T(8,128)(2,1)} %param.13), channel_id=1, source_target_pairs={{0,128},{4,132},{8,136},{12,140},{16,144},{20,148},{24,152},{28,15... | collective-permute-start | bytes 49160 | tf_op jit(solution)/shard_map/ppermute | solution.py:559
  8.2 1.5 %collective-permute-start.1 = (bf16[32,256]{1,0:T(8,128)(2,1)}, bf16[32,256]{1,0:T(8,128)(2,1)S(1)}, u32[]{:S(2)}, u32[]{:S(2)}) collective-permute-start(bf16[32,256]{1,0:T(8,128)(2,1)} %param.13), channel_id=1, source_target_pairs={{0,64},{4,68},{8,72},{12,76},{16,80},{20,84},{24,88},{28,92},{32,9... | collective-permute-start | bytes 49160 | tf_op jit(solution)/shard_map/ppermute | solution.py:559
  9.7 0.0 collective-permute-start.3
  9.7 3.4 %shard_map.137 = bf16[4,784,128]{2,1,0:T(8,128)(2,1)} custom-call(s32[1,4]{1,0:T(1,128)} %mask_ref.1, bf16[512,256]{1,0:T(8,128)(2,1)} %q_in.1, bf16[512,256]{1,0:T(8,128)(2,1)} %k_in.1, bf16[512,256]{1,0:T(8,128)(2,1)} %v_in.1), custom_call_target="tpu_custom_call" | custom-call | tf_op jit(solution)/shard_map/pallas_call | solution.py:113
  13.1 0.0 copy-start
  13.1 0.0 copy-start.5
  13.1 0.0 copy-start.2
  13.1 0.0 collective-permute-done.2
  13.1 0.0 collective-permute-done.1
  13.1 2.6 %collective-permute-done.3 = bf16[32,256]{1,0:T(8,128)(2,1)S(1)} collective-permute-done((bf16[32,256]{1,0:T(8,128)(2,1)}, bf16[32,256]{1,0:T(8,128)(2,1)S(1)}, u32[]{:S(2)}, u32[]{:S(2)}) %collective-permute-start.3) | collective-permute-done | bytes 16416 | tf_op jit(solution)/shard_map/ppermute | solution.py:559
  15.8 0.0 collective-permute-done.g2_in
  15.8 4.3 %all-to-all-start = ((bf16[4,784,128]{2,1,0:T(8,128)(2,1)}), bf16[4,784,128]{2,1,0:T(8,128)(2,1)S(1)}, u32[]{:S(2)}, u32[]{:S(2)}) async-start(bf16[4,784,128]{2,1,0:T(8,128)(2,1)} %shard_map.137), calls=%async_computation | async-start | bytes 1605632 | tf_op jit(solution)/shard_map/all_to_all | solution.py:549
  20.1 0.0 copy-done
  20.1 0.0 collective-permute-start.5
  20.1 0.5 collective-permute-start.6
  20.6 0.0 copy-done.5
  20.6 2.7 %collective-permute-start.9 = (bf16[128,256]{1,0:T(8,128)(2,1)S(1)}, bf16[128,256]{1,0:T(8,128)(2,1)S(1)}, u32[]{:S(2)}, u32[]{:S(2)}) collective-permute-start(bf16[128,256]{1,0:T(8,128)(2,1)S(1)} %constant_dynamic-update-slice_fusion.s0_in), channel_id=1, source_target_pairs={{0,48},{4,52},{8,56},{12,60},{16,32},{20,36},{24,40},{28,44},{32,1... | collective-permute-start | bytes 196616 | tf_op jit(solution)/shard_map/ppermute | solution.py:559
  23.3 1.0 collective-permute-start.8
  24.3 0.0 collective-permute-start.7
  24.4 0.0 collective-permute-done.5.g1_in
  24.4 2.2 %collective-permute-done.9.s3_in = bf16[128,256]{1,0:T(8,128)(2,1)S(1)} collective-permute-done((bf16[128,256]{1,0:T(8,128)(2,1)S(1)}, bf16[128,256]{1,0:T(8,128)(2,1)S(1)}, u32[]{:S(2)}, u32[]{:S(2)}) %collective-permute-start.9) | collective-permute-done | bytes 65568 | tf_op jit(solution)/shard_map/ppermute | solution.py:559
  26.5 1.3 %collective-permute-done.8.s2_in = bf16[128,256]{1,0:T(8,128)(2,1)S(1)} collective-permute-done((bf16[128,256]{1,0:T(8,128)(2,1)S(1)}, bf16[128,256]{1,0:T(8,128)(2,1)S(1)}, u32[]{:S(2)}, u32[]{:S(2)}) %collective-permute-start.8) | collective-permute-done | bytes 65568 | tf_op jit(solution)/shard_map/ppermute | solution.py:559
  27.9 0.8 collective-permute-done.7.s1_in
  28.6 0.0 collective-permute-done.6.g3_in
  28.6 0.0 copy-done.2
  28.6 2.0 %shard_map.138 = bf16[4,512,128]{2,1,0:T(8,128)(2,1)} custom-call(bf16[512,256]{1,0:T(8,128)(2,1)S(1)} %copy-done, bf16[512,256]{1,0:T(8,128)(2,1)S(1)} %collective-permute-done.5.g1_in, bf16[512,256]{1,0:T(8,128)(2,1)S(1)} %collective-permute-done.g2_in, bf16[512,256]{1,0:T(8,128)(2,1)S(1)} %collective-permute-done.6.g3_in, ...), custom_call_target="tpu_custom_call" | custom-call | tf_op jit(solution)/shard_map/pallas_call | solution.py:147
  30.6 0.0 all-to-all-done.row_in
  30.6 0.0 copy-start.3
  30.6 4.8 %all-to-all-start.1 = ((bf16[4,512,128]{2,1,0:T(8,128)(2,1)}), bf16[4,512,128]{2,1,0:T(8,128)(2,1)S(1)}, u32[]{:S(2)}, u32[]{:S(2)}) async-start(bf16[4,512,128]{2,1,0:T(8,128)(2,1)} %shard_map.138), calls=%async_computation.1 | async-start | bytes 1048576 | tf_op jit(solution)/shard_map/all_to_all | solution.py:549
  35.5 0.0 copy-done.3
  35.5 1.0 collective-permute-start.4
  36.5 7.2 %all-to-all-done.1.ga_in = bf16[4,512,128]{2,1,0:T(8,128)(2,1)S(1)} async-done(((bf16[4,512,128]{2,1,0:T(8,128)(2,1)}), bf16[4,512,128]{2,1,0:T(8,128)(2,1)S(1)}, u32[]{:S(2)}, u32[]{:S(2)}) %all-to-all-start.1) | async-done | bytes 524320 | tf_op jit(solution)/shard_map/all_to_all | solution.py:549
  43.7 0.0 copy-start.4
  43.7 3.5 %collective-permute-done.4.halo_in = bf16[3,512,128]{2,1,0:T(8,128)(2,1)S(1)} collective-permute-done((bf16[3,512,128]{2,1,0:T(8,128)(2,1)S(1)}, bf16[3,512,128]{2,1,0:T(8,128)(2,1)S(1)}, u32[]{:S(2)}, u32[]{:S(2)}) %collective-permute-start.4) | collective-permute-done | bytes 393248 | tf_op jit(solution)/shard_map/ppermute | solution.py:539
  47.2 0.0 copy-start.6
  47.2 0.0 copy-done.4
  47.2 0.7 copy-done.6
  48.0 28.3 %shard_map.139 = (bf16[4,768,128]{2,1,0:T(8,128)(2,1)}, f32[4,512,128]{2,1,0:T(8,128)}, bf16[3,512,128]{2,1,0:T(8,128)(2,1)}) custom-call(s32[64]{0:T(128)} %owner_ref.1, bf16[4,784,128]{2,1,0:T(8,128)(2,1)} %copy-done.3, bf16[3,512,128]{2,1,0:T(8,128)(2,1)} %copy-done.6, bf16[4,512,128]{2,1,0:T(8,128)(2,1)} %copy-done.4, f32[1,256]{1,0:T(1,128)} %bitcast.4, ...), custom_call_target="tpu_custom_call" | custom-call | flops 40000000000 | bytes 8000000 | tf_op jit(solution)/shard_map/pallas_call | solution.py:378
  76.2 0.0 copy-start.1
  76.2 4.7 %all-to-all-start.2 = ((bf16[4,768,128]{2,1,0:T(8,128)(2,1)}), bf16[4,768,128]{2,1,0:T(8,128)(2,1)S(1)}, u32[]{:S(2)}, u32[]{:S(2)}) async-start(bf16[4,768,128]{2,1,0:T(8,128)(2,1)} %get-tuple-element.27), calls=%async_computation.2 | async-start | bytes 1572864 | tf_op jit(solution)/shard_map/all_to_all | solution.py:549
  80.9 0.0 collective-permute-start.10
  80.9 8.1 %collective-permute-done.10.far_in = bf16[3,512,128]{2,1,0:T(8,128)(2,1)S(1)} collective-permute-done((bf16[3,512,128]{2,1,0:T(8,128)(2,1)}, bf16[3,512,128]{2,1,0:T(8,128)(2,1)S(1)}, u32[]{:S(2)}, u32[]{:S(2)}) %collective-permute-start.10) | collective-permute-done | bytes 393248 | tf_op jit(solution)/shard_map/ppermute | solution.py:539
  89.0 1.5 %all-to-all-done.2.att_in.near_in = bf16[4,768,128]{2,1,0:T(8,128)(2,1)S(1)} async-done(((bf16[4,768,128]{2,1,0:T(8,128)(2,1)}), bf16[4,768,128]{2,1,0:T(8,128)(2,1)S(1)}, u32[]{:S(2)}, u32[]{:S(2)}) %all-to-all-start.2) | async-done | bytes 786464 | tf_op jit(solution)/shard_map/all_to_all | solution.py:549
  90.5 0.0 copy-done.1
  90.5 2.1 %shard_map.140 = bf16[4,1024,128]{2,1,0:T(8,128)(2,1)} custom-call(bf16[4,768,128]{2,1,0:T(8,128)(2,1)S(1)} %all-to-all-done.2.att_in.near_in, bf16[512,256]{1,0:T(8,128)(2,1)S(1)} %copy-done, bf16[512,256]{1,0:T(8,128)(2,1)S(1)} %collective-permute-done.5.g1_in, bf16[512,256]{1,0:T(8,128)(2,1)S(1)} %collective-permute-done.g2_in, ...), custom_call_target="tpu_custom_call" | custom-call | tf_op jit(solution)/shard_map/pallas_call | solution.py:443
  92.6 14.7 %all_to_all.25.row_in = bf16[4,1024,128]{2,1,0:T(8,128)(2,1)S(1)} all-to-all(bf16[4,1024,128]{2,1,0:T(8,128)(2,1)} %shard_map.140), channel_id=1, replica_groups={{0,4,8,12},{16,20,24,28},{32,36,40,44},{48,52,56,60},{64,68,72,76},{80,..., dimensions={0} | all-to-all | bytes 2097152 | tf_op jit(solution)/shard_map/all_to_all | solution.py:549
  107.3 1.0 shard_map.142
  108.3 5.0 %all-to-all-start.4 = ((bf16[16,48,256]{2,1,0:T(8,128)(2,1)}), bf16[16,48,256]{2,1,0:T(8,128)(2,1)S(1)}, u32[]{:S(2)}, u32[]{:S(2)}) async-start(bf16[16,48,256]{2,1,0:T(8,128)(2,1)} %shard_map.142), calls=%async_computation.4 | async-start | bytes 786432 | tf_op jit(solution)/shard_map/all_to_all | solution.py:555
  113.3 1.2 shard_map.141
  114.5 10.7 %all-to-all-done.4.parts_in = bf16[16,48,256]{2,1,0:T(8,128)(2,1)S(1)} async-done(((bf16[16,48,256]{2,1,0:T(8,128)(2,1)}), bf16[16,48,256]{2,1,0:T(8,128)(2,1)S(1)}, u32[]{:S(2)}, u32[]{:S(2)}) %all-to-all-start.4) | async-done | bytes 393248 | tf_op jit(solution)/shard_map/all_to_all | solution.py:555
  125.2 0.8 shard_map.143
  (5 shorter events, 0.0 us)
Async XLA Ops:
  0.6 15.1 %collective-permute-start = (bf16[512,256]{1,0:T(8,128)(2,1)}, bf16[512,256]{1,0:T(8,128)(2,1)S(1)}, u32[]{:S(2)}, u32[]{:S(2)}) collective-permute-start(bf16[512,256]{1,0:T(8,128)(2,1)} %g0_in.3), channel_id=1, source_target_pairs={{0,2},{1,3},{2,0},{3,1},{4,6},{5,7},{6,4},{7,5},{8,10},{9,11},{10,... | collective-permute-start | bytes 786440 | tf_op jit(solution)/shard_map/ppermute | solution.py:543
  2.8 10.3 %collective-permute-start.2 = (bf16[32,256]{1,0:T(8,128)(2,1)}, bf16[32,256]{1,0:T(8,128)(2,1)S(1)}, u32[]{:S(2)}, u32[]{:S(2)}) collective-permute-start(bf16[32,256]{1,0:T(8,128)(2,1)} %param.13), channel_id=1, source_target_pairs={{0,128},{4,132},{8,136},{12,140},{16,144},{20,148},{24,152},{28,15... | collective-permute-start | bytes 49160 | tf_op jit(solution)/shard_map/ppermute | solution.py:559
  8.2 4.9 %collective-permute-start.1 = (bf16[32,256]{1,0:T(8,128)(2,1)}, bf16[32,256]{1,0:T(8,128)(2,1)S(1)}, u32[]{:S(2)}, u32[]{:S(2)}) collective-permute-start(bf16[32,256]{1,0:T(8,128)(2,1)} %param.13), channel_id=1, source_target_pairs={{0,64},{4,68},{8,72},{12,76},{16,80},{20,84},{24,88},{28,92},{32,9... | collective-permute-start | bytes 49160 | tf_op jit(solution)/shard_map/ppermute | solution.py:559
  9.7 6.1 %collective-permute-start.3 = (bf16[32,256]{1,0:T(8,128)(2,1)}, bf16[32,256]{1,0:T(8,128)(2,1)S(1)}, u32[]{:S(2)}, u32[]{:S(2)}) collective-permute-start(bf16[32,256]{1,0:T(8,128)(2,1)} %param.13), channel_id=1, source_target_pairs={{0,192},{4,196},{8,200},{12,204},{16,208},{20,212},{24,216},{28,22... | collective-permute-start | bytes 49160 | tf_op jit(solution)/shard_map/ppermute | solution.py:559
  13.1 7.0 %copy-start = (bf16[512,256]{1,0:T(8,128)(2,1)S(1)}, bf16[512,256]{1,0:T(8,128)(2,1)}, u32[]{:S(2)}) copy-start(bf16[512,256]{1,0:T(8,128)(2,1)} %g0_in.3) | copy-start | bytes 786436
  13.1 7.5 %copy-start.5 = (bf16[32,256]{1,0:T(8,128)(2,1)S(1)}, bf16[32,256]{1,0:T(8,128)(2,1)}, u32[]{:S(2)}) copy-start(bf16[32,256]{1,0:T(8,128)(2,1)} %param.13) | copy-start | bytes 49156
  13.1 15.5 %copy-start.2 = (bf16[256,1024]{1,0:T(8,128)(2,1)S(1)}, bf16[256,1024]{1,0:T(8,128)(2,1)}, u32[]{:S(2)}) copy-start(bf16[256,1024]{1,0:T(8,128)(2,1)} %weight_in.1) | copy-start | bytes 1572868
  15.8 14.8 %all-to-all-start = ((bf16[4,784,128]{2,1,0:T(8,128)(2,1)}), bf16[4,784,128]{2,1,0:T(8,128)(2,1)S(1)}, u32[]{:S(2)}, u32[]{:S(2)}) async-start(bf16[4,784,128]{2,1,0:T(8,128)(2,1)} %shard_map.137), calls=%async_computation | async-start | bytes 1605632 | tf_op jit(solution)/shard_map/all_to_all | solution.py:549
  20.1 4.3 %collective-permute-start.5 = (bf16[512,256]{1,0:T(8,128)(2,1)S(1)}, bf16[512,256]{1,0:T(8,128)(2,1)S(1)}, u32[]{:S(2)}, u32[]{:S(2)}) collective-permute-start(bf16[512,256]{1,0:T(8,128)(2,1)S(1)} %copy-done), channel_id=1, source_target_pairs={{0,1},{1,0},{2,3},{3,2},{4,5},{5,4},{6,7},{7,6},{8,9},{9,8},{10,11... | collective-permute-start | bytes 786440 | tf_op jit(solution)/shard_map/ppermute | solution.py:543
  20.1 8.5 %collective-permute-start.6 = (bf16[512,256]{1,0:T(8,128)(2,1)S(1)}, bf16[512,256]{1,0:T(8,128)(2,1)S(1)}, u32[]{:S(2)}, u32[]{:S(2)}) collective-permute-start(bf16[512,256]{1,0:T(8,128)(2,1)S(1)} %collective-permute-done.g2_in), channel_id=1, source_target_pairs={{0,1},{1,0},{2,3},{3,2},{4,5},{5,4},{6,7},{7,6},{8,9},{9,8},{10,11... | collective-permute-start | bytes 786440 | tf_op jit(solution)/shard_map/ppermute | solution.py:543
  20.6 5.9 %collective-permute-start.9 = (bf16[128,256]{1,0:T(8,128)(2,1)S(1)}, bf16[128,256]{1,0:T(8,128)(2,1)S(1)}, u32[]{:S(2)}, u32[]{:S(2)}) collective-permute-start(bf16[128,256]{1,0:T(8,128)(2,1)S(1)} %constant_dynamic-update-slice_fusion.s0_in), channel_id=1, source_target_pairs={{0,48},{4,52},{8,56},{12,60},{16,32},{20,36},{24,40},{28,44},{32,1... | collective-permute-start | bytes 196616 | tf_op jit(solution)/shard_map/ppermute | solution.py:559
  23.3 4.5 %collective-permute-start.8 = (bf16[128,256]{1,0:T(8,128)(2,1)S(1)}, bf16[128,256]{1,0:T(8,128)(2,1)S(1)}, u32[]{:S(2)}, u32[]{:S(2)}) collective-permute-start(bf16[128,256]{1,0:T(8,128)(2,1)S(1)} %constant_dynamic-update-slice_fusion.s0_in), channel_id=1, source_target_pairs={{0,32},{4,36},{8,40},{12,44},{16,48},{20,52},{24,56},{28,60},{32,0... | collective-permute-start | bytes 196616 | tf_op jit(solution)/shard_map/ppermute | solution.py:559
  24.3 4.3 %collective-permute-start.7 = (bf16[128,256]{1,0:T(8,128)(2,1)S(1)}, bf16[128,256]{1,0:T(8,128)(2,1)S(1)}, u32[]{:S(2)}, u32[]{:S(2)}) collective-permute-start(bf16[128,256]{1,0:T(8,128)(2,1)S(1)} %constant_dynamic-update-slice_fusion.s0_in), channel_id=1, source_target_pairs={{0,16},{4,20},{8,24},{12,28},{16,0},{20,4},{24,8},{28,12},{32,48},... | collective-permute-start | bytes 196616 | tf_op jit(solution)/shard_map/ppermute | solution.py:559
  30.6 4.9 %copy-start.3 = (bf16[4,784,128]{2,1,0:T(8,128)(2,1)}, bf16[4,784,128]{2,1,0:T(8,128)(2,1)S(1)}, u32[]{:S(2)}) copy-start(bf16[4,784,128]{2,1,0:T(8,128)(2,1)S(1)} %all-to-all-done.row_in) | copy-start | bytes 2408452
  30.6 13.1 %all-to-all-start.1 = ((bf16[4,512,128]{2,1,0:T(8,128)(2,1)}), bf16[4,512,128]{2,1,0:T(8,128)(2,1)S(1)}, u32[]{:S(2)}, u32[]{:S(2)}) async-start(bf16[4,512,128]{2,1,0:T(8,128)(2,1)} %shard_map.138), calls=%async_computation.1 | async-start | bytes 1048576 | tf_op jit(solution)/shard_map/all_to_all | solution.py:549
  35.5 11.8 %collective-permute-start.4 = (bf16[3,512,128]{2,1,0:T(8,128)(2,1)S(1)}, bf16[3,512,128]{2,1,0:T(8,128)(2,1)S(1)}, u32[]{:S(2)}, u32[]{:S(2)}) collective-permute-start(bf16[3,512,128]{2,1,0:T(8,128)(2,1)S(1)} %slice.4), channel_id=1, source_target_pairs={{0,16},{4,20},{8,24},{12,28},{16,32},{20,36},{24,40},{28,44},{32,4... | collective-permute-start | bytes 1179656 | tf_op jit(solution)/shard_map/ppermute | solution.py:539
  43.7 3.5 %copy-start.4 = (bf16[4,512,128]{2,1,0:T(8,128)(2,1)}, bf16[4,512,128]{2,1,0:T(8,128)(2,1)S(1)}, u32[]{:S(2)}) copy-start(bf16[4,512,128]{2,1,0:T(8,128)(2,1)S(1)} %all-to-all-done.1.ga_in) | copy-start | bytes 1572868
  47.2 0.7 copy-start.6
  76.2 14.3 %copy-start.1 = (f32[4,512,128]{2,1,0:T(8,128)S(1)}, f32[4,512,128]{2,1,0:T(8,128)}, u32[]{:S(2)}) copy-start(f32[4,512,128]{2,1,0:T(8,128)} %get-tuple-element.30.own_in) | copy-start | bytes 3145732
  76.2 14.3 %all-to-all-start.2 = ((bf16[4,768,128]{2,1,0:T(8,128)(2,1)}), bf16[4,768,128]{2,1,0:T(8,128)(2,1)S(1)}, u32[]{:S(2)}, u32[]{:S(2)}) async-start(bf16[4,768,128]{2,1,0:T(8,128)(2,1)} %get-tuple-element.27), calls=%async_computation.2 | async-start | bytes 1572864 | tf_op jit(solution)/shard_map/all_to_all | solution.py:549
  80.9 8.1 %collective-permute-start.10 = (bf16[3,512,128]{2,1,0:T(8,128)(2,1)}, bf16[3,512,128]{2,1,0:T(8,128)(2,1)S(1)}, u32[]{:S(2)}, u32[]{:S(2)}) collective-permute-start(bf16[3,512,128]{2,1,0:T(8,128)(2,1)} %get-tuple-element.28), channel_id=1, source_target_pairs={{0,240},{4,244},{8,248},{12,252},{16,0},{20,4},{24,8},{28,12},{32,... | collective-permute-start | bytes 1179656 | tf_op jit(solution)/shard_map/ppermute | solution.py:539
  108.3 16.9 %all-to-all-start.4 = ((bf16[16,48,256]{2,1,0:T(8,128)(2,1)}), bf16[16,48,256]{2,1,0:T(8,128)(2,1)S(1)}, u32[]{:S(2)}, u32[]{:S(2)}) async-start(bf16[16,48,256]{2,1,0:T(8,128)(2,1)} %shard_map.142), calls=%async_computation.4 | async-start | bytes 786432 | tf_op jit(solution)/shard_map/all_to_all | solution.py:555

commit v6 on v5

--- a/solution.py
+++ b/solution.py
@@ -569,7 +569,7 @@
     across = swapped(d_layer, 2)
     far_pos = [pos_store] + [masked(pos_store, ROW * 4 * j) for j in range(1, 4)]
     packed = pack_call(block_mask, query, key, value)
-    packed, across, *far_pos = lax.optimization_barrier((packed, across, *far_pos))
+    packed, across = lax.optimization_barrier((packed, across))
     far_pos = jnp.concatenate(far_pos, axis=0)
     slots = [far_pos] + [masked(far_pos, ROW * j) for j in range(1, 4)]
     row = in_row(packed)

time: 127 us -> 131 us (1.031)
  waiting for transfers between devices: 37.9 us -> 42.9 us
    ppermute x3, waiting for transfers between devices: 0.01 us -> 4.3 us  [swapped(): lax.ppermute(block, 'head', [(i, i ^ bit) for i in range(lax.axis_size('h...]
    ppermute x6, waiting for transfers between devices: 6.9 us -> 9.32 us  [masked(): lax.ppermute(block, 'ctx', [(i, i ^ mask) for i in range(lax.axis_size('c...]
    ppermute x2, waiting for transfers between devices: 11.6 us -> 10.1 us  [shifted(): lax.ppermute(block, 'ctx', [(i, (i + distance) % count) for i in range(co...]
    ppermute x6, starting transfers between devices: 10.7 us -> 12.2 us  [masked(): lax.ppermute(block, 'ctx', [(i, i ^ mask) for i in range(lax.axis_size('c...]
    all_to_all x1, starting transfers between devices: 5.01 us -> 3.56 us  [in_column(): return lax.all_to_all(block, 'ctx', 0, 0, axis_index_groups=groups)]
  transfers between devices with their start and end apart: 15 -> 15, of which waited for: 9 -> 11; matrix products, arithmetic and copies ran while one was open for 0% -> 0% of each run, Pallas kernels for 5% -> 5%
where the time goes in v6:
time: 131 us
  waiting for transfers between devices  42.9 us (33%)
  Pallas kernels  38.7 us (30%)
  starting transfers between devices  32.9 us (25%)
  blocking collectives  14.4 us (11%)
    pallas_call x1, Pallas kernels, core_call(): pl.pallas_call(core_kernel, grid=(ROW,), in_specs=smem_specs(1) + any_spe...  28.3 us
    all_to_all x1, blocking collectives, in_row(): return lax.all_to_all(block, 'ctx', 0, 0, axis_index_groups=groups)  14.4 us
    all_to_all x3, starting transfers between devices, in_row(): return lax.all_to_all(block, 'ctx', 0, 0, axis_index_groups=groups)  14 us
    ppermute x6, starting transfers between devices, masked(): lax.ppermute(block, 'ctx', [(i, i ^ mask) for i in range(lax.axis_size('c...  12.2 us
    all_to_all x1, waiting for transfers between devices, in_column(): return lax.all_to_all(block, 'ctx', 0, 0, axis_index_groups=groups)  10.7 us
    ppermute x2, waiting for transfers between devices, shifted(): lax.ppermute(block, 'ctx', [(i, (i + distance) % count) for i in range(co...  10.1 us
    ppermute x6, waiting for transfers between devices, masked(): lax.ppermute(block, 'ctx', [(i, i ^ mask) for i in range(lax.axis_size('c...  9.32 us
    all_to_all x3, waiting for transfers between devices, in_row(): return lax.all_to_all(block, 'ctx', 0, 0, axis_index_groups=groups)  8.54 us
  transfers between devices with their start and end apart: 15, of which 11 were waited for; matrix products, arithmetic and copies ran while one was open for 0% of the time, Pallas kernels for 5%

profile of v6, /device:TPU:16, one launch (start us, length us, event | category | flops | bytes accessed | tf_op | source)
XLA Modules:
  0.0 130.7 jit_solution(1589908795475362960)
XLA Ops:
  0.6 2.2 %collective-permute-start = (bf16[512,256]{1,0:T(8,128)(2,1)}, bf16[512,256]{1,0:T(8,128)(2,1)S(1)}, u32[]{:S(2)}, u32[]{:S(2)}) collective-permute-start(bf16[512,256]{1,0:T(8,128)(2,1)} %g0_in.3), channel_id=1, source_target_pairs={{0,2},{1,3},{2,0},{3,1},{4,6},{5,7},{6,4},{7,5},{8,10},{9,11},{10,... | collective-permute-start | bytes 786440 | tf_op jit(solution)/shard_map/ppermute | solution.py:543
  2.8 3.4 %shard_map.137 = bf16[4,784,128]{2,1,0:T(8,128)(2,1)} custom-call(s32[1,4]{1,0:T(1,128)} %mask_ref.1, bf16[512,256]{1,0:T(8,128)(2,1)} %q_in.1, bf16[512,256]{1,0:T(8,128)(2,1)} %k_in.1, bf16[512,256]{1,0:T(8,128)(2,1)} %v_in.1), custom_call_target="tpu_custom_call" | custom-call | tf_op jit(solution)/shard_map/pallas_call | solution.py:113
  6.2 0.0 copy-start.5
  6.2 0.0 copy-start
  6.2 0.0 copy-start.2
  6.2 4.3 %collective-permute-done.g2_in = bf16[512,256]{1,0:T(8,128)(2,1)S(1)} collective-permute-done((bf16[512,256]{1,0:T(8,128)(2,1)}, bf16[512,256]{1,0:T(8,128)(2,1)S(1)}, u32[]{:S(2)}, u32[]{:S(2)}) %collective-permute-start) | collective-permute-done | bytes 262176 | tf_op jit(solution)/shard_map/ppermute | solution.py:543
  10.5 4.3 %all-to-all-start = ((bf16[4,784,128]{2,1,0:T(8,128)(2,1)}), bf16[4,784,128]{2,1,0:T(8,128)(2,1)S(1)}, u32[]{:S(2)}, u32[]{:S(2)}) async-start(bf16[4,784,128]{2,1,0:T(8,128)(2,1)} %shard_map.137), calls=%async_computation | async-start | bytes 1605632 | tf_op jit(solution)/shard_map/all_to_all | solution.py:549
  14.8 0.0 copy-done.5
  14.8 7.2 %collective-permute-start.5 = (bf16[32,256]{1,0:T(8,128)(2,1)S(1)}, bf16[32,256]{1,0:T(8,128)(2,1)S(1)}, u32[]{:S(2)}, u32[]{:S(2)}) collective-permute-start(bf16[32,256]{1,0:T(8,128)(2,1)S(1)} %copy-done.5), channel_id=1, source_target_pairs={{0,128},{4,132},{8,136},{12,140},{16,144},{20,148},{24,152},{28,15... | collective-permute-start | bytes 49160 | tf_op jit(solution)/shard_map/ppermute | solution.py:559
  22.0 1.5 %collective-permute-start.4 = (bf16[32,256]{1,0:T(8,128)(2,1)S(1)}, bf16[32,256]{1,0:T(8,128)(2,1)S(1)}, u32[]{:S(2)}, u32[]{:S(2)}) collective-permute-start(bf16[32,256]{1,0:T(8,128)(2,1)S(1)} %copy-done.5), channel_id=1, source_target_pairs={{0,64},{4,68},{8,72},{12,76},{16,80},{20,84},{24,88},{28,92},{32,9... | collective-permute-start | bytes 49160 | tf_op jit(solution)/shard_map/ppermute | solution.py:559
  23.4 0.0 collective-permute-start.6
  23.4 0.0 copy-done
  23.4 0.0 collective-permute-start.2
  23.5 3.1 %collective-permute-done.4 = bf16[32,256]{1,0:T(8,128)(2,1)S(1)} collective-permute-done((bf16[32,256]{1,0:T(8,128)(2,1)S(1)}, bf16[32,256]{1,0:T(8,128)(2,1)S(1)}, u32[]{:S(2)}, u32[]{:S(2)}) %collective-permute-start.4) | collective-permute-done | bytes 16416 | tf_op jit(solution)/shard_map/ppermute | solution.py:559
  26.6 0.0 collective-permute-start.3
  26.6 0.0 collective-permute-done.5
  26.6 2.7 %collective-permute-done.6 = bf16[32,256]{1,0:T(8,128)(2,1)S(1)} collective-permute-done((bf16[32,256]{1,0:T(8,128)(2,1)S(1)}, bf16[32,256]{1,0:T(8,128)(2,1)S(1)}, u32[]{:S(2)}, u32[]{:S(2)}) %collective-permute-start.6) | collective-permute-done | bytes 16416 | tf_op jit(solution)/shard_map/ppermute | solution.py:559
  29.3 1.7 %collective-permute-start.9 = (bf16[128,256]{1,0:T(8,128)(2,1)S(1)}, bf16[128,256]{1,0:T(8,128)(2,1)S(1)}, u32[]{:S(2)}, u32[]{:S(2)}) collective-permute-start(bf16[128,256]{1,0:T(8,128)(2,1)S(1)} %constant_dynamic-update-slice_fusion.s0_in), channel_id=1, source_target_pairs={{0,48},{4,52},{8,56},{12,60},{16,32},{20,36},{24,40},{28,44},{32,1... | collective-permute-start | bytes 196616 | tf_op jit(solution)/shard_map/ppermute | solution.py:559
  31.0 1.0 collective-permute-start.8
  32.0 0.7 collective-permute-start.7
  32.8 1.7 %collective-permute-done.9.s3_in = bf16[128,256]{1,0:T(8,128)(2,1)S(1)} collective-permute-done((bf16[128,256]{1,0:T(8,128)(2,1)S(1)}, bf16[128,256]{1,0:T(8,128)(2,1)S(1)}, u32[]{:S(2)}, u32[]{:S(2)}) %collective-permute-start.9) | collective-permute-done | bytes 65568 | tf_op jit(solution)/shard_map/ppermute | solution.py:559
  34.5 0.8 collective-permute-done.8.s2_in
  35.3 1.0 collective-permute-done.7.s1_in
  36.3 0.0 collective-permute-done.2.g1_in
  36.3 0.0 collective-permute-done.3.g3_in
  36.3 0.0 copy-done.2
  36.3 2.0 %shard_map.138 = bf16[4,512,128]{2,1,0:T(8,128)(2,1)} custom-call(bf16[512,256]{1,0:T(8,128)(2,1)S(1)} %copy-done, bf16[512,256]{1,0:T(8,128)(2,1)S(1)} %collective-permute-done.2.g1_in, bf16[512,256]{1,0:T(8,128)(2,1)S(1)} %collective-permute-done.g2_in, bf16[512,256]{1,0:T(8,128)(2,1)S(1)} %collective-permute-done.3.g3_in, ...), custom_call_target="tpu_custom_call" | custom-call | tf_op jit(solution)/shard_map/pallas_call | solution.py:147
  38.3 0.0 all-to-all-done.row_in
  38.3 0.0 copy-start.3
  38.3 4.8 %all-to-all-start.1 = ((bf16[4,512,128]{2,1,0:T(8,128)(2,1)}), bf16[4,512,128]{2,1,0:T(8,128)(2,1)S(1)}, u32[]{:S(2)}, u32[]{:S(2)}) async-start(bf16[4,512,128]{2,1,0:T(8,128)(2,1)} %shard_map.138), calls=%async_computation.1 | async-start | bytes 1048576 | tf_op jit(solution)/shard_map/all_to_all | solution.py:549
  43.2 0.0 copy-done.3
  43.2 1.0 collective-permute-start.1
  44.2 7.0 %all-to-all-done.1.ga_in = bf16[4,512,128]{2,1,0:T(8,128)(2,1)S(1)} async-done(((bf16[4,512,128]{2,1,0:T(8,128)(2,1)}), bf16[4,512,128]{2,1,0:T(8,128)(2,1)S(1)}, u32[]{:S(2)}, u32[]{:S(2)}) %all-to-all-start.1) | async-done | bytes 524320 | tf_op jit(solution)/shard_map/all_to_all | solution.py:549
  51.2 0.0 copy-start.4
  51.2 2.1 %collective-permute-done.1.halo_in = bf16[3,512,128]{2,1,0:T(8,128)(2,1)S(1)} collective-permute-done((bf16[3,512,128]{2,1,0:T(8,128)(2,1)S(1)}, bf16[3,512,128]{2,1,0:T(8,128)(2,1)S(1)}, u32[]{:S(2)}, u32[]{:S(2)}) %collective-permute-start.1) | collective-permute-done | bytes 393248 | tf_op jit(solution)/shard_map/ppermute | solution.py:539
  53.3 0.0 copy-start.6
  53.3 0.0 copy-done.4
  53.3 0.7 copy-done.6
  54.0 28.3 %shard_map.139 = (bf16[4,768,128]{2,1,0:T(8,128)(2,1)}, f32[4,512,128]{2,1,0:T(8,128)}, bf16[3,512,128]{2,1,0:T(8,128)(2,1)}) custom-call(s32[64]{0:T(128)} %owner_ref.1, bf16[4,784,128]{2,1,0:T(8,128)(2,1)} %copy-done.3, bf16[3,512,128]{2,1,0:T(8,128)(2,1)} %copy-done.6, bf16[4,512,128]{2,1,0:T(8,128)(2,1)} %copy-done.4, f32[1,256]{1,0:T(1,128)} %bitcast.4, ...), custom_call_target="tpu_custom_call" | custom-call | flops 40000000000 | bytes 8000000 | tf_op jit(solution)/shard_map/pallas_call | solution.py:378
  82.3 0.0 copy-start.1
  82.3 4.9 %all-to-all-start.2 = ((bf16[4,768,128]{2,1,0:T(8,128)(2,1)}), bf16[4,768,128]{2,1,0:T(8,128)(2,1)S(1)}, u32[]{:S(2)}, u32[]{:S(2)}) async-start(bf16[4,768,128]{2,1,0:T(8,128)(2,1)} %get-tuple-element.19), calls=%async_computation.2 | async-start | bytes 1572864 | tf_op jit(solution)/shard_map/all_to_all | solution.py:549
  87.3 0.0 collective-permute-start.10
  87.3 8.0 %collective-permute-done.10.far_in = bf16[3,512,128]{2,1,0:T(8,128)(2,1)S(1)} collective-permute-done((bf16[3,512,128]{2,1,0:T(8,128)(2,1)}, bf16[3,512,128]{2,1,0:T(8,128)(2,1)S(1)}, u32[]{:S(2)}, u32[]{:S(2)}) %collective-permute-start.10) | collective-permute-done | bytes 393248 | tf_op jit(solution)/shard_map/ppermute | solution.py:539
  95.3 1.5 %all-to-all-done.2.att_in.near_in = bf16[4,768,128]{2,1,0:T(8,128)(2,1)S(1)} async-done(((bf16[4,768,128]{2,1,0:T(8,128)(2,1)}), bf16[4,768,128]{2,1,0:T(8,128)(2,1)S(1)}, u32[]{:S(2)}, u32[]{:S(2)}) %all-to-all-start.2) | async-done | bytes 786464 | tf_op jit(solution)/shard_map/all_to_all | solution.py:549
  96.8 0.0 copy-done.1
  96.8 2.1 %shard_map.140 = bf16[4,1024,128]{2,1,0:T(8,128)(2,1)} custom-call(bf16[4,768,128]{2,1,0:T(8,128)(2,1)S(1)} %all-to-all-done.2.att_in.near_in, bf16[512,256]{1,0:T(8,128)(2,1)S(1)} %copy-done, bf16[512,256]{1,0:T(8,128)(2,1)S(1)} %collective-permute-done.2.g1_in, bf16[512,256]{1,0:T(8,128)(2,1)S(1)} %collective-permute-done.g2_in, ...), custom_call_target="tpu_custom_call" | custom-call | tf_op jit(solution)/shard_map/pallas_call | solution.py:443
  98.8 14.4 %all_to_all.25.row_in = bf16[4,1024,128]{2,1,0:T(8,128)(2,1)S(1)} all-to-all(bf16[4,1024,128]{2,1,0:T(8,128)(2,1)} %shard_map.140), channel_id=1, replica_groups={{0,4,8,12},{16,20,24,28},{32,36,40,44},{48,52,56,60},{64,68,72,76},{80,..., dimensions={0} | all-to-all | bytes 2097152 | tf_op jit(solution)/shard_map/all_to_all | solution.py:549
  113.2 1.0 shard_map.142
  114.3 3.6 %all-to-all-start.4 = ((bf16[16,48,256]{2,1,0:T(8,128)(2,1)}), bf16[16,48,256]{2,1,0:T(8,128)(2,1)S(1)}, u32[]{:S(2)}, u32[]{:S(2)}) async-start(bf16[16,48,256]{2,1,0:T(8,128)(2,1)} %shard_map.142), calls=%async_computation.4 | async-start | bytes 786432 | tf_op jit(solution)/shard_map/all_to_all | solution.py:555
  117.8 1.2 shard_map.141
  119.0 10.7 %all-to-all-done.4.parts_in = bf16[16,48,256]{2,1,0:T(8,128)(2,1)S(1)} async-done(((bf16[16,48,256]{2,1,0:T(8,128)(2,1)}), bf16[16,48,256]{2,1,0:T(8,128)(2,1)S(1)}, u32[]{:S(2)}, u32[]{:S(2)}) %all-to-all-start.4) | async-done | bytes 393248 | tf_op jit(solution)/shard_map/all_to_all | solution.py:555
  129.7 0.8 shard_map.143
  (5 shorter events, 0.0 us)
Async XLA Ops:
  0.6 9.8 %collective-permute-start = (bf16[512,256]{1,0:T(8,128)(2,1)}, bf16[512,256]{1,0:T(8,128)(2,1)S(1)}, u32[]{:S(2)}, u32[]{:S(2)}) collective-permute-start(bf16[512,256]{1,0:T(8,128)(2,1)} %g0_in.3), channel_id=1, source_target_pairs={{0,2},{1,3},{2,0},{3,1},{4,6},{5,7},{6,4},{7,5},{8,10},{9,11},{10,... | collective-permute-start | bytes 786440 | tf_op jit(solution)/shard_map/ppermute | solution.py:543
  6.2 8.6 %copy-start.5 = (bf16[32,256]{1,0:T(8,128)(2,1)S(1)}, bf16[32,256]{1,0:T(8,128)(2,1)}, u32[]{:S(2)}) copy-start(bf16[32,256]{1,0:T(8,128)(2,1)} %param.13) | copy-start | bytes 49156
  6.2 17.3 %copy-start = (bf16[512,256]{1,0:T(8,128)(2,1)S(1)}, bf16[512,256]{1,0:T(8,128)(2,1)}, u32[]{:S(2)}) copy-start(bf16[512,256]{1,0:T(8,128)(2,1)} %g0_in.3) | copy-start | bytes 786436
  6.2 30.1 %copy-start.2 = (bf16[256,1024]{1,0:T(8,128)(2,1)S(1)}, bf16[256,1024]{1,0:T(8,128)(2,1)}, u32[]{:S(2)}) copy-start(bf16[256,1024]{1,0:T(8,128)(2,1)} %weight_in.1) | copy-start | bytes 1572868
  10.5 27.8 %all-to-all-start = ((bf16[4,784,128]{2,1,0:T(8,128)(2,1)}), bf16[4,784,128]{2,1,0:T(8,128)(2,1)S(1)}, u32[]{:S(2)}, u32[]{:S(2)}) async-start(bf16[4,784,128]{2,1,0:T(8,128)(2,1)} %shard_map.137), calls=%async_computation | async-start | bytes 1605632 | tf_op jit(solution)/shard_map/all_to_all | solution.py:549
  14.8 11.8 %collective-permute-start.5 = (bf16[32,256]{1,0:T(8,128)(2,1)S(1)}, bf16[32,256]{1,0:T(8,128)(2,1)S(1)}, u32[]{:S(2)}, u32[]{:S(2)}) collective-permute-start(bf16[32,256]{1,0:T(8,128)(2,1)S(1)} %copy-done.5), channel_id=1, source_target_pairs={{0,128},{4,132},{8,136},{12,140},{16,144},{20,148},{24,152},{28,15... | collective-permute-start | bytes 49160 | tf_op jit(solution)/shard_map/ppermute | solution.py:559
  22.0 4.6 %collective-permute-start.4 = (bf16[32,256]{1,0:T(8,128)(2,1)S(1)}, bf16[32,256]{1,0:T(8,128)(2,1)S(1)}, u32[]{:S(2)}, u32[]{:S(2)}) collective-permute-start(bf16[32,256]{1,0:T(8,128)(2,1)S(1)} %copy-done.5), channel_id=1, source_target_pairs={{0,64},{4,68},{8,72},{12,76},{16,80},{20,84},{24,88},{28,92},{32,9... | collective-permute-start | bytes 49160 | tf_op jit(solution)/shard_map/ppermute | solution.py:559
  23.4 5.8 %collective-permute-start.6 = (bf16[32,256]{1,0:T(8,128)(2,1)S(1)}, bf16[32,256]{1,0:T(8,128)(2,1)S(1)}, u32[]{:S(2)}, u32[]{:S(2)}) collective-permute-start(bf16[32,256]{1,0:T(8,128)(2,1)S(1)} %copy-done.5), channel_id=1, source_target_pairs={{0,192},{4,196},{8,200},{12,204},{16,208},{20,212},{24,216},{28,22... | collective-permute-start | bytes 49160 | tf_op jit(solution)/shard_map/ppermute | solution.py:559
  23.4 12.9 %collective-permute-start.2 = (bf16[512,256]{1,0:T(8,128)(2,1)S(1)}, bf16[512,256]{1,0:T(8,128)(2,1)S(1)}, u32[]{:S(2)}, u32[]{:S(2)}) collective-permute-start(bf16[512,256]{1,0:T(8,128)(2,1)S(1)} %copy-done), channel_id=1, source_target_pairs={{0,1},{1,0},{2,3},{3,2},{4,5},{5,4},{6,7},{7,6},{8,9},{9,8},{10,11... | collective-permute-start | bytes 786440 | tf_op jit(solution)/shard_map/ppermute | solution.py:543
  26.6 9.7 %collective-permute-start.3 = (bf16[512,256]{1,0:T(8,128)(2,1)S(1)}, bf16[512,256]{1,0:T(8,128)(2,1)S(1)}, u32[]{:S(2)}, u32[]{:S(2)}) collective-permute-start(bf16[512,256]{1,0:T(8,128)(2,1)S(1)} %collective-permute-done.g2_in), channel_id=1, source_target_pairs={{0,1},{1,0},{2,3},{3,2},{4,5},{5,4},{6,7},{7,6},{8,9},{9,8},{10,11... | collective-permute-start | bytes 786440 | tf_op jit(solution)/shard_map/ppermute | solution.py:543
  29.3 5.2 %collective-permute-start.9 = (bf16[128,256]{1,0:T(8,128)(2,1)S(1)}, bf16[128,256]{1,0:T(8,128)(2,1)S(1)}, u32[]{:S(2)}, u32[]{:S(2)}) collective-permute-start(bf16[128,256]{1,0:T(8,128)(2,1)S(1)} %constant_dynamic-update-slice_fusion.s0_in), channel_id=1, source_target_pairs={{0,48},{4,52},{8,56},{12,60},{16,32},{20,36},{24,40},{28,44},{32,1... | collective-permute-start | bytes 196616 | tf_op jit(solution)/shard_map/ppermute | solution.py:559
  31.0 4.3 %collective-permute-start.8 = (bf16[128,256]{1,0:T(8,128)(2,1)S(1)}, bf16[128,256]{1,0:T(8,128)(2,1)S(1)}, u32[]{:S(2)}, u32[]{:S(2)}) collective-permute-start(bf16[128,256]{1,0:T(8,128)(2,1)S(1)} %constant_dynamic-update-slice_fusion.s0_in), channel_id=1, source_target_pairs={{0,32},{4,36},{8,40},{12,44},{16,48},{20,52},{24,56},{28,60},{32,0... | collective-permute-start | bytes 196616 | tf_op jit(solution)/shard_map/ppermute | solution.py:559
  32.0 4.3 %collective-permute-start.7 = (bf16[128,256]{1,0:T(8,128)(2,1)S(1)}, bf16[128,256]{1,0:T(8,128)(2,1)S(1)}, u32[]{:S(2)}, u32[]{:S(2)}) collective-permute-start(bf16[128,256]{1,0:T(8,128)(2,1)S(1)} %constant_dynamic-update-slice_fusion.s0_in), channel_id=1, source_target_pairs={{0,16},{4,20},{8,24},{12,28},{16,0},{20,4},{24,8},{28,12},{32,48},... | collective-permute-start | bytes 196616 | tf_op jit(solution)/shard_map/ppermute | solution.py:559
  38.3 4.8 %copy-start.3 = (bf16[4,784,128]{2,1,0:T(8,128)(2,1)}, bf16[4,784,128]{2,1,0:T(8,128)(2,1)S(1)}, u32[]{:S(2)}) copy-start(bf16[4,784,128]{2,1,0:T(8,128)(2,1)S(1)} %all-to-all-done.row_in) | copy-start | bytes 2408452
  38.3 12.9 %all-to-all-start.1 = ((bf16[4,512,128]{2,1,0:T(8,128)(2,1)}), bf16[4,512,128]{2,1,0:T(8,128)(2,1)S(1)}, u32[]{:S(2)}, u32[]{:S(2)}) async-start(bf16[4,512,128]{2,1,0:T(8,128)(2,1)} %shard_map.138), calls=%async_computation.1 | async-start | bytes 1048576 | tf_op jit(solution)/shard_map/all_to_all | solution.py:549
  43.2 10.1 %collective-permute-start.1 = (bf16[3,512,128]{2,1,0:T(8,128)(2,1)S(1)}, bf16[3,512,128]{2,1,0:T(8,128)(2,1)S(1)}, u32[]{:S(2)}, u32[]{:S(2)}) collective-permute-start(bf16[3,512,128]{2,1,0:T(8,128)(2,1)S(1)} %slice.4), channel_id=1, source_target_pairs={{0,16},{4,20},{8,24},{12,28},{16,32},{20,36},{24,40},{28,44},{32,4... | collective-permute-start | bytes 1179656 | tf_op jit(solution)/shard_map/ppermute | solution.py:539
  51.2 2.1 %copy-start.4 = (bf16[4,512,128]{2,1,0:T(8,128)(2,1)}, bf16[4,512,128]{2,1,0:T(8,128)(2,1)S(1)}, u32[]{:S(2)}) copy-start(bf16[4,512,128]{2,1,0:T(8,128)(2,1)S(1)} %all-to-all-done.1.ga_in) | copy-start | bytes 1572868
  53.3 0.7 copy-start.6
  82.3 14.4 %copy-start.1 = (f32[4,512,128]{2,1,0:T(8,128)S(1)}, f32[4,512,128]{2,1,0:T(8,128)}, u32[]{:S(2)}) copy-start(f32[4,512,128]{2,1,0:T(8,128)} %get-tuple-element.22.own_in) | copy-start | bytes 3145732
  82.3 14.4 %all-to-all-start.2 = ((bf16[4,768,128]{2,1,0:T(8,128)(2,1)}), bf16[4,768,128]{2,1,0:T(8,128)(2,1)S(1)}, u32[]{:S(2)}, u32[]{:S(2)}) async-start(bf16[4,768,128]{2,1,0:T(8,128)(2,1)} %get-tuple-element.19), calls=%async_computation.2 | async-start | bytes 1572864 | tf_op jit(solution)/shard_map/all_to_all | solution.py:549
  87.3 8.0 %collective-permute-start.10 = (bf16[3,512,128]{2,1,0:T(8,128)(2,1)}, bf16[3,512,128]{2,1,0:T(8,128)(2,1)S(1)}, u32[]{:S(2)}, u32[]{:S(2)}) collective-permute-start(bf16[3,512,128]{2,1,0:T(8,128)(2,1)} %get-tuple-element.20), channel_id=1, source_target_pairs={{0,240},{4,244},{8,248},{12,252},{16,0},{20,4},{24,8},{28,12},{32,... | collective-permute-start | bytes 1179656 | tf_op jit(solution)/shard_map/ppermute | solution.py:539
  114.3 15.4 %all-to-all-start.4 = ((bf16[16,48,256]{2,1,0:T(8,128)(2,1)}), bf16[16,48,256]{2,1,0:T(8,128)(2,1)S(1)}, u32[]{:S(2)}, u32[]{:S(2)}) async-start(bf16[16,48,256]{2,1,0:T(8,128)(2,1)} %shard_map.142), calls=%async_computation.4 | async-start | bytes 786432 | tf_op jit(solution)/shard_map/all_to_all | solution.py:555
